TPU v7x, 32 devices: a whole 2x2x4 slice. The times are simulated.
32 devices in a mesh: group: 2 (over x), pts: 16 (over z, y, core).
Axes of the slice: x: 2, y: 2, z: 4, core: 2. Of those that a mesh axis runs over, the one named last changes fastest.
Arguments:
- coords: int32 [3, 49152], P(None, ('group', 'pts')), parts along dimension 1, may hold values from 0 to 1023
- field: bfloat16 [64, 49152], P(None, ('group', 'pts')), parts along dimension 1, may hold values from -6 to 6
- mode_list: int32 [4096], replicated, may hold values from 0 to 4095, each once
- spec_weight: bfloat16 [2, 4096, 2, 64, 64], P(None, 'pts'), may hold values from -0.5 to 0.5
- bypass_weight: bfloat16 [2, 64, 64], replicated, may hold values from -0.75 to 0.75
- bypass_bias: float32 [2, 64], replicated, may hold values from -3 to 3
Outputs:
- output: bfloat16 [64, 49152], P(None, ('group', 'pts')), parts along dimension 1
There are 2 independent parts, one for each index of `group`. A program takes and returns all parts, laid end to end along the dimension named above; an argument that names none is the same for every part. Nothing has to cross between parts.
Inputs may be any that keep to these rules, and one draw needn't show every extreme that they name: `mode_list`: each of the 4096 mode numbers appears exactly once.
All inputs are finite; a program needn't handle non-finite values.
Results may differ from a plain program's by a relative error of at most 0.0059.
Values may be sent and summed in bfloat16 or wider, within the bound.
No kernel may reach another device: no remote copies, remote signals or barrier semaphores. Data moves between devices by JAX's collectives and lax.ppermute only.
A program may use at most 192 MiB of HBM per device.

v0:
```python
import math

import jax
import jax.numpy as jnp
from jax import lax
from jax.sharding import PartitionSpec as P

KDIM = 16
GRID = 1024
LAYERS = 2


TWO_PI = 2.0 * math.pi


def direct_basis(wave_ids, coords):
    centre = KDIM // 2
    wave_x = wave_ids // (KDIM * KDIM) - centre
    wave_y = wave_ids // KDIM % KDIM - centre
    wave_z = wave_ids % KDIM - centre
    phase_index = (
        wave_x[:, None] * coords[0][None, :]
        + wave_y[:, None] * coords[1][None, :]
        + wave_z[:, None] * coords[2][None, :]
    )
    phase_index = jnp.mod(phase_index, GRID)
    radians = phase_index.astype(jnp.float32) * (TWO_PI / GRID)
    return jnp.concatenate(
        [jnp.cos(radians).astype(jnp.bfloat16), (-jnp.sin(radians)).astype(jnp.bfloat16)], 0
    )


def mix_modes(spectrum, weights):
    width = weights.shape[-1]
    real_in = spectrum[:, :width]
    imag_in = spectrum[:, width:]
    weight_real = weights[:, 0].astype(jnp.float32)
    weight_imag = weights[:, 1].astype(jnp.float32)
    high = lax.Precision.HIGHEST
    real_out = jnp.einsum("kc,kcd->kd", real_in, weight_real, precision=high) - jnp.einsum(
        "kc,kcd->kd", imag_in, weight_imag, precision=high
    )
    imag_out = jnp.einsum("kc,kcd->kd", real_in, weight_imag, precision=high) + jnp.einsum(
        "kc,kcd->kd", imag_in, weight_real, precision=high
    )
    return jnp.concatenate([real_out, imag_out], 1).astype(jnp.bfloat16)


def finish_layer(spectral, field, layer_weight, layer_bias, modes_total):
    direct = lax.dot_general(
        layer_weight, field, (((0,), (0,)), ((), ())), preferred_element_type=jnp.float32
    )
    summed = spectral * (1.0 / math.sqrt(modes_total)) + direct + layer_bias[:, None]
    return jax.nn.gelu(summed, approximate=False).astype(jnp.bfloat16)


def body(coords, field, mode_list, spec_weight, bypass_weight, bypass_bias):
    width = field.shape[0]
    point_count = field.shape[1]
    modes_total = mode_list.shape[0]
    block_size = math.gcd(modes_total, 512)
    block_count = modes_total // block_size
    normaliser = 1.0 / math.sqrt(point_count * lax.axis_size("pts"))

    def basis_for(wave_ids):
        return direct_basis(wave_ids, coords)

    wave_blocks = mode_list.reshape(block_count, block_size)
    blocked = lax.map(basis_for, wave_blocks)
    basis = (
        blocked.reshape(block_count, 2, block_size, point_count)
        .transpose(1, 0, 2, 3)
        .reshape(2 * modes_total, point_count)
    )
    for depth in range(LAYERS):
        current = field
        product = (
            lax.dot_general(
                basis, current, (((1,), (1,)), ((), ())), preferred_element_type=jnp.float32
            )
            * normaliser
        )
        partial_spectrum = jnp.concatenate([product[:modes_total], product[modes_total:]], 1)
        spectrum = lax.psum_scatter(partial_spectrum, "pts", scatter_dimension=0, tiled=True)
        mixed = mix_modes(spectrum, spec_weight[depth])
        gathered = lax.all_gather(mixed, "pts", axis=0, tiled=True)
        stacked = jnp.concatenate([gathered[:, :width], gathered[:, width:]], 0)
        spectral = lax.dot_general(
            stacked, basis, (((0,), (0,)), ((), ())), preferred_element_type=jnp.float32
        )
        field = finish_layer(
            spectral, current, bypass_weight[depth], bypass_bias[depth], modes_total
        )
    return field


def solution(mesh):
    placed = (
        P(None, ("group", "pts")),
        P(None, ("group", "pts")),
        P(),
        P(None, "pts", None, None, None),
        P(),
        P(),
    )
    return jax.shard_map(
        body, mesh=mesh, in_specs=placed, out_specs=P(None, ("group", "pts")), check_vma=False
    )
```

profile of v0, /device:TPU:1, one launch (start us, length us, event | category | flops | bytes accessed | tf_op | source)
XLA Modules:
  0.0 433.2 jit_solution(10487194853132339083)
XLA Ops:
  7.3 131.8 %while.13 = (s32[]{:T(128)}, bf16[8,1024,1536]{2,1,0:T(8,128)(2,1)}, s32[8,512]{1,0:T(8,128)S(1)}, s32[3,1536]{1,0:T(4,128)}, s32[]{:T(128)}) while((s32[]{:T(128)}, bf16[8,1024,1536]{2,1,0:T(8,128)(2,1)}, s32[8,512]{1,0:T(8,128)S(1)}, s32[3,1536]{1,0:T(4,128)}, s32[]{:T(128)}) %tuple.57), condition=%wide.region_1.2_spmd, body=%wide.region_0.1_spmd.sunk | while | flops 22828544 | bytes 9511489 | solution.py:69
  8.2 13.6 %cosine_convert_fusion.2 = (bf16[512,1536]{1,0:T(8,128)(2,1)S(1)}, bf16[512,1536]{1,0:T(8,128)(2,1)S(1)}) fusion(s32[1536]{0:T(1024)S(1)} %get-tuple-element.177, s32[512]{0:T(512)S(1)} %get-tuple-element.178, s32[1536]{0:T(1024)S(1)} %get-tuple-element.179, s32[512]{0:T(512)S(1)} %get-tuple-element.180, s32[1536]{0:T(1024)S(1)} %get-tuple-element.181, ...), kind=kLoop, calls=%fused_computation.9.clone.1 | loop fusion | flops 16515072 | bytes 3170304 | tf_op jit(solution)/shard_map/while/body/eval_jaxpr/convert_element_type | solution.py:29
  21.9 2.0 fusion.71
  24.8 13.6 %cosine_convert_fusion.2 = (bf16[512,1536]{1,0:T(8,128)(2,1)S(1)}, bf16[512,1536]{1,0:T(8,128)(2,1)S(1)}) fusion(s32[1536]{0:T(1024)S(1)} %get-tuple-element.177, s32[512]{0:T(512)S(1)} %get-tuple-element.178, s32[1536]{0:T(1024)S(1)} %get-tuple-element.179, s32[512]{0:T(512)S(1)} %get-tuple-element.180, s32[1536]{0:T(1024)S(1)} %get-tuple-element.181, ...), kind=kLoop, calls=%fused_computation.9.clone.1 | loop fusion | flops 16515072 | bytes 3170304 | tf_op jit(solution)/shard_map/while/body/eval_jaxpr/convert_element_type | solution.py:29
  41.3 13.6 %cosine_convert_fusion.2 = (bf16[512,1536]{1,0:T(8,128)(2,1)S(1)}, bf16[512,1536]{1,0:T(8,128)(2,1)S(1)}) fusion(s32[1536]{0:T(1024)S(1)} %get-tuple-element.177, s32[512]{0:T(512)S(1)} %get-tuple-element.178, s32[1536]{0:T(1024)S(1)} %get-tuple-element.179, s32[512]{0:T(512)S(1)} %get-tuple-element.180, s32[1536]{0:T(1024)S(1)} %get-tuple-element.181, ...), kind=kLoop, calls=%fused_computation.9.clone.1 | loop fusion | flops 16515072 | bytes 3170304 | tf_op jit(solution)/shard_map/while/body/eval_jaxpr/convert_element_type | solution.py:29
  57.7 13.6 %cosine_convert_fusion.2 = (bf16[512,1536]{1,0:T(8,128)(2,1)S(1)}, bf16[512,1536]{1,0:T(8,128)(2,1)S(1)}) fusion(s32[1536]{0:T(1024)S(1)} %get-tuple-element.177, s32[512]{0:T(512)S(1)} %get-tuple-element.178, s32[1536]{0:T(1024)S(1)} %get-tuple-element.179, s32[512]{0:T(512)S(1)} %get-tuple-element.180, s32[1536]{0:T(1024)S(1)} %get-tuple-element.181, ...), kind=kLoop, calls=%fused_computation.9.clone.1 | loop fusion | flops 16515072 | bytes 3170304 | tf_op jit(solution)/shard_map/while/body/eval_jaxpr/convert_element_type | solution.py:29
  74.2 13.6 %cosine_convert_fusion.2 = (bf16[512,1536]{1,0:T(8,128)(2,1)S(1)}, bf16[512,1536]{1,0:T(8,128)(2,1)S(1)}) fusion(s32[1536]{0:T(1024)S(1)} %get-tuple-element.177, s32[512]{0:T(512)S(1)} %get-tuple-element.178, s32[1536]{0:T(1024)S(1)} %get-tuple-element.179, s32[512]{0:T(512)S(1)} %get-tuple-element.180, s32[1536]{0:T(1024)S(1)} %get-tuple-element.181, ...), kind=kLoop, calls=%fused_computation.9.clone.1 | loop fusion | flops 16515072 | bytes 3170304 | tf_op jit(solution)/shard_map/while/body/eval_jaxpr/convert_element_type | solution.py:29
  90.6 13.6 %cosine_convert_fusion.2 = (bf16[512,1536]{1,0:T(8,128)(2,1)S(1)}, bf16[512,1536]{1,0:T(8,128)(2,1)S(1)}) fusion(s32[1536]{0:T(1024)S(1)} %get-tuple-element.177, s32[512]{0:T(512)S(1)} %get-tuple-element.178, s32[1536]{0:T(1024)S(1)} %get-tuple-element.179, s32[512]{0:T(512)S(1)} %get-tuple-element.180, s32[1536]{0:T(1024)S(1)} %get-tuple-element.181, ...), kind=kLoop, calls=%fused_computation.9.clone.1 | loop fusion | flops 16515072 | bytes 3170304 | tf_op jit(solution)/shard_map/while/body/eval_jaxpr/convert_element_type | solution.py:29
  107.1 13.6 %cosine_convert_fusion.2 = (bf16[512,1536]{1,0:T(8,128)(2,1)S(1)}, bf16[512,1536]{1,0:T(8,128)(2,1)S(1)}) fusion(s32[1536]{0:T(1024)S(1)} %get-tuple-element.177, s32[512]{0:T(512)S(1)} %get-tuple-element.178, s32[1536]{0:T(1024)S(1)} %get-tuple-element.179, s32[512]{0:T(512)S(1)} %get-tuple-element.180, s32[1536]{0:T(1024)S(1)} %get-tuple-element.181, ...), kind=kLoop, calls=%fused_computation.9.clone.1 | loop fusion | flops 16515072 | bytes 3170304 | tf_op jit(solution)/shard_map/while/body/eval_jaxpr/convert_element_type | solution.py:29
  123.6 13.6 %cosine_convert_fusion.2 = (bf16[512,1536]{1,0:T(8,128)(2,1)S(1)}, bf16[512,1536]{1,0:T(8,128)(2,1)S(1)}) fusion(s32[1536]{0:T(1024)S(1)} %get-tuple-element.177, s32[512]{0:T(512)S(1)} %get-tuple-element.178, s32[1536]{0:T(1024)S(1)} %get-tuple-element.179, s32[512]{0:T(512)S(1)} %get-tuple-element.180, s32[1536]{0:T(1024)S(1)} %get-tuple-element.181, ...), kind=kLoop, calls=%fused_computation.9.clone.1 | loop fusion | flops 16515072 | bytes 3170304 | tf_op jit(solution)/shard_map/while/body/eval_jaxpr/convert_element_type | solution.py:29
  139.1 20.8 %copy.7 = bf16[2,8,512,1536]{3,2,1,0:T(8,128)(2,1)} copy(bf16[2,8,512,1536]{3,2,0,1:T(8,128)(2,1)} %bitcast.65) | data formatting | bytes 50331648 | tf_op jit(solution)/shard_map/transpose | solution.py:72
  159.9 12.3 %convolution_multiply_fusion.1 = f32[8192,64]{0,1:T(8,128)S(1)} fusion(bf16[8192,1536]{1,0:T(8,128)(2,1)} %bitcast.61, bf16[64,1536]{1,0:T(8,128)(2,1)S(1)} %copy-done), kind=kOutput, calls=%fused_computation.33 | convolution fusion | flops 1611137024 | bytes 27459584 | tf_op jit(solution)/shard_map/dot_general | solution.py:78
  174.0 6.0 %slice_bitcast_fusion = (bf16[256,2,64,64]{0,3,2,1:T(8,128)(2,1)}, bf16[256,2,64,64]{0,3,2,1:T(8,128)(2,1)}) fusion(bf16[2,256,2,64,64]{1,4,3,2,0:T(8,128)(2,1)} %param.11), kind=kLoop, calls=%fused_computation.50 | loop fusion | bytes 16777216 | tf_op jit(solution)/shard_map/squeeze | solution.py:85
  180.0 56.2 %reduce-scatter.3.cloned.1.call-done = f32[256,128]{0,1:T(8,128)} async-done(((f32[4096,128]{0,1:T(8,128)}), f32[256,128]{0,1:T(8,128)}) %reduce-scatter.3.cloned.1.call-update) | async-done | bytes 131088 | tf_op jit(solution)/shard_map/reduce_scatter | solution.py:84
  237.0 3.0 fusion.11
  241.5 38.9 %all-gather.3.cloned.1.call-done = bf16[4096,128]{1,0:T(8,128)(2,1)} async-done(((bf16[256,128]{1,0:T(8,128)(2,1)}), bf16[4096,128]{1,0:T(8,128)(2,1)}) %all-gather.3.cloned.1.call-update) | async-done | bytes 1048592 | tf_op jit(solution)/shard_map/all_gather | solution.py:86
  280.3 2.1 fusion.57
  282.4 10.1 %convolution_multiply_fusion.3 = f32[64,1536]{1,0:T(8,128)S(1)} fusion(bf16[8192,1536]{1,0:T(8,128)(2,1)} %bitcast.62, bf16[4096,64]{1,0:T(8,128)(2,1)S(1)} %get-tuple-element.135, bf16[4096,64]{1,0:T(8,128)(2,1)S(1)} %get-tuple-element.134), kind=kOutput, calls=%fused_computation.57 | convolution fusion | flops 1612808192 | bytes 26607616 | tf_op jit(solution)/shard_map/dot_general | solution.py:88
  293.6 12.3 %convolution_multiply_fusion = f32[8192,64]{0,1:T(8,128)S(1)} fusion(bf16[8192,1536]{1,0:T(8,128)(2,1)} %bitcast.63, bf16[64,1536]{1,0:T(8,128)(2,1)S(1)} %fusion.28), kind=kOutput, calls=%fused_computation.32 | convolution fusion | flops 1611137024 | bytes 27459584 | tf_op jit(solution)/shard_map/dot_general | solution.py:78
  307.7 58.6 %reduce-scatter.5.cloned.1.call-done = f32[256,128]{0,1:T(8,128)} async-done(((f32[4096,128]{0,1:T(8,128)}), f32[256,128]{0,1:T(8,128)}) %reduce-scatter.5.cloned.1.call-update) | async-done | bytes 131088 | tf_op jit(solution)/shard_map/reduce_scatter | solution.py:84
  367.2 3.0 fusion.15
  371.6 38.8 %all-gather.5.cloned.1.call-done = bf16[4096,128]{1,0:T(8,128)(2,1)} async-done(((bf16[256,128]{1,0:T(8,128)(2,1)}), bf16[4096,128]{1,0:T(8,128)(2,1)}) %all-gather.5.cloned.1.call-update) | async-done | bytes 1048592 | tf_op jit(solution)/shard_map/all_gather | solution.py:86
  410.4 2.1 fusion.56
  412.5 14.1 %fusion.31 = bf16[64,1536]{1,0:T(8,128)(2,1)} fusion(f32[64,1536]{1,0:T(8,128)S(1)} %convolution_bitcast_fusion, bf16[8192,1536]{1,0:T(8,128)(2,1)} %bitcast.64, bf16[4096,64]{1,0:T(8,128)(2,1)S(1)} %get-tuple-element.133, bf16[4096,64]{1,0:T(8,128)(2,1)S(1)} %get-tuple-element.132, f32[64]{0:T(128)S(1)} %get-tuple-element.140), kind=kOutput, calls=%fused_computation.78 | convolution fusion | flops 1619394560 | bytes 26804480 | tf_op jit(solution)/shard_map/dot_general | solution.py:88
  (69 shorter events, 30.4 us)
Async XLA Ops:
  6.5 153.4 %copy-start = (bf16[64,1536]{1,0:T(8,128)(2,1)S(1)}, bf16[64,1536]{1,0:T(8,128)(2,1)}, u32[]{:S(2)}) copy-start(bf16[64,1536]{1,0:T(8,128)(2,1)} %param.9) | copy-start | bytes 589828
  6.5 229.6 %reduce-scatter.3.cloned.1.call-start = ((), (), s32[]{:S(2)}) async-start(), calls=%async_computation.2 | async-start | bytes 2228224 | tf_op jit(solution)/shard_map/reduce_scatter | solution.py:84
  173.9 106.4 %all-gather.3.cloned.1.call-start = ((), (), s32[]{:S(2)}) async-start(), calls=%async_computation.3 | async-start | bytes 1114112 | tf_op jit(solution)/shard_map/all_gather | solution.py:86
  237.0 4.4 %copy-start.2 = (f32[2,64]{1,0:T(2,128)S(1)}, f32[2,64]{1,0:T(2,128)}, u32[]{:S(2)}) copy-start(f32[2,64]{1,0:T(2,128)} %param.13) | copy-start | bytes 1540
  241.2 125.1 %reduce-scatter.5.cloned.1.call-start = ((), (), s32[]{:S(2)}) async-start(), calls=%async_computation.4 | async-start | bytes 2228224 | tf_op jit(solution)/shard_map/reduce_scatter | solution.py:84
  282.4 10.1 %copy-start.1 = (bf16[2,64,64]{2,1,0:T(8,128)(2,1)S(1)}, bf16[2,64,64]{2,1,0:T(8,128)(2,1)}, u32[]{:S(2)}) copy-start(bf16[2,64,64]{2,1,0:T(8,128)(2,1)} %param.12) | copy-start | bytes 49156
  307.6 102.8 %all-gather.5.cloned.1.call-start = ((), (), s32[]{:S(2)}) async-start(), calls=%async_computation.5 | async-start | bytes 1114112 | tf_op jit(solution)/shard_map/all_gather | solution.py:86
Sparse Core Ops, SparseCore 0:
  174.0 62.0 reduce-scatter.2
  241.3 38.9 all-gather.2
  307.7 58.5 reduce-scatter.4
  371.5 38.8 all-gather.4
where the time goes:
time: 434 us; the launch traced here: 433 us
  waiting for transfers between devices  193 us (44%)
  other arithmetic  135 us (31%)
  matrix products  50.2 us (12%)
  local copies, waits for them, and re-layouts  41.8 us (10%)
  between operations  13.3 us (3%)
    reduce_scatter x2, waiting for transfers between devices, body(): lax.psum_scatter(partial_spectrum, 'pts', scatter_dimension=0, tiled=True)  115 us
    convert_element_type x8, other arithmetic, direct_basis(): jnp.cos(radians).astype(jnp.bfloat16)  109 us
    all_gather x2, waiting for transfers between devices, body(): gathered = lax.all_gather(mixed, 'pts', axis=0, tiled=True)  77.6 us
    dot_general x2, matrix products, body(): lax.dot_general(basis, current, (((1,), (1,)), ((), ())), preferred_eleme...  24.7 us
    dot_general x2, matrix products, body(): lax.dot_general(stacked, basis, (((0,), (0,)), ((), ())), preferred_eleme...  24.2 us
    transpose x1, local copies, waits for them, and re-layouts, body(): basis = blocked.reshape(block_count, 2, block_size, point_count).transpos...  20.8 us
    dynamic_update_slice x8, other arithmetic, body(): blocked = lax.map(basis_for, wave_blocks)  15.2 us
  transfers between devices with their start and end apart: 4, of which 4 were waited for; matrix products, arithmetic and copies ran while one was open for 1% of the time, Pallas kernels for 0%

commit v1 on v0

v1 whole, which is shorter than its diff:
```python
import math

import jax
import jax.numpy as jnp
import numpy as np
from jax import lax
from jax.experimental import pallas as pl
from jax.experimental.pallas import tpu as pltpu
from jax.sharding import PartitionSpec as P

KDIM = 16
GRID = 1024
LAYERS = 2
TWO_PI = 2.0 * math.pi
HALF = KDIM // 2
KZ = HALF + 1
GROUPS = HALF + 3
ROWS_A = GROUPS * 32
ROWS_Q = KZ * ROWS_A
VMEM = 56 * 1024 * 1024
F32 = jnp.float32
BF16 = jnp.bfloat16


def params():
    return pltpu.CompilerParams(vmem_limit_bytes=VMEM)


def vmem():
    return pl.BlockSpec(memory_space=pltpu.VMEM)


def smem():
    return pl.BlockSpec(memory_space=pltpu.SMEM)


def table_rows(mode_list):
    kx = mode_list // (KDIM * KDIM) - HALF
    ky = mode_list // KDIM % KDIM - HALF
    kz = mode_list % KDIM - HALF
    flip = kx < 0
    ky = jnp.where(flip, -ky, ky)
    kz = jnp.where(flip, -kz, kz)
    ax, ay, az = jnp.abs(kx), jnp.abs(ky), jnp.abs(kz)
    quarter = 2 * (ky < 0).astype(jnp.int32) + (kz < 0).astype(jnp.int32)
    group = jnp.where(ay < HALF, ax, jnp.where(ax < HALF, HALF + 1, HALF + 2))
    inner = jnp.where(ay < HALF, ay, jnp.where(ax < HALF, ax, 0))
    row = ((az * GROUPS + group) * 4 + quarter) * 8 + inner
    return row, flip


def tables_kernel(coords_ref, a_ref, cs_ref):
    angle = coords_ref[...].astype(F32) * (TWO_PI / GRID)
    one_c, one_s = jnp.cos(angle), jnp.sin(angle)
    cos, sin = [jnp.ones_like(angle), one_c], [jnp.zeros_like(angle), one_s]
    for k in range(2, HALF + 1):
        i, j = k // 2, k - k // 2
        cos.append(cos[i] * cos[j] - sin[i] * sin[j])
        sin.append(sin[i] * cos[j] + cos[i] * sin[j])
    cx = jnp.concatenate([c[0:1] for c in cos[:HALF]], 0)
    sx = jnp.concatenate([s[0:1] for s in sin[:HALF]], 0)
    cy = jnp.concatenate([c[1:2] for c in cos[:HALF]], 0)
    sy = jnp.concatenate([s[1:2] for s in sin[:HALF]], 0)
    for g in range(GROUPS):
        if g <= HALF:
            c, s = cos[g][0:1], sin[g][0:1]
            parts = [c * cy, c * sy, s * cy, s * sy]
        elif g == HALF + 1:
            c, s = cos[HALF][1:2], sin[HALF][1:2]
            parts = [cx * c, cx * s, sx * c, sx * s]
        else:
            c, s = cos[HALF][1:2], sin[HALF][1:2]
            first = (lax.broadcasted_iota(jnp.int32, cx.shape, 0) == 0).astype(F32)
            cl, sl = first * cos[HALF][0:1], first * sin[HALF][0:1]
            parts = [cl * c, cl * s, sl * c, sl * s]
        a_ref[g * 32 : (g + 1) * 32, :] = jnp.concatenate(parts, 0).astype(BF16)
    pad = jnp.zeros((7, angle.shape[1]), F32)
    cs_ref[...] = jnp.concatenate(
        [c[2:3] for c in cos] + [pad] + [s[2:3] for s in sin] + [pad], 0
    )


def make_tables(coords):
    points = coords.shape[1]
    return pl.pallas_call(
        tables_kernel,
        out_shape=(
            jax.ShapeDtypeStruct((ROWS_A, points), BF16),
            jax.ShapeDtypeStruct((32, points), F32),
        ),
        in_specs=[vmem()],
        out_specs=(vmem(), vmem()),
        compiler_params=params(),
    )(coords)


def sign_lanes(width):
    lane = lax.broadcasted_iota(jnp.int32, (8, 2 * width), 1)
    return jnp.where(lane < width, 1.0, -1.0).astype(F32)


def forward_kernel(norm, a_ref, cs_ref, own_ref, other_ref, q_ref, hs_ref, b_ref):
    width = own_ref.shape[0]
    points = own_ref.shape[1]
    hs_ref[:, :points] = own_ref[...].astype(F32) * norm
    hs_ref[:, points:] = other_ref[...].astype(F32) * norm

    def product(b):
        return lax.dot_general(
            a_ref[...], b, (((1,), (1,)), ((), ())), preferred_element_type=F32
        )

    first = product(hs_ref[...].astype(BF16))
    q_ref[0:ROWS_A, :] = jnp.concatenate([first, jnp.zeros_like(first)], 1)

    for pair in range(HALF // 2):
        for half in range(2):
            k = 2 * pair + 1 + half
            b_ref[2 * half * width : (2 * half + 1) * width, :] = (
                hs_ref[...] * cs_ref[k : k + 1, :]
            ).astype(BF16)
            b_ref[(2 * half + 1) * width : (2 * half + 2) * width, :] = (
                hs_ref[...] * cs_ref[16 + k : 17 + k, :]
            ).astype(BF16)
        both = product(b_ref[...])
        k = 2 * pair + 1
        q_ref[k * ROWS_A : (k + 1) * ROWS_A, :] = both[:, : 2 * width]
        q_ref[(k + 1) * ROWS_A : (k + 2) * ROWS_A, :] = both[:, 2 * width :]

    sign = sign_lanes(width)

    def combine(i, carry):
        base = pl.multiple_of(i * 32, 32)
        cc = q_ref[pl.ds(base, 8), :]
        cs = q_ref[pl.ds(base + 8, 8), :]
        sc = q_ref[pl.ds(base + 16, 8), :]
        ss = q_ref[pl.ds(base + 24, 8), :]
        for y in range(2):
            u = cc + ss if y else cc - ss
            v = pltpu.roll(sc - cs if y else sc + cs, width, 1)
            q_ref[pl.ds(base + 16 * y, 8), :] = u * sign - v
            q_ref[pl.ds(base + 16 * y + 8, 8), :] = u + v * sign
        return carry

    lax.fori_loop(0, KZ * GROUPS, combine, 0, unroll=3)


def gather_rows(idx_ref, q_ref, out_ref, offset):
    def step(j, carry):
        out_ref[pl.ds(j, 1), :] = q_ref[pl.ds(idx_ref[offset + j], 1), :]
        return carry

    lax.fori_loop(0, out_ref.shape[0], step, 0, unroll=16)


def forward(idx, a, cs, own, other, norm, rows):
    width, points = own.shape
    kept = rows // 2

    def kernel(idx_ref, a_ref, cs_ref, own_ref, other_ref, keep_ref, send_ref, q_ref, hs_ref, b_ref, stage_ref):
        forward_kernel(norm, a_ref, cs_ref, own_ref, other_ref, q_ref, hs_ref, b_ref)
        gather_rows(idx_ref, q_ref, stage_ref, kept)
        send_ref[...] = stage_ref[...].astype(BF16)
        gather_rows(idx_ref, q_ref, keep_ref, 0)

    return pl.pallas_call(
        kernel,
        out_shape=(
            jax.ShapeDtypeStruct((kept, 2 * width), F32),
            jax.ShapeDtypeStruct((kept, 2 * width), BF16),
        ),
        in_specs=[smem()] + [vmem()] * 4,
        out_specs=(vmem(), vmem()),
        scratch_shapes=[
            pltpu.VMEM((ROWS_Q, 2 * width), F32),
            pltpu.VMEM((width, 2 * points), F32),
            pltpu.VMEM((4 * width, 2 * points), BF16),
            pltpu.VMEM((kept, 2 * width), F32),
        ],
        compiler_params=params(),
    )(idx, a, cs, own, other)


def mix_kernel(scale, keep_ref, got_ref, flip_ref, w_ref, out_ref, s_ref, acc_ref):
    step = pl.program_id(0)
    width = acc_ref.shape[0] // 2

    @pl.when(step == 0)
    def _():
        total = keep_ref[...] + got_ref[...].astype(F32)
        s_ref[...] = total.T
        s_ref[width:, :] = s_ref[width:, :] * flip_ref[...]
        acc_ref[...] = jnp.zeros_like(acc_ref)

    block = w_ref.shape[2]
    real, imag = acc_ref[:width, :], acc_ref[width:, :]
    for i in range(block):
        row = step * block + i
        re = s_ref[pl.ds(row, 1), :]
        im = s_ref[pl.ds(width + row, 1), :]
        wr = w_ref[0, 0, i].astype(F32)
        wi = w_ref[0, 1, i].astype(F32)
        real = real + re * wr - im * wi
        imag = imag + re * wi + im * wr
    acc_ref[:width, :] = real
    acc_ref[width:, :] = imag

    @pl.when(step == pl.num_programs(0) - 1)
    def _():
        acc_ref[:width, :] = acc_ref[:width, :] * scale
        acc_ref[width:, :] = acc_ref[width:, :] * (flip_ref[...] * scale)
        out_ref[...] = acc_ref[...].T.astype(BF16)


def mix(keep, got, flip, weights, layer, scale):
    modes, double = keep.shape
    width = double // 2
    block = 8

    def kernel(*refs):
        mix_kernel(scale, *refs)

    fixed = lambda i: (0, 0)
    return pl.pallas_call(
        kernel,
        grid=(width // block,),
        out_shape=jax.ShapeDtypeStruct((modes, double), BF16),
        in_specs=[
            pl.BlockSpec((modes, double), fixed),
            pl.BlockSpec((modes, double), fixed),
            pl.BlockSpec((1, modes), fixed),
            pl.BlockSpec((1, 2, block, width, modes), lambda i: (layer, 0, i, 0, 0)),
        ],
        out_specs=pl.BlockSpec((modes, double), fixed),
        scratch_shapes=[pltpu.VMEM((double, modes), F32), pltpu.VMEM((double, modes), F32)],
        compiler_params=params(),
    )(keep, got, flip, weights)


def inverse_kernel(idx_ref, a_ref, cs_ref, mixed_ref, own_ref, other_ref, z_ref, m_ref, t_ref):
    width = own_ref.shape[0]
    points = own_ref.shape[1]
    m_ref[...] = mixed_ref[...].astype(F32)

    def clear(i, carry):
        z_ref[pl.ds(pl.multiple_of(i * 32, 32), 32), :] = jnp.zeros((32, 2 * width), F32)
        return carry

    lax.fori_loop(0, 2 * ROWS_Q // 32, clear, 0, unroll=6)

    def place(j, carry):
        z_ref[pl.ds(idx_ref[j], 1), :] = m_ref[pl.ds(j, 1), :]
        return carry

    lax.fori_loop(0, m_ref.shape[0], place, 0, unroll=16)
    sign = sign_lanes(width)

    def combine(i, carry):
        base = pl.multiple_of(i * 32, 32)
        u, v = [], []
        for y in range(2):
            lo = base + 16 * y
            plus = z_ref[pl.ds(lo, 8), :] + z_ref[pl.ds(ROWS_Q + lo, 8), :]
            minus = z_ref[pl.ds(lo + 8, 8), :] + z_ref[pl.ds(ROWS_Q + lo + 8, 8), :]
            u.append(plus * sign + minus)
            v.append(pltpu.roll(plus - minus * sign, width, 1))
        z_ref[pl.ds(base, 8), :] = u[0] + u[1]
        z_ref[pl.ds(base + 8, 8), :] = v[1] - v[0]
        z_ref[pl.ds(base + 16, 8), :] = -v[0] - v[1]
        z_ref[pl.ds(base + 24, 8), :] = u[1] - u[0]
        return carry

    lax.fori_loop(0, KZ * GROUPS, combine, 0, unroll=3)
    for k in range(KZ):
        t_ref[k * 2 * width : (k + 1) * 2 * width, :] = z_ref[
            k * ROWS_A : (k + 1) * ROWS_A, :
        ].T.astype(BF16)

    chunk = math.gcd(points, 512)
    for part, out_ref in enumerate((own_ref, other_ref)):
        for at in range(0, points, chunk):
            here = slice(part * points + at, part * points + at + chunk)
            r = lax.dot_general(
                t_ref[...], a_ref[:, here], (((1,), (0,)), ((), ())), preferred_element_type=F32
            )
            total = r[:width]
            for k in range(1, KZ):
                lo = 2 * k * width
                total = total + r[lo : lo + width] * cs_ref[k : k + 1, here]
                total = total + r[lo + width : lo + 2 * width] * cs_ref[16 + k : 17 + k, here]
            out_ref[:, at : at + chunk] = total.astype(out_ref.dtype)


def inverse(idx, a, cs, mixed, points):
    rows, double = mixed.shape
    width = double // 2
    return pl.pallas_call(
        inverse_kernel,
        out_shape=(
            jax.ShapeDtypeStruct((width, points), F32),
            jax.ShapeDtypeStruct((width, points), F32),
        ),
        in_specs=[smem()] + [vmem()] * 3,
        out_specs=(vmem(), vmem()),
        scratch_shapes=[
            pltpu.VMEM((2 * ROWS_Q, double), F32),
            pltpu.VMEM((rows, double), F32),
            pltpu.VMEM((KZ * double, ROWS_A), BF16),
        ],
        compiler_params=params(),
    )(idx, a, cs, mixed)


def body(coords, field, mode_list, spec_weight, bypass_weight, bypass_bias):
    width, points = field.shape
    modes_total = mode_list.shape[0]
    count = lax.axis_size("pts")
    bits = count.bit_length() - 1
    me = lax.axis_index("pts")
    local = modes_total // count
    norm = 1.0 / math.sqrt(points * count)
    scale = 1.0 / math.sqrt(modes_total)

    def swap(x, bit):
        return lax.ppermute(x, "pts", [(i, i ^ (1 << bit)) for i in range(count)])

    row, flip = table_rows(mode_list)
    signs = jnp.where(flip, -1.0, 1.0).astype(F32)
    my_signs = lax.dynamic_slice(signs, (me * local,), (local,)).reshape(1, local)
    place = row + jnp.where(flip, ROWS_Q, 0)
    order = np.array(
        [sum(((t >> (bits - 2 - b)) & 1) << (b + 1) for b in range(bits - 1)) for t in range(count // 2)]
    )
    owners = jnp.bitwise_xor(me, jnp.asarray(order, jnp.int32))
    idx_get = row.reshape(count, local)[owners].reshape(-1)
    idx_put = place.reshape(count, local)[owners].reshape(-1)
    weights = jnp.transpose(spec_weight, (0, 2, 3, 4, 1))

    a, cs = make_tables(jnp.concatenate([coords, swap(coords, 0)], 1))
    for depth in range(LAYERS):
        other = swap(field, 0)
        keep, send = forward(idx_get, a, cs, field, other, norm, modes_total // 2)
        for bit in range(1, bits):
            got = swap(send, bit)
            if bit == bits - 1:
                break
            half = keep.shape[0] // 2
            send = (keep[half:] + got[half:].astype(F32)).astype(BF16)
            keep = keep[:half] + got[:half].astype(F32)
        mixed = mix(keep, got, my_signs, weights, depth, scale)
        for bit in range(bits - 1, 0, -1):
            mixed = jnp.concatenate([mixed, swap(mixed, bit)], 0)
        spectral, theirs = inverse(idx_put, a, cs, mixed, points)
        spectral = spectral + swap(theirs, 0)
        direct = lax.dot_general(
            bypass_weight[depth], field, (((0,), (0,)), ((), ())), preferred_element_type=F32
        )
        summed = spectral + direct + bypass_bias[depth][:, None]
        field = jax.nn.gelu(summed, approximate=False).astype(BF16)
    return field


def solution(mesh):
    placed = (
        P(None, ("group", "pts")),
        P(None, ("group", "pts")),
        P(),
        P(None, "pts", None, None, None),
        P(),
        P(),
    )
    return jax.shard_map(
        body, mesh=mesh, in_specs=placed, out_specs=P(None, ("group", "pts")), check_vma=False
    )
```

time: 434 us -> 162 us (0.37)
  waiting for transfers between devices: 193 us -> 39.9 us
  other arithmetic: 135 us -> 15.6 us
  Pallas kernels: 0 us -> 60.7 us
  matrix products: 50.2 us -> 2.96 us
  local copies, waits for them, and re-layouts: 41.8 us -> 4.96 us
  starting transfers between devices: 0.31 us -> 36.6 us
  between operations: 13.3 us -> 0.09 us
    reduce_scatter x2 -> x0, waiting for transfers between devices: 115 us -> none  [body(): lax.psum_scatter(partial_spectrum, 'pts', scatter_dimension=0, tiled=True)]
    convert_element_type x8 -> x5, other arithmetic: 109 us -> 5.46 us  [the longest x4 3.51 us: body(): send = (keep[half:] + got[half:].astype(F32)).astype(BF16)]
    all_gather x2 -> x0, waiting for transfers between devices: 77.6 us -> none  [body(): gathered = lax.all_gather(mixed, 'pts', axis=0, tiled=True)]
    pallas_call x0 -> x7, Pallas kernels: none -> 60.7 us  [the longest x2 23.4 us: inverse(): pl.pallas_call(inverse_kernel, out_shape=(jax.ShapeDtypeStruct((width, po...]
    dot_general x6 -> x2, matrix products: 50.2 us -> 2.96 us  [body(): lax.dot_general(bypass_weight[depth], field, (((0,), (0,)), ((), ())), pr...]
    ppermute x0 -> x17, waiting for transfers between devices: none -> 39.9 us  [swap(): return lax.ppermute(x, 'pts', [(i, i ^ 1 << bit) for i in range(count)])]
    ppermute x0 -> x17, starting transfers between devices: none -> 36.6 us  [swap(): return lax.ppermute(x, 'pts', [(i, i ^ 1 << bit) for i in range(count)])]
    transpose x1 -> x0, local copies, waits for them, and re-layouts: 20.8 us -> none  [body(): basis = blocked.reshape(block_count, 2, block_size, point_count).transpos...]
  transfers between devices with their start and end apart: 4 -> 17, of which waited for: 4 -> 15; matrix products, arithmetic and copies ran while one was open for 1% -> 4% of each run, Pallas kernels for 0% -> 2%
where the time goes in v1:
time: 162 us; the launch traced here: 161 us
  Pallas kernels  60.7 us (37%)
  waiting for transfers between devices  39.9 us (25%)
  starting transfers between devices  36.6 us (23%)
  other arithmetic  15.6 us (10%)
  local copies, waits for them, and re-layouts  4.96 us (3%)
  matrix products  2.96 us (2%)
    ppermute x17, waiting for transfers between devices, swap(): return lax.ppermute(x, 'pts', [(i, i ^ 1 << bit) for i in range(count)])  39.9 us
    ppermute x17, starting transfers between devices, swap(): return lax.ppermute(x, 'pts', [(i, i ^ 1 << bit) for i in range(count)])  36.6 us
    pallas_call x2, Pallas kernels, inverse(): pl.pallas_call(inverse_kernel, out_shape=(jax.ShapeDtypeStruct((width, po...  23.4 us
    pallas_call x2, Pallas kernels, forward(): pl.pallas_call(kernel, out_shape=(jax.ShapeDtypeStruct((kept, 2 * width),...  21.4 us
    pallas_call x2, Pallas kernels, mix(): pl.pallas_call(kernel, grid=(width // block,), out_shape=jax.ShapeDtypeSt...  12.8 us
    concatenate x6, other arithmetic, body(): mixed = jnp.concatenate([mixed, swap(mixed, bit)], 0)  6.76 us
    unnamed x20, local copies, waits for them, and re-layouts  3.83 us
    convert_element_type x4, other arithmetic, body(): send = (keep[half:] + got[half:].astype(F32)).astype(BF16)  3.51 us
  transfers between devices with their start and end apart: 17, of which 15 were waited for; matrix products, arithmetic and copies ran while one was open for 4% of the time, Pallas kernels for 2%

profile of v1, /device:TPU:1, one launch (start us, length us, event | category | flops | bytes accessed | tf_op | source)
XLA Modules:
  0.0 160.8 jit_solution(17158144119461836773)
XLA Ops:
  4.5 3.1 %shard_map.73 = (bf16[352,3072]{1,0:T(8,128)(2,1)}, f32[32,3072]{1,0:T(8,128)}) custom-call(s32[3,3072]{1,0:T(4,128)} %pad_add_fusion.coords_ref), custom_call_target="tpu_custom_call" | custom-call | tf_op jit(solution)/shard_map/pallas_call | solution.py:85
  8.3 10.8 %shard_map.74 = (f32[1024,128]{1,0:T(8,128)}, bf16[1024,128]{1,0:T(8,128)(2,1)}) custom-call(s32[2048]{0:T(1024)} %bitcast.26, bf16[352,3072]{1,0:T(8,128)(2,1)} %get-tuple-element.15.a_ref, f32[32,3072]{1,0:T(8,128)} %get-tuple-element.16.cs_ref, bf16[64,1536]{1,0:T(8,128)(2,1)} %own_ref.1, bf16[64,1536]{1,0:T(8,128)(2,1)} %copy-done.3), custom_call_target="tpu_custom_call" | custom-call | tf_op jit(solution)/shard_map/pallas_call | solution.py:166
  19.1 2.3 %collective-permute-start.2 = (bf16[1024,128]{1,0:T(8,128)(2,1)}, bf16[1024,128]{1,0:T(8,128)(2,1)S(1)}, u32[]{:S(2)}, u32[]{:S(2)}) collective-permute-start(bf16[1024,128]{1,0:T(8,128)(2,1)} %get-tuple-element.18), channel_id=1, source_target_pairs={{0,2},{1,3},{2,0},{3,1},{4,6},{5,7},{6,4},{7,5},{8,10},{9,11},{10,... | collective-permute-start | bytes 786440 | tf_op jit(solution)/shard_map/ppermute | solution.py:325
  21.4 6.4 %collective-permute-done.2 = bf16[1024,128]{1,0:T(8,128)(2,1)S(1)} collective-permute-done((bf16[1024,128]{1,0:T(8,128)(2,1)}, bf16[1024,128]{1,0:T(8,128)(2,1)S(1)}, u32[]{:S(2)}, u32[]{:S(2)}) %collective-permute-start.2) | collective-permute-done | bytes 262176 | tf_op jit(solution)/shard_map/ppermute | solution.py:325
  30.1 2.6 %collective-permute-done.3 = bf16[512,128]{1,0:T(8,128)(2,1)S(1)} collective-permute-done((bf16[512,128]{1,0:T(8,128)(2,1)S(1)}, bf16[512,128]{1,0:T(8,128)(2,1)S(1)}, u32[]{:S(2)}, u32[]{:S(2)}) %collective-permute-start.3) | collective-permute-done | bytes 131104 | tf_op jit(solution)/shard_map/ppermute | solution.py:325
  33.5 2.2 %collective-permute-start.4 = (bf16[256,128]{1,0:T(8,128)(2,1)S(1)}, bf16[256,128]{1,0:T(8,128)(2,1)S(1)}, u32[]{:S(2)}, u32[]{:S(2)}) collective-permute-start(bf16[256,128]{1,0:T(8,128)(2,1)S(1)} %get-tuple-element.34), channel_id=1, source_target_pairs={{0,8},{1,9},{2,10},{3,11},{4,12},{5,13},{6,14},{7,15},{8,0},{9,1},... | collective-permute-start | bytes 196616 | tf_op jit(solution)/shard_map/ppermute | solution.py:325
  38.1 6.4 %shard_map.75 = bf16[256,128]{1,0:T(8,128)(2,1)} custom-call(f32[256,128]{1,0:T(8,128)} %get-tuple-element.35.refs_0_, bf16[256,128]{1,0:T(8,128)(2,1)} %copy-done.5, f32[1,256]{1,0:T(1,128)} %bitcast.32, bf16[2,2,64,64,256]{4,3,2,1,0:T(8,128)(2,1)} %bitcast.24), custom_call_target="tpu_custom_call" | custom-call | tf_op jit(solution)/shard_map/pallas_call | solution.py:224
  44.5 2.2 %collective-permute-start.5 = (bf16[256,128]{1,0:T(8,128)(2,1)}, bf16[256,128]{1,0:T(8,128)(2,1)S(1)}, u32[]{:S(2)}, u32[]{:S(2)}) collective-permute-start(bf16[256,128]{1,0:T(8,128)(2,1)} %shard_map.75), channel_id=1, source_target_pairs={{0,8},{1,9},{2,10},{3,11},{4,12},{5,13},{6,14},{7,15},{8,0},{9,1},... | collective-permute-start | bytes 196616 | tf_op jit(solution)/shard_map/ppermute | solution.py:325
  46.8 2.0 %collective-permute-done.5 = bf16[256,128]{1,0:T(8,128)(2,1)S(1)} collective-permute-done((bf16[256,128]{1,0:T(8,128)(2,1)}, bf16[256,128]{1,0:T(8,128)(2,1)S(1)}, u32[]{:S(2)}, u32[]{:S(2)}) %collective-permute-start.5) | collective-permute-done | bytes 65568 | tf_op jit(solution)/shard_map/ppermute | solution.py:325
  51.4 2.6 %collective-permute-done.6 = bf16[512,128]{1,0:T(8,128)(2,1)S(1)} collective-permute-done((bf16[512,128]{1,0:T(8,128)(2,1)S(1)}, bf16[512,128]{1,0:T(8,128)(2,1)S(1)}, u32[]{:S(2)}, u32[]{:S(2)}) %collective-permute-start.6) | collective-permute-done | bytes 131104 | tf_op jit(solution)/shard_map/ppermute | solution.py:325
  57.5 2.6 %collective-permute-done.7 = bf16[1024,128]{1,0:T(8,128)(2,1)S(1)} collective-permute-done((bf16[1024,128]{1,0:T(8,128)(2,1)S(1)}, bf16[1024,128]{1,0:T(8,128)(2,1)S(1)}, u32[]{:S(2)}, u32[]{:S(2)}) %collective-permute-start.7) | collective-permute-done | bytes 262176 | tf_op jit(solution)/shard_map/ppermute | solution.py:325
  61.7 11.6 %shard_map.76 = (f32[64,1536]{1,0:T(8,128)}, f32[64,1536]{1,0:T(8,128)}) custom-call(s32[2048]{0:T(1024)} %bitcast.28, bf16[352,3072]{1,0:T(8,128)(2,1)} %get-tuple-element.15.a_ref, f32[32,3072]{1,0:T(8,128)} %get-tuple-element.16.cs_ref, bf16[2048,128]{1,0:T(8,128)(2,1)} %pad_maximum_fusion.mixed_ref), custom_call_target="tpu_custom_call" | custom-call | tf_op jit(solution)/shard_map/pallas_call | solution.py:297
  73.4 6.3 %collective-permute-start.8 = (f32[64,1536]{1,0:T(8,128)}, f32[64,1536]{1,0:T(8,128)S(1)}, u32[]{:S(2)}, u32[]{:S(2)}) collective-permute-start(f32[64,1536]{1,0:T(8,128)} %get-tuple-element.20), channel_id=1, source_target_pairs={{0,1},{1,0},{2,3},{3,2},{4,5},{5,4},{6,7},{7,6},{8,9},{9,8},{10,11... | collective-permute-start | bytes 1179656 | tf_op jit(solution)/shard_map/ppermute | solution.py:325
  85.4 10.6 %shard_map.77 = (f32[1024,128]{1,0:T(8,128)}, bf16[1024,128]{1,0:T(8,128)(2,1)}) custom-call(s32[2048]{0:T(1024)} %bitcast.27, bf16[352,3072]{1,0:T(8,128)(2,1)} %get-tuple-element.15.a_ref, f32[32,3072]{1,0:T(8,128)} %get-tuple-element.16.cs_ref, bf16[64,1536]{1,0:T(8,128)(2,1)} %copy-done, bf16[64,1536]{1,0:T(8,128)(2,1)} %copy-done.4), custom_call_target="tpu_custom_call" | custom-call | tf_op jit(solution)/shard_map/pallas_call | solution.py:166
  97.5 6.3 %collective-permute-done.10 = bf16[1024,128]{1,0:T(8,128)(2,1)S(1)} collective-permute-done((bf16[1024,128]{1,0:T(8,128)(2,1)}, bf16[1024,128]{1,0:T(8,128)(2,1)S(1)}, u32[]{:S(2)}, u32[]{:S(2)}) %collective-permute-start.10) | collective-permute-done | bytes 262176 | tf_op jit(solution)/shard_map/ppermute | solution.py:325
  106.7 2.4 %collective-permute-done.11 = bf16[512,128]{1,0:T(8,128)(2,1)S(1)} collective-permute-done((bf16[512,128]{1,0:T(8,128)(2,1)S(1)}, bf16[512,128]{1,0:T(8,128)(2,1)S(1)}, u32[]{:S(2)}, u32[]{:S(2)}) %collective-permute-start.11) | collective-permute-done | bytes 131104 | tf_op jit(solution)/shard_map/ppermute | solution.py:325
  109.7 3.0 %collective-permute-start.12 = (bf16[256,128]{1,0:T(8,128)(2,1)S(1)}, bf16[256,128]{1,0:T(8,128)(2,1)S(1)}, u32[]{:S(2)}, u32[]{:S(2)}) collective-permute-start(bf16[256,128]{1,0:T(8,128)(2,1)S(1)} %get-tuple-element.32), channel_id=1, source_target_pairs={{0,8},{1,9},{2,10},{3,11},{4,12},{5,13},{6,14},{7,15},{8,0},{9,1},... | collective-permute-start | bytes 196616 | tf_op jit(solution)/shard_map/ppermute | solution.py:325
  115.0 6.4 %shard_map.78 = bf16[256,128]{1,0:T(8,128)(2,1)} custom-call(f32[256,128]{1,0:T(8,128)} %get-tuple-element.33.refs_0_, bf16[256,128]{1,0:T(8,128)(2,1)} %copy-done.6, f32[1,256]{1,0:T(1,128)} %bitcast.33, bf16[2,2,64,64,256]{4,3,2,1,0:T(8,128)(2,1)} %bitcast.25), custom_call_target="tpu_custom_call" | custom-call | tf_op jit(solution)/shard_map/pallas_call | solution.py:224
  121.4 2.4 %collective-permute-start.13 = (bf16[256,128]{1,0:T(8,128)(2,1)}, bf16[256,128]{1,0:T(8,128)(2,1)S(1)}, u32[]{:S(2)}, u32[]{:S(2)}) collective-permute-start(bf16[256,128]{1,0:T(8,128)(2,1)} %shard_map.78), channel_id=1, source_target_pairs={{0,8},{1,9},{2,10},{3,11},{4,12},{5,13},{6,14},{7,15},{8,0},{9,1},... | collective-permute-start | bytes 196616 | tf_op jit(solution)/shard_map/ppermute | solution.py:325
  128.4 2.4 %collective-permute-done.14 = bf16[512,128]{1,0:T(8,128)(2,1)S(1)} collective-permute-done((bf16[512,128]{1,0:T(8,128)(2,1)S(1)}, bf16[512,128]{1,0:T(8,128)(2,1)S(1)}, u32[]{:S(2)}, u32[]{:S(2)}) %collective-permute-start.14) | collective-permute-done | bytes 131104 | tf_op jit(solution)/shard_map/ppermute | solution.py:325
  132.9 4.0 %collective-permute-done.15 = bf16[1024,128]{1,0:T(8,128)(2,1)S(1)} collective-permute-done((bf16[1024,128]{1,0:T(8,128)(2,1)S(1)}, bf16[1024,128]{1,0:T(8,128)(2,1)S(1)}, u32[]{:S(2)}, u32[]{:S(2)}) %collective-permute-start.15) | collective-permute-done | bytes 262176 | tf_op jit(solution)/shard_map/ppermute | solution.py:325
  138.6 11.8 %shard_map.79 = (f32[64,1536]{1,0:T(8,128)}, f32[64,1536]{1,0:T(8,128)}) custom-call(s32[2048]{0:T(1024)} %bitcast.29, bf16[352,3072]{1,0:T(8,128)(2,1)} %get-tuple-element.15.a_ref, f32[32,3072]{1,0:T(8,128)} %get-tuple-element.16.cs_ref, bf16[2048,128]{1,0:T(8,128)(2,1)} %pad_maximum_fusion.1.mixed_ref), custom_call_target="tpu_custom_call" | custom-call | tf_op jit(solution)/shard_map/pallas_call | solution.py:297
  150.4 6.1 %collective-permute-start.16 = (f32[64,1536]{1,0:T(8,128)}, f32[64,1536]{1,0:T(8,128)S(1)}, u32[]{:S(2)}, u32[]{:S(2)}) collective-permute-start(f32[64,1536]{1,0:T(8,128)} %get-tuple-element.24), channel_id=1, source_target_pairs={{0,1},{1,0},{2,3},{3,2},{4,5},{5,4},{6,7},{7,6},{8,9},{9,8},{10,11... | collective-permute-start | bytes 1179656 | tf_op jit(solution)/shard_map/ppermute | solution.py:325
  158.0 2.7 %fusion.5 = bf16[64,1536]{1,0:T(8,128)(2,1)} fusion(f32[64,1536]{1,0:T(8,128)} %get-tuple-element.23, f32[64,1536]{1,0:T(8,128)S(1)} %collective-permute-done.16, f32[64]{0:T(128)S(1)} %get-tuple-element.36, bf16[64,1536]{1,0:T(8,128)(2,1)S(1)} %copy-done.1, bf16[2,64,64]{2,1,0:T(8,128)(2,1)S(1)} %copy-done.7), kind=kOutput, calls=%fused_computation.12 | convolution fusion | flops 19267584 | bytes 1196544 | tf_op jit(solution)/shard_map/dot_general | solution.py:355
  (60 shorter events, 41.5 us)
Async XLA Ops:
  0.0 3.1 %collective-permute-start = (s32[3,1536]{1,0:T(4,128)}, s32[3,1536]{1,0:T(4,128)S(1)}, u32[]{:S(2)}, u32[]{:S(2)}) collective-permute-start(s32[3,1536]{1,0:T(4,128)} %param.7), channel_id=1, source_target_pairs={{0,1},{1,0},{2,3},{3,2},{4,5},{5,4},{6,7},{7,6},{8,9},{9,8},{10,11... | collective-permute-start | bytes 55304 | tf_op jit(solution)/shard_map/ppermute | solution.py:325
  0.1 7.5 %collective-permute-start.1 = (bf16[64,1536]{1,0:T(8,128)(2,1)}, bf16[64,1536]{1,0:T(8,128)(2,1)S(1)}, u32[]{:S(2)}, u32[]{:S(2)}) collective-permute-start(bf16[64,1536]{1,0:T(8,128)(2,1)} %own_ref.1), channel_id=1, source_target_pairs={{0,1},{1,0},{2,3},{3,2},{4,5},{5,4},{6,7},{7,6},{8,9},{9,8},{10,11... | collective-permute-start | bytes 589832 | tf_op jit(solution)/shard_map/ppermute | solution.py:325
  7.6 0.7 copy-start.3
  19.1 60.7 %copy-start.8 = (f32[2,64]{1,0:T(2,128)S(1)}, f32[2,64]{1,0:T(2,128)}, u32[]{:S(2)}) copy-start(f32[2,64]{1,0:T(2,128)} %param.12) | copy-start | bytes 1540
  19.1 60.7 %copy-start.2 = (bf16[64,1536]{1,0:T(8,128)(2,1)S(1)}, bf16[64,1536]{1,0:T(8,128)(2,1)}, u32[]{:S(2)}) copy-start(bf16[64,1536]{1,0:T(8,128)(2,1)} %own_ref.1) | copy-start | bytes 589828
  19.1 60.7 %copy-start.7 = (bf16[2,64,64]{2,1,0:T(8,128)(2,1)S(1)}, bf16[2,64,64]{2,1,0:T(8,128)(2,1)}, u32[]{:S(2)}) copy-start(bf16[2,64,64]{2,1,0:T(8,128)(2,1)} %param.11) | copy-start | bytes 49156
  19.1 8.7 %collective-permute-start.2 = (bf16[1024,128]{1,0:T(8,128)(2,1)}, bf16[1024,128]{1,0:T(8,128)(2,1)S(1)}, u32[]{:S(2)}, u32[]{:S(2)}) collective-permute-start(bf16[1024,128]{1,0:T(8,128)(2,1)} %get-tuple-element.18), channel_id=1, source_target_pairs={{0,2},{1,3},{2,0},{3,1},{4,6},{5,7},{6,4},{7,5},{8,10},{9,11},{10,... | collective-permute-start | bytes 786440 | tf_op jit(solution)/shard_map/ppermute | solution.py:325
  28.9 3.9 %collective-permute-start.3 = (bf16[512,128]{1,0:T(8,128)(2,1)S(1)}, bf16[512,128]{1,0:T(8,128)(2,1)S(1)}, u32[]{:S(2)}, u32[]{:S(2)}) collective-permute-start(bf16[512,128]{1,0:T(8,128)(2,1)S(1)} %get-tuple-element.30), channel_id=1, source_target_pairs={{0,4},{1,5},{2,6},{3,7},{4,0},{5,1},{6,2},{7,3},{8,12},{9,13},{10,... | collective-permute-start | bytes 393224 | tf_op jit(solution)/shard_map/ppermute | solution.py:325
  33.5 4.0 %collective-permute-start.4 = (bf16[256,128]{1,0:T(8,128)(2,1)S(1)}, bf16[256,128]{1,0:T(8,128)(2,1)S(1)}, u32[]{:S(2)}, u32[]{:S(2)}) collective-permute-start(bf16[256,128]{1,0:T(8,128)(2,1)S(1)} %get-tuple-element.34), channel_id=1, source_target_pairs={{0,8},{1,9},{2,10},{3,11},{4,12},{5,13},{6,14},{7,15},{8,0},{9,1},... | collective-permute-start | bytes 196616 | tf_op jit(solution)/shard_map/ppermute | solution.py:325
  44.5 4.2 %collective-permute-start.5 = (bf16[256,128]{1,0:T(8,128)(2,1)}, bf16[256,128]{1,0:T(8,128)(2,1)S(1)}, u32[]{:S(2)}, u32[]{:S(2)}) collective-permute-start(bf16[256,128]{1,0:T(8,128)(2,1)} %shard_map.75), channel_id=1, source_target_pairs={{0,8},{1,9},{2,10},{3,11},{4,12},{5,13},{6,14},{7,15},{8,0},{9,1},... | collective-permute-start | bytes 196616 | tf_op jit(solution)/shard_map/ppermute | solution.py:325
  49.6 4.3 %collective-permute-start.6 = (bf16[512,128]{1,0:T(8,128)(2,1)S(1)}, bf16[512,128]{1,0:T(8,128)(2,1)S(1)}, u32[]{:S(2)}, u32[]{:S(2)}) collective-permute-start(bf16[512,128]{1,0:T(8,128)(2,1)S(1)} %pad_maximum_fusion.4), channel_id=1, source_target_pairs={{0,4},{1,5},{2,6},{3,7},{4,0},{5,1},{6,2},{7,3},{8,12},{9,13},{10,... | collective-permute-start | bytes 393224 | tf_op jit(solution)/shard_map/ppermute | solution.py:325
  54.8 5.3 %collective-permute-start.7 = (bf16[1024,128]{1,0:T(8,128)(2,1)S(1)}, bf16[1024,128]{1,0:T(8,128)(2,1)S(1)}, u32[]{:S(2)}, u32[]{:S(2)}) collective-permute-start(bf16[1024,128]{1,0:T(8,128)(2,1)S(1)} %pad_maximum_fusion.2), channel_id=1, source_target_pairs={{0,2},{1,3},{2,0},{3,1},{4,6},{5,7},{6,4},{7,5},{8,10},{9,11},{10,... | collective-permute-start | bytes 786440 | tf_op jit(solution)/shard_map/ppermute | solution.py:325
  73.4 7.9 %collective-permute-start.8 = (f32[64,1536]{1,0:T(8,128)}, f32[64,1536]{1,0:T(8,128)S(1)}, u32[]{:S(2)}, u32[]{:S(2)}) collective-permute-start(f32[64,1536]{1,0:T(8,128)} %get-tuple-element.20), channel_id=1, source_target_pairs={{0,1},{1,0},{2,3},{3,2},{4,5},{5,4},{6,7},{7,6},{8,9},{9,8},{10,11... | collective-permute-start | bytes 1179656 | tf_op jit(solution)/shard_map/ppermute | solution.py:325
  83.2 1.5 copy-start
  83.2 1.5 collective-permute-start.9
  84.7 0.7 copy-start.4
  96.0 62.0 %copy-start.1 = (bf16[64,1536]{1,0:T(8,128)(2,1)S(1)}, bf16[64,1536]{1,0:T(8,128)(2,1)}, u32[]{:S(2)}) copy-start(bf16[64,1536]{1,0:T(8,128)(2,1)} %copy-done) | copy-start | bytes 589828
  96.0 7.8 %collective-permute-start.10 = (bf16[1024,128]{1,0:T(8,128)(2,1)}, bf16[1024,128]{1,0:T(8,128)(2,1)S(1)}, u32[]{:S(2)}, u32[]{:S(2)}) collective-permute-start(bf16[1024,128]{1,0:T(8,128)(2,1)} %get-tuple-element.22), channel_id=1, source_target_pairs={{0,2},{1,3},{2,0},{3,1},{4,6},{5,7},{6,4},{7,5},{8,10},{9,11},{10,... | collective-permute-start | bytes 786440 | tf_op jit(solution)/shard_map/ppermute | solution.py:325
  104.9 4.1 %collective-permute-start.11 = (bf16[512,128]{1,0:T(8,128)(2,1)S(1)}, bf16[512,128]{1,0:T(8,128)(2,1)S(1)}, u32[]{:S(2)}, u32[]{:S(2)}) collective-permute-start(bf16[512,128]{1,0:T(8,128)(2,1)S(1)} %get-tuple-element.28), channel_id=1, source_target_pairs={{0,4},{1,5},{2,6},{3,7},{4,0},{5,1},{6,2},{7,3},{8,12},{9,13},{10,... | collective-permute-start | bytes 393224 | tf_op jit(solution)/shard_map/ppermute | solution.py:325
  109.7 4.7 %collective-permute-start.12 = (bf16[256,128]{1,0:T(8,128)(2,1)S(1)}, bf16[256,128]{1,0:T(8,128)(2,1)S(1)}, u32[]{:S(2)}, u32[]{:S(2)}) collective-permute-start(bf16[256,128]{1,0:T(8,128)(2,1)S(1)} %get-tuple-element.32), channel_id=1, source_target_pairs={{0,8},{1,9},{2,10},{3,11},{4,12},{5,13},{6,14},{7,15},{8,0},{9,1},... | collective-permute-start | bytes 196616 | tf_op jit(solution)/shard_map/ppermute | solution.py:325
  121.4 4.3 %collective-permute-start.13 = (bf16[256,128]{1,0:T(8,128)(2,1)}, bf16[256,128]{1,0:T(8,128)(2,1)S(1)}, u32[]{:S(2)}, u32[]{:S(2)}) collective-permute-start(bf16[256,128]{1,0:T(8,128)(2,1)} %shard_map.78), channel_id=1, source_target_pairs={{0,8},{1,9},{2,10},{3,11},{4,12},{5,13},{6,14},{7,15},{8,0},{9,1},... | collective-permute-start | bytes 196616 | tf_op jit(solution)/shard_map/ppermute | solution.py:325
  126.5 4.3 %collective-permute-start.14 = (bf16[512,128]{1,0:T(8,128)(2,1)S(1)}, bf16[512,128]{1,0:T(8,128)(2,1)S(1)}, u32[]{:S(2)}, u32[]{:S(2)}) collective-permute-start(bf16[512,128]{1,0:T(8,128)(2,1)S(1)} %pad_maximum_fusion.5), channel_id=1, source_target_pairs={{0,4},{1,5},{2,6},{3,7},{4,0},{5,1},{6,2},{7,3},{8,12},{9,13},{10,... | collective-permute-start | bytes 393224 | tf_op jit(solution)/shard_map/ppermute | solution.py:325
  131.6 5.3 %collective-permute-start.15 = (bf16[1024,128]{1,0:T(8,128)(2,1)S(1)}, bf16[1024,128]{1,0:T(8,128)(2,1)S(1)}, u32[]{:S(2)}, u32[]{:S(2)}) collective-permute-start(bf16[1024,128]{1,0:T(8,128)(2,1)S(1)} %pad_maximum_fusion.3), channel_id=1, source_target_pairs={{0,2},{1,3},{2,0},{3,1},{4,6},{5,7},{6,4},{7,5},{8,10},{9,11},{10,... | collective-permute-start | bytes 786440 | tf_op jit(solution)/shard_map/ppermute | solution.py:325
  150.4 7.7 %collective-permute-start.16 = (f32[64,1536]{1,0:T(8,128)}, f32[64,1536]{1,0:T(8,128)S(1)}, u32[]{:S(2)}, u32[]{:S(2)}) collective-permute-start(f32[64,1536]{1,0:T(8,128)} %get-tuple-element.24), channel_id=1, source_target_pairs={{0,1},{1,0},{2,3},{3,2},{4,5},{5,4},{6,7},{7,6},{8,9},{9,8},{10,11... | collective-permute-start | bytes 1179656 | tf_op jit(solution)/shard_map/ppermute | solution.py:325
  (2 other events, 1.2 us)

commit v2 on v1

v2 whole, which is shorter than its diff:
```python
import math

import jax
import jax.numpy as jnp
from jax import lax
from jax.experimental import pallas as pl
from jax.experimental.pallas import tpu as pltpu
from jax.sharding import PartitionSpec as P

KDIM = 16
GRID = 1024
LAYERS = 2
TWO_PI = 2.0 * math.pi
HALF = KDIM // 2
KZ = HALF + 1
GROUPS = HALF + 3
ROWS_A = GROUPS * 32
ROWS_Q = KZ * ROWS_A
VMEM = 24 * 1024 * 1024
F32 = jnp.float32
BF16 = jnp.bfloat16


def params():
    return pltpu.CompilerParams(vmem_limit_bytes=VMEM)


def vmem():
    return pl.BlockSpec(memory_space=pltpu.VMEM)


def smem():
    return pl.BlockSpec(memory_space=pltpu.SMEM)


def table_rows(mode_list):
    kx = mode_list // (KDIM * KDIM) - HALF
    ky = mode_list // KDIM % KDIM - HALF
    kz = mode_list % KDIM - HALF
    flip = kx < 0
    ky = jnp.where(flip, -ky, ky)
    kz = jnp.where(flip, -kz, kz)
    ax, ay, az = jnp.abs(kx), jnp.abs(ky), jnp.abs(kz)
    quarter = 2 * (ky < 0).astype(jnp.int32) + (kz < 0).astype(jnp.int32)
    group = jnp.where(ay < HALF, ax, jnp.where(ax < HALF, HALF + 1, HALF + 2))
    inner = jnp.where(ay < HALF, ay, jnp.where(ax < HALF, ax, 0))
    row = ((az * GROUPS + group) * 4 + quarter) * 8 + inner
    return row, flip


def tables_kernel(own_ref, other_ref, a_ref, cs_ref):
    points = jnp.concatenate([own_ref[...], other_ref[...]], 1)
    angle = points.astype(F32) * (TWO_PI / GRID)
    one_c, one_s = jnp.cos(angle), jnp.sin(angle)
    cos, sin = [jnp.ones_like(angle), one_c], [jnp.zeros_like(angle), one_s]
    for k in range(2, HALF + 1):
        i, j = k // 2, k - k // 2
        cos.append(cos[i] * cos[j] - sin[i] * sin[j])
        sin.append(sin[i] * cos[j] + cos[i] * sin[j])
    cx = jnp.concatenate([c[0:1] for c in cos[:HALF]], 0)
    sx = jnp.concatenate([s[0:1] for s in sin[:HALF]], 0)
    cy = jnp.concatenate([c[1:2] for c in cos[:HALF]], 0)
    sy = jnp.concatenate([s[1:2] for s in sin[:HALF]], 0)
    for g in range(GROUPS):
        if g <= HALF:
            c, s = cos[g][0:1], sin[g][0:1]
            parts = [c * cy, c * sy, s * cy, s * sy]
        elif g == HALF + 1:
            c, s = cos[HALF][1:2], sin[HALF][1:2]
            parts = [cx * c, cx * s, sx * c, sx * s]
        else:
            c, s = cos[HALF][1:2], sin[HALF][1:2]
            first = (lax.broadcasted_iota(jnp.int32, cx.shape, 0) == 0).astype(F32)
            cl, sl = first * cos[HALF][0:1], first * sin[HALF][0:1]
            parts = [cl * c, cl * s, sl * c, sl * s]
        a_ref[g * 32 : (g + 1) * 32, :] = jnp.concatenate(parts, 0).astype(BF16)
    pad = jnp.zeros((7, angle.shape[1]), F32)
    cs_ref[...] = jnp.concatenate(
        [c[2:3] for c in cos] + [pad] + [s[2:3] for s in sin] + [pad], 0
    )


def make_tables(own, other):
    points = 2 * own.shape[1]
    return pl.pallas_call(
        tables_kernel,
        out_shape=(
            jax.ShapeDtypeStruct((ROWS_A, points), BF16),
            jax.ShapeDtypeStruct((32, points), F32),
        ),
        in_specs=[vmem(), vmem()],
        out_specs=(vmem(), vmem()),
        compiler_params=params(),
    )(own, other)


def sign_lanes(width):
    lane = lax.broadcasted_iota(jnp.int32, (8, 2 * width), 1)
    return jnp.where(lane < width, 1.0, -1.0).astype(F32)


def owners_of(count):
    bits = count.bit_length() - 1
    return [
        sum(((t >> (bits - 2 - b)) & 1) << (b + 1) for b in range(bits - 1))
        for t in range(count // 2)
    ]


def spectrum(norm, a_ref, cs_ref, own_ref, other_ref, q_ref, hs_ref, b_refs):
    width, points = own_ref.shape
    hs_ref[:, :points] = own_ref[...].astype(F32) * norm
    hs_ref[:, points:] = other_ref[...].astype(F32) * norm

    def product(b):
        return lax.dot_general(
            a_ref[...], b, (((1,), (1,)), ((), ())), preferred_element_type=F32
        )

    first = product(hs_ref[...].astype(BF16))
    q_ref[0:ROWS_A, :] = jnp.concatenate([first, jnp.zeros_like(first)], 1)

    for pair in range(HALF // 2):
        b_ref = b_refs[pair % 2]
        for half in range(2):
            k = 2 * pair + 1 + half
            b_ref[2 * half * width : (2 * half + 1) * width, :] = (
                hs_ref[...] * cs_ref[k : k + 1, :]
            ).astype(BF16)
            b_ref[(2 * half + 1) * width : (2 * half + 2) * width, :] = (
                hs_ref[...] * cs_ref[16 + k : 17 + k, :]
            ).astype(BF16)
        both = product(b_ref[...])
        k = 2 * pair + 1
        q_ref[k * ROWS_A : (k + 1) * ROWS_A, :] = both[:, : 2 * width]
        q_ref[(k + 1) * ROWS_A : (k + 2) * ROWS_A, :] = both[:, 2 * width :]

    sign = sign_lanes(width)

    def combine(i, carry):
        base = pl.multiple_of(i * 32, 32)
        cc = q_ref[pl.ds(base, 8), :]
        cs = q_ref[pl.ds(base + 8, 8), :]
        sc = q_ref[pl.ds(base + 16, 8), :]
        ss = q_ref[pl.ds(base + 24, 8), :]
        for y in range(2):
            u = cc + ss if y else cc - ss
            v = pltpu.roll(sc - cs if y else sc + cs, width, 1)
            q_ref[pl.ds(base + 16 * y, 8), :] = u * sign - v
            q_ref[pl.ds(base + 16 * y + 8, 8), :] = u + v * sign
        return carry

    lax.fori_loop(0, KZ * GROUPS, combine, 0, unroll=9)


def gather_rows(row_ref, me_ref, q_ref, out_ref, owners, local):
    for at, owner in enumerate(owners):
        base = jnp.bitwise_xor(me_ref[0], owner) * local

        def step(j, carry, base=base, at=at):
            out_ref[pl.ds(at * local + j, 1), :] = q_ref[pl.ds(row_ref[base + j], 1), :]
            return carry

        lax.fori_loop(0, local, step, 0, unroll=32)


def forward(rows, me, a, cs, own, other, norm, owners, local):
    width, points = own.shape
    sent = len(owners) * local

    def kernel(row_ref, me_ref, a_ref, cs_ref, own_ref, other_ref, q_ref, send_ref, hs_ref, b0_ref, b1_ref, stage_ref):
        spectrum(norm, a_ref, cs_ref, own_ref, other_ref, q_ref, hs_ref, (b0_ref, b1_ref))
        gather_rows(row_ref, me_ref, q_ref, stage_ref, owners, local)
        send_ref[...] = stage_ref[...].astype(BF16)

    return pl.pallas_call(
        kernel,
        out_shape=(
            jax.ShapeDtypeStruct((ROWS_Q, 2 * width), F32),
            jax.ShapeDtypeStruct((sent, 2 * width), BF16),
        ),
        in_specs=[smem()] * 2 + [vmem()] * 4,
        out_specs=(vmem(), vmem()),
        scratch_shapes=[
            pltpu.VMEM((width, 2 * points), F32),
            pltpu.VMEM((4 * width, 2 * points), BF16),
            pltpu.VMEM((4 * width, 2 * points), BF16),
            pltpu.VMEM((sent, 2 * width), F32),
        ],
        compiler_params=params(),
        name="forward",
    )(rows, me, a, cs, own, other)


def keep_rows(rows, me, q, owners, local):
    def kernel(row_ref, me_ref, q_ref, out_ref):
        gather_rows(row_ref, me_ref, q_ref, out_ref, owners, local)

    return pl.pallas_call(
        kernel,
        out_shape=jax.ShapeDtypeStruct((len(owners) * local, q.shape[1]), F32),
        in_specs=[smem()] * 2 + [vmem()],
        out_specs=vmem(),
        compiler_params=params(),
        name="keep_rows",
    )(rows, me, q)


def mix(keep, got, flip, weights, layer, scale):
    modes, double = keep.shape
    width = double // 2
    block = 16

    def kernel(keep_ref, got_ref, flip_ref, w_ref, out_ref, s_ref, acc_ref):
        step = pl.program_id(0)

        @pl.when(step == 0)
        def _():
            s_ref[...] = (keep_ref[...] + got_ref[...].astype(F32)).T
            s_ref[width:, :] = s_ref[width:, :] * flip_ref[...]

        def add(i, carry):
            real, imag = carry
            re = s_ref[pl.ds(i, 1), :]
            im = s_ref[pl.ds(width + i, 1), :]
            wr = w_ref[0, 0, i].astype(F32)
            wi = w_ref[0, 1, i].astype(F32)
            return real + re * wr - im * wi, imag + re * wi + im * wr

        zero = jnp.zeros((block, modes), F32)
        real, imag = lax.fori_loop(0, width, add, (zero, zero), unroll=16)
        at = pl.multiple_of(step * block, block)
        acc_ref[pl.ds(at, block), :] = real * scale
        acc_ref[pl.ds(width + at, block), :] = imag * (flip_ref[...] * scale)

        @pl.when(step == pl.num_programs(0) - 1)
        def _():
            out_ref[...] = acc_ref[...].T.astype(BF16)

    fixed = lambda i: (0, 0)
    return pl.pallas_call(
        kernel,
        grid=(width // block,),
        out_shape=jax.ShapeDtypeStruct((modes, double), BF16),
        in_specs=[
            pl.BlockSpec((modes, double), fixed),
            pl.BlockSpec((modes, double), fixed),
            pl.BlockSpec((1, modes), fixed),
            pl.BlockSpec((1, 2, width, block, modes), lambda i: (layer, 0, 0, i, 0)),
        ],
        out_specs=pl.BlockSpec((modes, double), fixed),
        scratch_shapes=[pltpu.VMEM((double, modes), F32), pltpu.VMEM((double, modes), F32)],
        compiler_params=params(),
        name="mix",
    )(keep, got, flip, weights)


def place_rows(place_ref, me_ref, m_ref, z_ref, owners, local):
    for at, owner in enumerate(owners):
        base = jnp.bitwise_xor(me_ref[0], owner) * local

        def step(j, carry, base=base, at=at):
            z_ref[pl.ds(place_ref[base + j], 1), :] = m_ref[pl.ds(at * local + j, 1), :]
            return carry

        lax.fori_loop(0, local, step, 0, unroll=32)


def place_first(places, me, pieces, owners, local):
    double = pieces[0].shape[1]
    count = len(owners) * local
    n = len(pieces)

    def kernel(place_ref, me_ref, *refs):
        z_ref, m_ref = refs[n:]
        at = 0
        for ref in refs[:n]:
            m_ref[at : at + ref.shape[0], :] = ref[...].astype(F32)
            at += ref.shape[0]

        def clear(i, carry):
            z_ref[pl.ds(pl.multiple_of(i * 32, 32), 32), :] = jnp.zeros((32, double), F32)
            return carry

        lax.fori_loop(0, 2 * ROWS_Q // 32, clear, 0, unroll=6)
        place_rows(place_ref, me_ref, m_ref, z_ref, owners, local)

    return pl.pallas_call(
        kernel,
        out_shape=jax.ShapeDtypeStruct((2 * ROWS_Q, double), F32),
        in_specs=[smem()] * 2 + [vmem()] * n,
        out_specs=vmem(),
        scratch_shapes=[pltpu.VMEM((count, double), F32)],
        compiler_params=params(),
        name="place_first",
    )(places, me, *pieces)


def evaluate(t_ref, a_ref, cs_ref, start, points, width, write):
    chunk = math.gcd(points, 512)
    for at in range(0, points, chunk):
        here = slice(start + at, start + at + chunk)
        r = lax.dot_general(
            t_ref[...], a_ref[:, here], (((1,), (0,)), ((), ())), preferred_element_type=F32
        )
        total = r[:width]
        for k in range(1, KZ):
            lo = 2 * k * width
            total = total + r[lo : lo + width] * cs_ref[k : k + 1, here]
            total = total + r[lo + width : lo + 2 * width] * cs_ref[16 + k : 17 + k, here]
        write(slice(at, at + chunk), total)


def inverse_other(places, me, z, piece, a, cs, owners, local):
    double = piece.shape[1]
    width = double // 2
    points = a.shape[1] // 2

    def kernel(place_ref, me_ref, z_ref, piece_ref, a_ref, cs_ref, other_ref, t_ref, zz_ref, m_ref):
        m_ref[...] = piece_ref[...].astype(F32)
        place_rows(place_ref, me_ref, m_ref, zz_ref, owners, local)
        sign = sign_lanes(width)

        def combine(i, carry):
            base = pl.multiple_of(i * 32, 32)
            u, v = [], []
            for y in range(2):
                lo = base + 16 * y
                plus = zz_ref[pl.ds(lo, 8), :] + zz_ref[pl.ds(ROWS_Q + lo, 8), :]
                minus = zz_ref[pl.ds(lo + 8, 8), :] + zz_ref[pl.ds(ROWS_Q + lo + 8, 8), :]
                u.append(plus * sign + minus)
                v.append(pltpu.roll(plus - minus * sign, width, 1))
            zz_ref[pl.ds(base, 8), :] = u[0] + u[1]
            zz_ref[pl.ds(base + 8, 8), :] = v[1] - v[0]
            zz_ref[pl.ds(base + 16, 8), :] = -v[0] - v[1]
            zz_ref[pl.ds(base + 24, 8), :] = u[1] - u[0]
            return carry

        lax.fori_loop(0, KZ * GROUPS, combine, 0, unroll=9)
        for k in range(KZ):
            t_ref[k * double : (k + 1) * double, :] = zz_ref[
                k * ROWS_A : (k + 1) * ROWS_A, :
            ].T.astype(BF16)

        def write(here, total):
            other_ref[:, here] = total

        evaluate(t_ref, a_ref, cs_ref, points, points, width, write)

    return pl.pallas_call(
        kernel,
        out_shape=(
            jax.ShapeDtypeStruct((width, points), F32),
            jax.ShapeDtypeStruct((KZ * double, ROWS_A), BF16),
            jax.ShapeDtypeStruct(z.shape, F32),
        ),
        in_specs=[smem()] * 2 + [vmem()] * 4,
        out_specs=(vmem(), vmem(), vmem()),
        input_output_aliases={2: 2},
        scratch_shapes=[pltpu.VMEM(piece.shape, F32)],
        compiler_params=params(),
        name="inverse_other",
    )(places, me, z, piece, a, cs)[:2]


def inverse_own(t, a, cs, field, weight, bias):
    width, points = field.shape

    def kernel(t_ref, a_ref, cs_ref, field_ref, weight_ref, bias_ref, out_ref):
        def write(here, total):
            direct = lax.dot_general(
                weight_ref[...],
                field_ref[:, here],
                (((0,), (0,)), ((), ())),
                preferred_element_type=F32,
            )
            out_ref[:, here] = total + direct + bias_ref[...]

        evaluate(t_ref, a_ref, cs_ref, 0, points, width, write)

    return pl.pallas_call(
        kernel,
        out_shape=jax.ShapeDtypeStruct((width, points), F32),
        in_specs=[vmem()] * 6,
        out_specs=vmem(),
        compiler_params=params(),
        name="inverse_own",
    )(t, a, cs, field, weight, bias)


def finish(own, got):
    def kernel(own_ref, got_ref, out_ref):
        x = own_ref[...] + got_ref[...]
        out_ref[...] = (0.5 * x * (1.0 + lax.erf(x * math.sqrt(0.5)))).astype(BF16)

    return pl.pallas_call(
        kernel,
        out_shape=jax.ShapeDtypeStruct(own.shape, BF16),
        in_specs=[vmem()] * 2,
        out_specs=vmem(),
        compiler_params=params(),
        name="finish",
    )(own, got)


def body(coords, field, mode_list, spec_weight, bypass_weight, bypass_bias):
    width, points = field.shape
    modes_total = mode_list.shape[0]
    count = lax.axis_size("pts")
    bits = count.bit_length() - 1
    me = lax.axis_index("pts")
    local = modes_total // count
    norm = 1.0 / math.sqrt(points * count)
    scale = 1.0 / math.sqrt(modes_total)

    def swap(x, bit):
        return lax.ppermute(x, "pts", [(i, i ^ (1 << bit)) for i in range(count)])

    rows, flip = table_rows(mode_list)
    places = rows + jnp.where(flip, ROWS_Q, 0)
    signs = jnp.where(flip, -1.0, 1.0).astype(F32)
    my_signs = lax.dynamic_slice(signs, (me * local,), (local,)).reshape(1, local)
    me_array = jnp.full((1,), me, jnp.int32)
    owners = owners_of(count)
    near, far = owners[: count // 4], owners[count // 4 :]
    weights = jnp.transpose(spec_weight, (0, 2, 3, 4, 1))

    a, cs = make_tables(coords, swap(coords, 0))
    for depth in range(LAYERS):
        q, send = forward(rows, me_array, a, cs, field, swap(field, 0), norm, far, local)
        got = swap(send, 1)
        keep = keep_rows(rows, me_array, q, near, local)
        for bit in range(2, bits):
            half = keep.shape[0] // 2
            send = (keep[half:] + got[half:].astype(F32)).astype(BF16)
            keep = keep[:half] + got[:half].astype(F32)
            got = swap(send, bit)
        mixed = mix(keep, got, my_signs, weights, depth, scale)
        pieces = [mixed]
        for bit in range(bits - 1, 1, -1):
            pieces.append(swap(jnp.concatenate(pieces, 0), bit))
        last = swap(jnp.concatenate(pieces, 0), 1)
        z = place_first(places, me_array, pieces, near, local)
        theirs, t = inverse_other(places, me_array, z, last, a, cs, far, local)
        got = swap(theirs, 0)
        own = inverse_own(t, a, cs, field, bypass_weight[depth], bypass_bias[depth][:, None])
        field = finish(own, got)
    return field


def solution(mesh):
    placed = (
        P(None, ("group", "pts")),
        P(None, ("group", "pts")),
        P(),
        P(None, "pts", None, None, None),
        P(),
        P(),
    )
    return jax.shard_map(
        body, mesh=mesh, in_specs=placed, out_specs=P(None, ("group", "pts")), check_vma=False
    )
```

time: 162 us -> 125 us (0.77)
  Pallas kernels: 60.7 us -> 44.2 us
  other arithmetic: 15.6 us -> 1.05 us
  local copies, waits for them, and re-layouts: 4.96 us -> 12.4 us
  starting transfers between devices: 36.6 us -> 30.6 us
  waiting for transfers between devices: 39.9 us -> 36.1 us
  matrix products: 2.96 us -> 0 us
    pallas_call x2, Pallas kernels: 12.8 us -> 4.11 us  [mix(): pl.pallas_call(kernel, grid=(width // block,), out_shape=jax.ShapeDtypeSt...]
    concatenate x7 -> x4, other arithmetic: 8.12 us -> 0.05 us  [the longest x2 0.04 us: body(): last = swap(jnp.concatenate(pieces, 0), 1)]
    unnamed x20 -> x16, local copies, waits for them, and re-layouts: 3.83 us -> 11.5 us
    ppermute x17, starting transfers between devices: 36.6 us -> 30.6 us  [swap(): return lax.ppermute(x, 'pts', [(i, i ^ 1 << bit) for i in range(count)])]
    pallas_call x4 -> x12, Pallas kernels: 44.8 us -> 38.9 us  [the longest x2 12.1 us: forward(): pl.pallas_call(kernel, out_shape=(jax.ShapeDtypeStruct((ROWS_Q, 2 * width...]
    ppermute x17, waiting for transfers between devices: 39.9 us -> 36.1 us  [swap(): return lax.ppermute(x, 'pts', [(i, i ^ 1 << bit) for i in range(count)])]
    convert_element_type x4, other arithmetic: 3.51 us -> 0.15 us  [body(): send = (keep[half:] + got[half:].astype(F32)).astype(BF16)]
    dot_general x2 -> x0, matrix products: 2.96 us -> none  [body(): lax.dot_general(bypass_weight[depth], field, (((0,), (0,)), ((), ())), pr...]
  transfers between devices with their start and end apart: 17 -> 17, of which waited for: 15 -> 14; matrix products, arithmetic and copies ran while one was open for 4% -> 1% of each run, Pallas kernels for 2% -> 11%
where the time goes in v2:
time: 125 us; the launch traced here: 124 us
  Pallas kernels  44.2 us (35%)
  waiting for transfers between devices  36.1 us (29%)
  starting transfers between devices  30.6 us (24%)
  local copies, waits for them, and re-layouts  12.4 us (10%)
    ppermute x17, waiting for transfers between devices, swap(): return lax.ppermute(x, 'pts', [(i, i ^ 1 << bit) for i in range(count)])  36.1 us
    ppermute x17, starting transfers between devices, swap(): return lax.ppermute(x, 'pts', [(i, i ^ 1 << bit) for i in range(count)])  30.6 us
    pallas_call x2, Pallas kernels, forward(): pl.pallas_call(kernel, out_shape=(jax.ShapeDtypeStruct((ROWS_Q, 2 * width...  12.1 us
    pallas_call x2, Pallas kernels, inverse_other(): pl.pallas_call(kernel, out_shape=(jax.ShapeDtypeStruct((width, points), F...  12 us
    unnamed x16, local copies, waits for them, and re-layouts  11.5 us
    pallas_call x2, Pallas kernels, place_first(): pl.pallas_call(kernel, out_shape=jax.ShapeDtypeStruct((2 * ROWS_Q, double...  4.64 us
    pallas_call x2, Pallas kernels, inverse_own(): pl.pallas_call(kernel, out_shape=jax.ShapeDtypeStruct((width, points), F3...  4.27 us
    pallas_call x2, Pallas kernels, mix(): pl.pallas_call(kernel, grid=(width // block,), out_shape=jax.ShapeDtypeSt...  4.11 us
  transfers between devices with their start and end apart: 17, of which 14 were waited for; matrix products, arithmetic and copies ran while one was open for 1% of the time, Pallas kernels for 11%

profile of v2, /device:TPU:1, one launch (start us, length us, event | category | flops | bytes accessed | tf_op | source)
XLA Modules:
  0.0 124.5 jit_solution(16161273262156996983)
XLA Ops:
  4.2 6.1 %forward.2 = (f32[3168,128]{1,0:T(8,128)S(1)}, bf16[1024,128]{1,0:T(8,128)(2,1)S(1)}) custom-call(s32[4096]{0:T(1024)S(1)} %get-tuple-element.26.row_ref, s32[1]{0:T(128)} %bitcast.me_ref, bf16[352,3072]{1,0:T(8,128)(2,1)S(1)} %get-tuple-element.15.a_ref, f32[32,3072]{1,0:T(8,128)S(1)} %get-tuple-element.16.cs_ref, bf16[64,1536]{1,0:T(8,128)(2,1)S(1)} %copy-done.4, ...), custom_call_target="tpu_custom_call" | custom-call | tf_op jit(solution)/shard_map/forward/pallas_call | solution.py:176
  10.4 2.5 %collective-permute-start.2 = (bf16[1024,128]{1,0:T(8,128)(2,1)S(1)}, bf16[1024,128]{1,0:T(8,128)(2,1)S(1)}, u32[]{:S(2)}, u32[]{:S(2)}) collective-permute-start(bf16[1024,128]{1,0:T(8,128)(2,1)S(1)} %get-tuple-element.18), channel_id=1, source_target_pairs={{0,2},{1,3},{2,0},{3,1},{4,6},{5,7},{6,4},{7,5},{8,10},{9,11},{10,... | collective-permute-start | bytes 786440 | tf_op jit(solution)/shard_map/ppermute | solution.py:417
  14.9 4.4 %collective-permute-done.2 = bf16[1024,128]{1,0:T(8,128)(2,1)S(1)} collective-permute-done((bf16[1024,128]{1,0:T(8,128)(2,1)S(1)}, bf16[1024,128]{1,0:T(8,128)(2,1)S(1)}, u32[]{:S(2)}, u32[]{:S(2)}) %collective-permute-start.2) | collective-permute-done | bytes 262176 | tf_op jit(solution)/shard_map/ppermute | solution.py:417
  20.5 2.9 %collective-permute-done.3 = bf16[512,128]{1,0:T(8,128)(2,1)S(1)} collective-permute-done((bf16[512,128]{1,0:T(8,128)(2,1)S(1)}, bf16[512,128]{1,0:T(8,128)(2,1)S(1)}, u32[]{:S(2)}, u32[]{:S(2)}) %collective-permute-start.3) | collective-permute-done | bytes 131104 | tf_op jit(solution)/shard_map/ppermute | solution.py:417
  25.5 2.8 %collective-permute-done.4.got_ref = bf16[256,128]{1,0:T(8,128)(2,1)S(1)} collective-permute-done((bf16[256,128]{1,0:T(8,128)(2,1)S(1)}, bf16[256,128]{1,0:T(8,128)(2,1)S(1)}, u32[]{:S(2)}, u32[]{:S(2)}) %collective-permute-start.4) | collective-permute-done | bytes 65568 | tf_op jit(solution)/shard_map/ppermute | solution.py:417
  28.3 3.4 %copy-done = bf16[2,256,2,64,64]{1,4,3,2,0:T(8,128)(2,1)S(1)} copy-done((bf16[2,256,2,64,64]{1,4,3,2,0:T(8,128)(2,1)S(1)}, bf16[2,256,2,64,64]{1,4,3,2,0:T(8,128)(2,1)}, u32[]{:S(2)}) %copy-start) | copy-done | bytes 8388632
  35.1 3.5 %collective-permute-done.5.refs_1_ = bf16[256,128]{1,0:T(8,128)(2,1)S(1)} collective-permute-done((bf16[256,128]{1,0:T(8,128)(2,1)S(1)}, bf16[256,128]{1,0:T(8,128)(2,1)S(1)}, u32[]{:S(2)}, u32[]{:S(2)}) %collective-permute-start.5) | collective-permute-done | bytes 65568 | tf_op jit(solution)/shard_map/ppermute | solution.py:417
  38.7 3.7 %collective-permute-done.6.refs_2_ = bf16[512,128]{1,0:T(8,128)(2,1)S(1)} collective-permute-done((bf16[512,128]{1,0:T(8,128)(2,1)S(1)}, bf16[512,128]{1,0:T(8,128)(2,1)S(1)}, u32[]{:S(2)}, u32[]{:S(2)}) %collective-permute-start.6) | collective-permute-done | bytes 131104 | tf_op jit(solution)/shard_map/ppermute | solution.py:417
  43.0 2.3 %place_first.2.z_ref = f32[6336,128]{1,0:T(8,128)S(1)} custom-call(s32[4096]{0:T(1024)S(1)} %get-tuple-element.25.place_ref, s32[1]{0:T(128)} %bitcast.me_ref, bf16[256,128]{1,0:T(8,128)(2,1)S(1)} %mix.2.refs_0_, bf16[256,128]{1,0:T(8,128)(2,1)S(1)} %collective-permute-done.5.refs_1_, bf16[512,128]{1,0:T(8,128)(2,1)S(1)} %collective-permute-done.6.refs_2_), custom_call_target="tpu_custom_call" | custom-call | tf_op jit(solution)/shard_map/place_first/pallas_call | solution.py:288
  45.3 2.4 %collective-permute-done.7.piece_ref = bf16[1024,128]{1,0:T(8,128)(2,1)S(1)} collective-permute-done((bf16[1024,128]{1,0:T(8,128)(2,1)S(1)}, bf16[1024,128]{1,0:T(8,128)(2,1)S(1)}, u32[]{:S(2)}, u32[]{:S(2)}) %collective-permute-start.7) | collective-permute-done | bytes 262176 | tf_op jit(solution)/shard_map/ppermute | solution.py:417
  47.7 5.9 %inverse_other.2 = (f32[64,1536]{1,0:T(8,128)}, bf16[1152,352]{1,0:T(8,128)(2,1)S(1)}, f32[6336,128]{1,0:T(8,128)S(1)}) custom-call(s32[4096]{0:T(1024)S(1)} %get-tuple-element.25.place_ref, s32[1]{0:T(128)} %bitcast.me_ref, f32[6336,128]{1,0:T(8,128)S(1)} %place_first.2.z_ref, ...), custom_call_target="tpu_custom_call", output_to_operand_aliasing={{2}: (2, {})} | custom-call | tf_op jit(solution)/shard_map/inverse_other/pallas_call | solution.py:350
  53.6 5.2 %collective-permute-start.8 = (f32[64,1536]{1,0:T(8,128)}, f32[64,1536]{1,0:T(8,128)}, u32[]{:S(2)}, u32[]{:S(2)}) collective-permute-start(f32[64,1536]{1,0:T(8,128)} %get-tuple-element.20), channel_id=1, source_target_pairs={{0,1},{1,0},{2,3},{3,2},{4,5},{5,4},{6,7},{7,6},{8,9},{9,8},{10,11... | collective-permute-start | bytes 1179656 | tf_op jit(solution)/shard_map/ppermute | solution.py:417
  60.6 2.1 %inverse_own.2.own_ref = f32[64,1536]{1,0:T(8,128)S(1)} custom-call(bf16[1152,352]{1,0:T(8,128)(2,1)S(1)} %get-tuple-element.19.t_ref, bf16[352,3072]{1,0:T(8,128)(2,1)S(1)} %get-tuple-element.15.a_ref, f32[32,3072]{1,0:T(8,128)S(1)} %get-tuple-element.16.cs_ref, bf16[64,1536]{1,0:T(8,128)(2,1)S(1)} %copy-done.5, ...), custom_call_target="tpu_custom_call" | custom-call | tf_op jit(solution)/shard_map/inverse_own/pallas_call | solution.py:381
  65.3 6.0 %forward.3 = (f32[3168,128]{1,0:T(8,128)S(1)}, bf16[1024,128]{1,0:T(8,128)(2,1)S(1)}) custom-call(s32[4096]{0:T(1024)S(1)} %get-tuple-element.26.row_ref, s32[1]{0:T(128)} %bitcast.me_ref, bf16[352,3072]{1,0:T(8,128)(2,1)S(1)} %get-tuple-element.15.a_ref, f32[32,3072]{1,0:T(8,128)S(1)} %get-tuple-element.16.cs_ref, ...), custom_call_target="tpu_custom_call" | custom-call | tf_op jit(solution)/shard_map/forward/pallas_call | solution.py:176
  74.7 4.4 %collective-permute-done.10 = bf16[1024,128]{1,0:T(8,128)(2,1)S(1)} collective-permute-done((bf16[1024,128]{1,0:T(8,128)(2,1)S(1)}, bf16[1024,128]{1,0:T(8,128)(2,1)S(1)}, u32[]{:S(2)}, u32[]{:S(2)}) %collective-permute-start.10) | collective-permute-done | bytes 262176 | tf_op jit(solution)/shard_map/ppermute | solution.py:417
  81.0 2.9 %collective-permute-done.11 = bf16[512,128]{1,0:T(8,128)(2,1)S(1)} collective-permute-done((bf16[512,128]{1,0:T(8,128)(2,1)S(1)}, bf16[512,128]{1,0:T(8,128)(2,1)S(1)}, u32[]{:S(2)}, u32[]{:S(2)}) %collective-permute-start.11) | collective-permute-done | bytes 131104 | tf_op jit(solution)/shard_map/ppermute | solution.py:417
  83.9 2.8 %collective-permute-start.12 = (bf16[256,128]{1,0:T(8,128)(2,1)S(1)}, bf16[256,128]{1,0:T(8,128)(2,1)S(1)}, u32[]{:S(2)}, u32[]{:S(2)}) collective-permute-start(bf16[256,128]{1,0:T(8,128)(2,1)S(1)} %get-tuple-element.32), channel_id=1, source_target_pairs={{0,8},{1,9},{2,10},{3,11},{4,12},{5,13},{6,14},{7,15},{8,0},{9,1},... | collective-permute-start | bytes 196616 | tf_op jit(solution)/shard_map/ppermute | solution.py:417
  88.3 3.4 %copy-done.1 = bf16[2,256,2,64,64]{1,4,3,2,0:T(8,128)(2,1)S(1)} copy-done((bf16[2,256,2,64,64]{1,4,3,2,0:T(8,128)(2,1)S(1)}, bf16[2,256,2,64,64]{1,4,3,2,0:T(8,128)(2,1)}, u32[]{:S(2)}) %copy-start.1) | copy-done | bytes 8388632
  93.8 2.5 %collective-permute-start.13 = (bf16[256,128]{1,0:T(8,128)(2,1)S(1)}, bf16[256,128]{1,0:T(8,128)(2,1)S(1)}, u32[]{:S(2)}, u32[]{:S(2)}) collective-permute-start(bf16[256,128]{1,0:T(8,128)(2,1)S(1)} %mix.3.refs_0_), channel_id=1, source_target_pairs={{0,8},{1,9},{2,10},{3,11},{4,12},{5,13},{6,14},{7,15},{8,0},{9,1},... | collective-permute-start | bytes 196616 | tf_op jit(solution)/shard_map/ppermute | solution.py:417
  99.7 2.6 %collective-permute-done.14.refs_2_ = bf16[512,128]{1,0:T(8,128)(2,1)S(1)} collective-permute-done((bf16[512,128]{1,0:T(8,128)(2,1)S(1)}, bf16[512,128]{1,0:T(8,128)(2,1)S(1)}, u32[]{:S(2)}, u32[]{:S(2)}) %collective-permute-start.14) | collective-permute-done | bytes 131104 | tf_op jit(solution)/shard_map/ppermute | solution.py:417
  103.7 2.3 %place_first.3.z_ref = f32[6336,128]{1,0:T(8,128)S(1)} custom-call(s32[4096]{0:T(1024)S(1)} %get-tuple-element.25.place_ref, s32[1]{0:T(128)} %bitcast.me_ref, bf16[256,128]{1,0:T(8,128)(2,1)S(1)} %mix.3.refs_0_, bf16[256,128]{1,0:T(8,128)(2,1)S(1)} %collective-permute-done.13.refs_1_, bf16[512,128]{1,0:T(8,128)(2,1)S(1)} %collective-permute-done.14.refs_2_), custom_call_target="tpu_custom_call" | custom-call | tf_op jit(solution)/shard_map/place_first/pallas_call | solution.py:288
  107.7 6.1 %inverse_other.3 = (f32[64,1536]{1,0:T(8,128)}, bf16[1152,352]{1,0:T(8,128)(2,1)S(1)}, f32[6336,128]{1,0:T(8,128)S(1)}) custom-call(s32[4096]{0:T(1024)S(1)} %get-tuple-element.25.place_ref, s32[1]{0:T(128)} %bitcast.me_ref, f32[6336,128]{1,0:T(8,128)S(1)} %place_first.3.z_ref, ...), custom_call_target="tpu_custom_call", output_to_operand_aliasing={{2}: (2, {})} | custom-call | tf_op jit(solution)/shard_map/inverse_other/pallas_call | solution.py:350
  114.7 5.6 %collective-permute-start.16 = (f32[64,1536]{1,0:T(8,128)}, f32[64,1536]{1,0:T(8,128)S(1)}, u32[]{:S(2)}, u32[]{:S(2)}) collective-permute-start(f32[64,1536]{1,0:T(8,128)} %get-tuple-element.24), channel_id=1, source_target_pairs={{0,1},{1,0},{2,3},{3,2},{4,5},{5,4},{6,7},{7,6},{8,9},{9,8},{10,11... | collective-permute-start | bytes 1179656 | tf_op jit(solution)/shard_map/ppermute | solution.py:417
  121.5 2.1 %inverse_own.3.own_ref = f32[64,1536]{1,0:T(8,128)S(1)} custom-call(bf16[1152,352]{1,0:T(8,128)(2,1)S(1)} %copy-done.3, bf16[352,3072]{1,0:T(8,128)(2,1)S(1)} %get-tuple-element.15.a_ref, f32[32,3072]{1,0:T(8,128)S(1)} %get-tuple-element.16.cs_ref, bf16[64,1536]{1,0:T(8,128)(2,1)S(1)} %finish.2.own_ref.field_ref, ...), custom_call_target="tpu_custom_call" | custom-call | tf_op jit(solution)/shard_map/inverse_own/pallas_call | solution.py:381
  (55 shorter events, 36.4 us)
Async XLA Ops:
  0.0 1.4 %collective-permute-start = (s32[3,1536]{1,0:T(4,128)}, s32[3,1536]{1,0:T(4,128)S(1)}, u32[]{:S(2)}, u32[]{:S(2)}) collective-permute-start(s32[3,1536]{1,0:T(4,128)} %own_ref.2), channel_id=1, source_target_pairs={{0,1},{1,0},{2,3},{3,2},{4,5},{5,4},{6,7},{7,6},{8,9},{9,8},{10,11... | collective-permute-start | bytes 55304 | tf_op jit(solution)/shard_map/ppermute | solution.py:417
  0.1 3.2 %collective-permute-start.1 = (bf16[64,1536]{1,0:T(8,128)(2,1)}, bf16[64,1536]{1,0:T(8,128)(2,1)S(1)}, u32[]{:S(2)}, u32[]{:S(2)}) collective-permute-start(bf16[64,1536]{1,0:T(8,128)(2,1)} %field_ref.1), channel_id=1, source_target_pairs={{0,1},{1,0},{2,3},{3,2},{4,5},{5,4},{6,7},{7,6},{8,9},{9,8},{10,11... | collective-permute-start | bytes 589832 | tf_op jit(solution)/shard_map/ppermute | solution.py:417
  3.3 0.9 copy-start.4
  10.4 8.9 %collective-permute-start.2 = (bf16[1024,128]{1,0:T(8,128)(2,1)S(1)}, bf16[1024,128]{1,0:T(8,128)(2,1)S(1)}, u32[]{:S(2)}, u32[]{:S(2)}) collective-permute-start(bf16[1024,128]{1,0:T(8,128)(2,1)S(1)} %get-tuple-element.18), channel_id=1, source_target_pairs={{0,2},{1,3},{2,0},{3,1},{4,6},{5,7},{6,4},{7,5},{8,10},{9,11},{10,... | collective-permute-start | bytes 786440 | tf_op jit(solution)/shard_map/ppermute | solution.py:417
  19.3 4.2 %collective-permute-start.3 = (bf16[512,128]{1,0:T(8,128)(2,1)S(1)}, bf16[512,128]{1,0:T(8,128)(2,1)S(1)}, u32[]{:S(2)}, u32[]{:S(2)}) collective-permute-start(bf16[512,128]{1,0:T(8,128)(2,1)S(1)} %get-tuple-element.30), channel_id=1, source_target_pairs={{0,4},{1,5},{2,6},{3,7},{4,0},{5,1},{6,2},{7,3},{8,12},{9,13},{10,... | collective-permute-start | bytes 393224 | tf_op jit(solution)/shard_map/ppermute | solution.py:417
  23.5 4.8 %collective-permute-start.4 = (bf16[256,128]{1,0:T(8,128)(2,1)S(1)}, bf16[256,128]{1,0:T(8,128)(2,1)S(1)}, u32[]{:S(2)}, u32[]{:S(2)}) collective-permute-start(bf16[256,128]{1,0:T(8,128)(2,1)S(1)} %get-tuple-element.34), channel_id=1, source_target_pairs={{0,8},{1,9},{2,10},{3,11},{4,12},{5,13},{6,14},{7,15},{8,0},{9,1},... | collective-permute-start | bytes 196616 | tf_op jit(solution)/shard_map/ppermute | solution.py:417
  28.3 3.4 %copy-start = (bf16[2,256,2,64,64]{1,4,3,2,0:T(8,128)(2,1)S(1)}, bf16[2,256,2,64,64]{1,4,3,2,0:T(8,128)(2,1)}, u32[]{:S(2)}) copy-start(bf16[2,256,2,64,64]{1,4,3,2,0:T(8,128)(2,1)} %param.9) | copy-start | bytes 25165828
  33.7 4.8 %collective-permute-start.5 = (bf16[256,128]{1,0:T(8,128)(2,1)S(1)}, bf16[256,128]{1,0:T(8,128)(2,1)S(1)}, u32[]{:S(2)}, u32[]{:S(2)}) collective-permute-start(bf16[256,128]{1,0:T(8,128)(2,1)S(1)} %mix.2.refs_0_), channel_id=1, source_target_pairs={{0,8},{1,9},{2,10},{3,11},{4,12},{5,13},{6,14},{7,15},{8,0},{9,1},... | collective-permute-start | bytes 196616 | tf_op jit(solution)/shard_map/ppermute | solution.py:417
  38.5 3.9 %collective-permute-start.6 = (bf16[512,128]{1,0:T(8,128)(2,1)S(1)}, bf16[512,128]{1,0:T(8,128)(2,1)S(1)}, u32[]{:S(2)}, u32[]{:S(2)}) collective-permute-start(bf16[512,128]{1,0:T(8,128)(2,1)S(1)} %pad_maximum_fusion.2), channel_id=1, source_target_pairs={{0,4},{1,5},{2,6},{3,7},{4,0},{5,1},{6,2},{7,3},{8,12},{9,13},{10,... | collective-permute-start | bytes 393224 | tf_op jit(solution)/shard_map/ppermute | solution.py:417
  42.4 5.3 %collective-permute-start.7 = (bf16[1024,128]{1,0:T(8,128)(2,1)S(1)}, bf16[1024,128]{1,0:T(8,128)(2,1)S(1)}, u32[]{:S(2)}, u32[]{:S(2)}) collective-permute-start(bf16[1024,128]{1,0:T(8,128)(2,1)S(1)} %pad_maximum_fusion), channel_id=1, source_target_pairs={{0,2},{1,3},{2,0},{3,1},{4,6},{5,7},{6,4},{7,5},{8,10},{9,11},{10,... | collective-permute-start | bytes 786440 | tf_op jit(solution)/shard_map/ppermute | solution.py:417
  45.3 13.5 %copy-start.7 = (f32[2,64]{1,0:T(2,128)S(1)}, f32[2,64]{1,0:T(2,128)}, u32[]{:S(2)}) copy-start(f32[2,64]{1,0:T(2,128)} %param.11) | copy-start | bytes 1540
  53.6 9.1 %collective-permute-start.8 = (f32[64,1536]{1,0:T(8,128)}, f32[64,1536]{1,0:T(8,128)}, u32[]{:S(2)}, u32[]{:S(2)}) collective-permute-start(f32[64,1536]{1,0:T(8,128)} %get-tuple-element.20), channel_id=1, source_target_pairs={{0,1},{1,0},{2,3},{3,2},{4,5},{5,4},{6,7},{7,6},{8,9},{9,8},{10,11... | collective-permute-start | bytes 1179656 | tf_op jit(solution)/shard_map/ppermute | solution.py:417
  59.7 0.9 copy-start.5
  63.8 1.5 %collective-permute-start.9 = (bf16[64,1536]{1,0:T(8,128)(2,1)S(1)}, bf16[64,1536]{1,0:T(8,128)(2,1)S(1)}, u32[]{:S(2)}, u32[]{:S(2)}) collective-permute-start(bf16[64,1536]{1,0:T(8,128)(2,1)S(1)} %finish.2.own_ref.field_ref), channel_id=1, source_target_pairs={{0,1},{1,0},{2,3},{3,2},{4,5},{5,4},{6,7},{7,6},{8,9},{9,8},{10,11... | collective-permute-start | bytes 589832 | tf_op jit(solution)/shard_map/ppermute | solution.py:417
  71.3 7.8 %collective-permute-start.10 = (bf16[1024,128]{1,0:T(8,128)(2,1)S(1)}, bf16[1024,128]{1,0:T(8,128)(2,1)S(1)}, u32[]{:S(2)}, u32[]{:S(2)}) collective-permute-start(bf16[1024,128]{1,0:T(8,128)(2,1)S(1)} %get-tuple-element.22), channel_id=1, source_target_pairs={{0,2},{1,3},{2,0},{3,1},{4,6},{5,7},{6,4},{7,5},{8,10},{9,11},{10,... | collective-permute-start | bytes 786440 | tf_op jit(solution)/shard_map/ppermute | solution.py:417
  79.2 4.7 %collective-permute-start.11 = (bf16[512,128]{1,0:T(8,128)(2,1)S(1)}, bf16[512,128]{1,0:T(8,128)(2,1)S(1)}, u32[]{:S(2)}, u32[]{:S(2)}) collective-permute-start(bf16[512,128]{1,0:T(8,128)(2,1)S(1)} %get-tuple-element.28), channel_id=1, source_target_pairs={{0,4},{1,5},{2,6},{3,7},{4,0},{5,1},{6,2},{7,3},{8,12},{9,13},{10,... | collective-permute-start | bytes 393224 | tf_op jit(solution)/shard_map/ppermute | solution.py:417
  83.9 4.4 %collective-permute-start.12 = (bf16[256,128]{1,0:T(8,128)(2,1)S(1)}, bf16[256,128]{1,0:T(8,128)(2,1)S(1)}, u32[]{:S(2)}, u32[]{:S(2)}) collective-permute-start(bf16[256,128]{1,0:T(8,128)(2,1)S(1)} %get-tuple-element.32), channel_id=1, source_target_pairs={{0,8},{1,9},{2,10},{3,11},{4,12},{5,13},{6,14},{7,15},{8,0},{9,1},... | collective-permute-start | bytes 196616 | tf_op jit(solution)/shard_map/ppermute | solution.py:417
  88.3 3.4 %copy-start.1 = (bf16[2,256,2,64,64]{1,4,3,2,0:T(8,128)(2,1)S(1)}, bf16[2,256,2,64,64]{1,4,3,2,0:T(8,128)(2,1)}, u32[]{:S(2)}) copy-start(bf16[2,256,2,64,64]{1,4,3,2,0:T(8,128)(2,1)} %param.9) | copy-start | bytes 25165828
  93.8 4.2 %collective-permute-start.13 = (bf16[256,128]{1,0:T(8,128)(2,1)S(1)}, bf16[256,128]{1,0:T(8,128)(2,1)S(1)}, u32[]{:S(2)}, u32[]{:S(2)}) collective-permute-start(bf16[256,128]{1,0:T(8,128)(2,1)S(1)} %mix.3.refs_0_), channel_id=1, source_target_pairs={{0,8},{1,9},{2,10},{3,11},{4,12},{5,13},{6,14},{7,15},{8,0},{9,1},... | collective-permute-start | bytes 196616 | tf_op jit(solution)/shard_map/ppermute | solution.py:417
  98.0 4.4 %collective-permute-start.14 = (bf16[512,128]{1,0:T(8,128)(2,1)S(1)}, bf16[512,128]{1,0:T(8,128)(2,1)S(1)}, u32[]{:S(2)}, u32[]{:S(2)}) collective-permute-start(bf16[512,128]{1,0:T(8,128)(2,1)S(1)} %pad_maximum_fusion.3), channel_id=1, source_target_pairs={{0,4},{1,5},{2,6},{3,7},{4,0},{5,1},{6,2},{7,3},{8,12},{9,13},{10,... | collective-permute-start | bytes 393224 | tf_op jit(solution)/shard_map/ppermute | solution.py:417
  102.4 5.3 %collective-permute-start.15 = (bf16[1024,128]{1,0:T(8,128)(2,1)S(1)}, bf16[1024,128]{1,0:T(8,128)(2,1)S(1)}, u32[]{:S(2)}, u32[]{:S(2)}) collective-permute-start(bf16[1024,128]{1,0:T(8,128)(2,1)S(1)} %pad_maximum_fusion.1), channel_id=1, source_target_pairs={{0,2},{1,3},{2,0},{3,1},{4,6},{5,7},{6,4},{7,5},{8,10},{9,11},{10,... | collective-permute-start | bytes 786440 | tf_op jit(solution)/shard_map/ppermute | solution.py:417
  113.8 0.9 copy-start.2
  114.7 9.0 %collective-permute-start.16 = (f32[64,1536]{1,0:T(8,128)}, f32[64,1536]{1,0:T(8,128)S(1)}, u32[]{:S(2)}, u32[]{:S(2)}) collective-permute-start(f32[64,1536]{1,0:T(8,128)} %get-tuple-element.24), channel_id=1, source_target_pairs={{0,1},{1,0},{2,3},{3,2},{4,5},{5,4},{6,7},{7,6},{8,9},{9,8},{10,11... | collective-permute-start | bytes 1179656 | tf_op jit(solution)/shard_map/ppermute | solution.py:417
  120.4 1.2 copy-start.3
  (1 other events, 0.7 us)

commit v3 on v2

--- a/solution.py
+++ b/solution.py
@@ -19,6 +19,10 @@
 VMEM = 24 * 1024 * 1024
 F32 = jnp.float32
 BF16 = jnp.bfloat16
+
+
+def cost(microseconds):
+    return pl.CostEstimate(flops=int(microseconds * 1.1e9), bytes_accessed=0, transcendentals=0)
 
 
 def params():
@@ -88,9 +92,11 @@
             jax.ShapeDtypeStruct((ROWS_A, points), BF16),
             jax.ShapeDtypeStruct((32, points), F32),
         ),
-        in_specs=[vmem(), vmem()],
+        in_specs=[vmem()] * 2,
         out_specs=(vmem(), vmem()),
         compiler_params=params(),
+        cost_estimate=cost(1.2),
+        name="tables",
     )(own, other)
 
 
@@ -164,30 +170,33 @@
         lax.fori_loop(0, local, step, 0, unroll=32)
 
 
-def forward(rows, me, a, cs, own, other, norm, owners, local):
+def forward(rows, me, a, cs, own, other, norm, first, second, local):
     width, points = own.shape
-    sent = len(owners) * local
-
-    def kernel(row_ref, me_ref, a_ref, cs_ref, own_ref, other_ref, q_ref, send_ref, hs_ref, b0_ref, b1_ref, stage_ref):
+    shapes = [(len(owners) * local, 2 * width) for owners in (first, second)]
+
+    def kernel(row_ref, me_ref, a_ref, cs_ref, own_ref, other_ref, q_ref, first_ref, second_ref, hs_ref, b0_ref, b1_ref, stage_ref):
         spectrum(norm, a_ref, cs_ref, own_ref, other_ref, q_ref, hs_ref, (b0_ref, b1_ref))
-        gather_rows(row_ref, me_ref, q_ref, stage_ref, owners, local)
-        send_ref[...] = stage_ref[...].astype(BF16)
+        gather_rows(row_ref, me_ref, q_ref, stage_ref, first + second, local)
+        first_ref[...] = stage_ref[: shapes[0][0], :].astype(BF16)
+        second_ref[...] = stage_ref[shapes[0][0] :, :].astype(BF16)
 
     return pl.pallas_call(
         kernel,
         out_shape=(
             jax.ShapeDtypeStruct((ROWS_Q, 2 * width), F32),
-            jax.ShapeDtypeStruct((sent, 2 * width), BF16),
+            jax.ShapeDtypeStruct(shapes[0], BF16),
+            jax.ShapeDtypeStruct(shapes[1], BF16),
         ),
         in_specs=[smem()] * 2 + [vmem()] * 4,
-        out_specs=(vmem(), vmem()),
+        out_specs=(vmem(), vmem(), vmem()),
         scratch_shapes=[
             pltpu.VMEM((width, 2 * points), F32),
             pltpu.VMEM((4 * width, 2 * points), BF16),
             pltpu.VMEM((4 * width, 2 * points), BF16),
-            pltpu.VMEM((sent, 2 * width), F32),
+            pltpu.VMEM((shapes[0][0] + shapes[1][0], 2 * width), F32),
         ],
         compiler_params=params(),
+        cost_estimate=cost(6.0),
         name="forward",
     )(rows, me, a, cs, own, other)
 
@@ -202,57 +211,71 @@
         in_specs=[smem()] * 2 + [vmem()],
         out_specs=vmem(),
         compiler_params=params(),
+        cost_estimate=cost(2.0),
         name="keep_rows",
     )(rows, me, q)
 
 
-def mix(keep, got, flip, weights, layer, scale):
-    modes, double = keep.shape
+def merge(keep, got, count):
+    rows = got.shape[0] // count
+
+    def kernel(keep_ref, got_ref, *out_refs):
+        for n, ref in enumerate(out_refs):
+            here = slice(n * rows, (n + 1) * rows)
+            total = keep_ref[rows + n * rows : 2 * rows + n * rows, :] + got_ref[here, :].astype(F32)
+            ref[...] = total.astype(BF16)
+
+    return pl.pallas_call(
+        kernel,
+        out_shape=(jax.ShapeDtypeStruct((rows, got.shape[1]), BF16),) * count,
+        in_specs=[vmem()] * 2,
+        out_specs=(vmem(),) * count,
+        compiler_params=params(),
+        cost_estimate=cost(0.3),
+        name="merge",
+    )(keep, got)
+
+
+def mix(keep, gots, flip, weights, layer, scale):
+    modes, double = flip.shape[1], keep.shape[1]
     width = double // 2
     block = 16
 
-    def kernel(keep_ref, got_ref, flip_ref, w_ref, out_ref, s_ref, acc_ref):
-        step = pl.program_id(0)
-
-        @pl.when(step == 0)
-        def _():
-            s_ref[...] = (keep_ref[...] + got_ref[...].astype(F32)).T
-            s_ref[width:, :] = s_ref[width:, :] * flip_ref[...]
-
-        def add(i, carry):
-            real, imag = carry
-            re = s_ref[pl.ds(i, 1), :]
-            im = s_ref[pl.ds(width + i, 1), :]
-            wr = w_ref[0, 0, i].astype(F32)
-            wi = w_ref[0, 1, i].astype(F32)
-            return real + re * wr - im * wi, imag + re * wi + im * wr
-
-        zero = jnp.zeros((block, modes), F32)
-        real, imag = lax.fori_loop(0, width, add, (zero, zero), unroll=16)
-        at = pl.multiple_of(step * block, block)
-        acc_ref[pl.ds(at, block), :] = real * scale
-        acc_ref[pl.ds(width + at, block), :] = imag * (flip_ref[...] * scale)
-
-        @pl.when(step == pl.num_programs(0) - 1)
-        def _():
-            out_ref[...] = acc_ref[...].T.astype(BF16)
-
-    fixed = lambda i: (0, 0)
-    return pl.pallas_call(
-        kernel,
-        grid=(width // block,),
+    def kernel(flip_ref, w_ref, keep_ref, *refs):
+        got_refs, (out_ref, s_ref, acc_ref) = refs[:-3], refs[-3:]
+        total = keep_ref[:modes, :]
+        for ref in got_refs:
+            total = total + ref[...].astype(F32)
+        s_ref[...] = total.T
+        s_ref[width:, :] = s_ref[width:, :] * flip_ref[...]
+
+        for at in range(0, width, block):
+
+            def add(i, carry, at=at):
+                real, imag = carry
+                re = s_ref[pl.ds(i, 1), :]
+                im = s_ref[pl.ds(width + i, 1), :]
+                wr = w_ref[layer, 0, i, at : at + block].astype(F32)
+                wi = w_ref[layer, 1, i, at : at + block].astype(F32)
+                return real + re * wr - im * wi, imag + re * wi + im * wr
+
+            zero = jnp.zeros((block, modes), F32)
+            real, imag = lax.fori_loop(0, width, add, (zero, zero), unroll=16)
+            acc_ref[at : at + block, :] = real * scale
+            acc_ref[width + at : width + at + block, :] = imag * (flip_ref[...] * scale)
+
+        out_ref[...] = acc_ref[...].T.astype(BF16)
+
+    return pl.pallas_call(
+        kernel,
         out_shape=jax.ShapeDtypeStruct((modes, double), BF16),
-        in_specs=[
-            pl.BlockSpec((modes, double), fixed),
-            pl.BlockSpec((modes, double), fixed),
-            pl.BlockSpec((1, modes), fixed),
-            pl.BlockSpec((1, 2, width, block, modes), lambda i: (layer, 0, 0, i, 0)),
-        ],
-        out_specs=pl.BlockSpec((modes, double), fixed),
+        in_specs=[vmem()] * (3 + len(gots)),
+        out_specs=vmem(),
         scratch_shapes=[pltpu.VMEM((double, modes), F32), pltpu.VMEM((double, modes), F32)],
         compiler_params=params(),
+        cost_estimate=cost(1.8),
         name="mix",
-    )(keep, got, flip, weights)
+    )(flip, weights, keep, *gots)
 
 
 def place_rows(place_ref, me_ref, m_ref, z_ref, owners, local):
@@ -266,34 +289,48 @@
         lax.fori_loop(0, local, step, 0, unroll=32)
 
 
-def place_first(places, me, pieces, owners, local):
+def clear_table(double):
+    def kernel(z_ref):
+        def clear(i, carry):
+            z_ref[pl.ds(pl.multiple_of(i * 32, 32), 32), :] = jnp.zeros((32, double), F32)
+            return carry
+
+        lax.fori_loop(0, 2 * ROWS_Q // 32, clear, 0, unroll=6)
+
+    return pl.pallas_call(
+        kernel,
+        out_shape=jax.ShapeDtypeStruct((2 * ROWS_Q, double), F32),
+        out_specs=vmem(),
+        compiler_params=params(),
+        cost_estimate=cost(0.8),
+        name="clear_table",
+    )()
+
+
+def place_pieces(places, me, z, pieces, owners, local):
     double = pieces[0].shape[1]
     count = len(owners) * local
     n = len(pieces)
 
-    def kernel(place_ref, me_ref, *refs):
+    def kernel(place_ref, me_ref, before_ref, *refs):
         z_ref, m_ref = refs[n:]
         at = 0
         for ref in refs[:n]:
             m_ref[at : at + ref.shape[0], :] = ref[...].astype(F32)
             at += ref.shape[0]
-
-        def clear(i, carry):
-            z_ref[pl.ds(pl.multiple_of(i * 32, 32), 32), :] = jnp.zeros((32, double), F32)
-            return carry
-
-        lax.fori_loop(0, 2 * ROWS_Q // 32, clear, 0, unroll=6)
         place_rows(place_ref, me_ref, m_ref, z_ref, owners, local)
 
     return pl.pallas_call(
         kernel,
-        out_shape=jax.ShapeDtypeStruct((2 * ROWS_Q, double), F32),
-        in_specs=[smem()] * 2 + [vmem()] * n,
+        out_shape=jax.ShapeDtypeStruct(z.shape, F32),
+        in_specs=[smem()] * 2 + [vmem()] * (n + 1),
         out_specs=vmem(),
+        input_output_aliases={2: 0},
         scratch_shapes=[pltpu.VMEM((count, double), F32)],
         compiler_params=params(),
-        name="place_first",
-    )(places, me, *pieces)
+        cost_estimate=cost(0.5 + 0.45 * count / 256),
+        name="place_pieces",
+    )(places, me, z, *pieces)
 
 
 def evaluate(t_ref, a_ref, cs_ref, start, points, width, write):
@@ -359,22 +396,29 @@
         input_output_aliases={2: 2},
         scratch_shapes=[pltpu.VMEM(piece.shape, F32)],
         compiler_params=params(),
+        cost_estimate=cost(4.5),
         name="inverse_other",
     )(places, me, z, piece, a, cs)[:2]
 
 
-def inverse_own(t, a, cs, field, weight, bias):
+def inverse_own(t, a, cs, field, weight, bias, layer):
     width, points = field.shape
 
     def kernel(t_ref, a_ref, cs_ref, field_ref, weight_ref, bias_ref, out_ref):
+        diagonal = lax.broadcasted_iota(jnp.int32, (width, width), 0) == lax.broadcasted_iota(
+            jnp.int32, (width, width), 1
+        )
+        row = bias_ref[layer : layer + 1, :]
+        column = jnp.sum(jnp.where(diagonal, row, 0.0), axis=1, keepdims=True)
+
         def write(here, total):
             direct = lax.dot_general(
-                weight_ref[...],
+                weight_ref[layer],
                 field_ref[:, here],
                 (((0,), (0,)), ((), ())),
                 preferred_element_type=F32,
             )
-            out_ref[:, here] = total + direct + bias_ref[...]
+            out_ref[:, here] = total + direct + column
 
         evaluate(t_ref, a_ref, cs_ref, 0, points, width, write)
 
@@ -384,6 +428,7 @@
         in_specs=[vmem()] * 6,
         out_specs=vmem(),
         compiler_params=params(),
+        cost_estimate=cost(2.1),
         name="inverse_own",
     )(t, a, cs, field, weight, bias)
 
@@ -399,6 +444,7 @@
         in_specs=[vmem()] * 2,
         out_specs=vmem(),
         compiler_params=params(),
+        cost_estimate=cost(0.8),
         name="finish",
     )(own, got)
 
@@ -413,8 +459,8 @@
     norm = 1.0 / math.sqrt(points * count)
     scale = 1.0 / math.sqrt(modes_total)
 
-    def swap(x, bit):
-        return lax.ppermute(x, "pts", [(i, i ^ (1 << bit)) for i in range(count)])
+    def swap(x, mask):
+        return lax.ppermute(x, "pts", [(i, i ^ mask) for i in range(count)])
 
     rows, flip = table_rows(mode_list)
     places = rows + jnp.where(flip, ROWS_Q, 0)
@@ -425,25 +471,44 @@
     near, far = owners[: count // 4], owners[count // 4 :]
     weights = jnp.transpose(spec_weight, (0, 2, 3, 4, 1))
 
-    a, cs = make_tables(coords, swap(coords, 0))
+    quad = count // 8
+    part = quad // 2 * local
+
+    theirs = swap(field, 1)
+    a, cs = make_tables(coords, swap(coords, 1))
     for depth in range(LAYERS):
-        q, send = forward(rows, me_array, a, cs, field, swap(field, 0), norm, far, local)
-        got = swap(send, 1)
+        if depth:
+            theirs = swap(field, 1)
+        q, far_send, near_send = forward(
+            rows, me_array, a, cs, field, theirs, norm, far[quad // 2 :], far[: quad // 2], local
+        )
+        far_got, near_got = swap(far_send, 2), swap(near_send, 2)
         keep = keep_rows(rows, me_array, q, near, local)
-        for bit in range(2, bits):
-            half = keep.shape[0] // 2
-            send = (keep[half:] + got[half:].astype(F32)).astype(BF16)
-            keep = keep[:half] + got[:half].astype(F32)
-            got = swap(send, bit)
-        mixed = mix(keep, got, my_signs, weights, depth, scale)
-        pieces = [mixed]
-        for bit in range(bits - 1, 1, -1):
-            pieces.append(swap(jnp.concatenate(pieces, 0), bit))
-        last = swap(jnp.concatenate(pieces, 0), 1)
-        z = place_first(places, me_array, pieces, near, local)
-        theirs, t = inverse_other(places, me_array, z, last, a, cs, far, local)
-        got = swap(theirs, 0)
-        own = inverse_own(t, a, cs, field, bypass_weight[depth], bypass_bias[depth][:, None])
+        sends = merge(keep, far_got, 3)
+        gots = [near_got] + [swap(x, mask) for x, mask in zip(sends, (8, 4, 12))]
+        for bit in range(4, bits):
+            total = keep[:part] if bit == 4 else keep
+            for got in gots:
+                total = total + got.astype(F32)
+            half = total.shape[0] // 2
+            keep = total[:half]
+            gots = [swap(total[half:].astype(BF16), 1 << bit)]
+        pieces = mix(keep, gots, my_signs, weights, depth, scale)
+        z = clear_table(2 * width)
+        for bit in range(bits - 1, 3, -1):
+            pieces = jnp.concatenate([pieces, swap(pieces, 1 << bit)], 0)
+        over = swap(pieces, 8)
+        z = place_pieces(places, me_array, z, [pieces], near[: quad // 2], local)
+        pieces = jnp.concatenate([pieces, over], 0)
+        across, far_first = swap(pieces, 4), swap(pieces, 2)
+        z = place_pieces(places, me_array, z, [over], near[quad // 2 : quad], local)
+        last = swap(across, 2)
+        z = place_pieces(
+            places, me_array, z, [across, far_first], near[quad:] + far[:quad], local
+        )
+        theirs, t = inverse_other(places, me_array, z, last, a, cs, far[quad:], local)
+        got = swap(theirs, 1)
+        own = inverse_own(t, a, cs, field, bypass_weight, bypass_bias, depth)
         field = finish(own, got)
     return field
 

time: 125 us -> 105 us (0.84)
  local copies, waits for them, and re-layouts: 12.4 us -> 0.77 us
  waiting for transfers between devices: 36.1 us -> 30.9 us
  starting transfers between devices: 30.6 us -> 28.1 us
    unnamed x16 -> x12, local copies, waits for them, and re-layouts: 11.5 us -> 0.77 us
    ppermute x17 -> x23, waiting for transfers between devices: 36.1 us -> 30.9 us  [swap(): return lax.ppermute(x, 'pts', [(i, i ^ mask) for i in range(count)])]
    pallas_call x4 -> x12, Pallas kernels: 8.75 us -> 12.4 us  [the longest x6 8.58 us: place_pieces(): pl.pallas_call(kernel, out_shape=jax.ShapeDtypeStruct(z.shape, F32), in_s...]
    pallas_call x2, Pallas kernels: 12 us -> 9.25 us  [inverse_other(): pl.pallas_call(kernel, out_shape=(jax.ShapeDtypeStruct((width, points), F...]
    ppermute x17 -> x23, starting transfers between devices: 30.6 us -> 28.1 us  [swap(): return lax.ppermute(x, 'pts', [(i, i ^ mask) for i in range(count)])]
  transfers between devices with their start and end apart: 17 -> 23, of which waited for: 14 -> 16; matrix products, arithmetic and copies ran while one was open for 1% -> 1% of each run, Pallas kernels for 11% -> 18%
where the time goes in v3:
time: 105 us
  Pallas kernels  44.2 us (42%)
  waiting for transfers between devices  30.9 us (29%)
  starting transfers between devices  28.1 us (27%)
    ppermute x23, waiting for transfers between devices, swap(): return lax.ppermute(x, 'pts', [(i, i ^ mask) for i in range(count)])  30.9 us
    ppermute x23, starting transfers between devices, swap(): return lax.ppermute(x, 'pts', [(i, i ^ mask) for i in range(count)])  28.1 us
    pallas_call x2, Pallas kernels, forward(): pl.pallas_call(kernel, out_shape=(jax.ShapeDtypeStruct((ROWS_Q, 2 * width...  12.1 us
    pallas_call x2, Pallas kernels, inverse_other(): pl.pallas_call(kernel, out_shape=(jax.ShapeDtypeStruct((width, points), F...  9.25 us
    pallas_call x6, Pallas kernels, place_pieces(): pl.pallas_call(kernel, out_shape=jax.ShapeDtypeStruct(z.shape, F32), in_s...  8.58 us
    pallas_call x2, Pallas kernels, inverse_own(): pl.pallas_call(kernel, out_shape=jax.ShapeDtypeStruct((width, points), F3...  4.32 us
    pallas_call x2, Pallas kernels, keep_rows(): pl.pallas_call(kernel, out_shape=jax.ShapeDtypeStruct((len(owners) * loca...  4.06 us
    pallas_call x2, Pallas kernels, mix(): pl.pallas_call(kernel, out_shape=jax.ShapeDtypeStruct((modes, double), BF...  3.3 us
  transfers between devices with their start and end apart: 23, of which 16 were waited for; matrix products, arithmetic and copies ran while one was open for 1% of the time, Pallas kernels for 18%

profile of v3, /device:TPU:1, one launch (start us, length us, event | category | flops | bytes accessed | tf_op | source)
XLA Modules:
  0.0 105.1 jit_solution(15151215395184290100)
XLA Ops:
  3.3 6.2 %forward.2 = (f32[3168,128]{1,0:T(8,128)S(1)}, bf16[768,128]{1,0:T(8,128)(2,1)S(1)}, bf16[256,128]{1,0:T(8,128)(2,1)S(1)}) custom-call(s32[4096]{0:T(1024)S(1)} %get-tuple-element.42.row_ref, s32[1]{0:T(128)} %bitcast.me_ref, bf16[352,3072]{1,0:T(8,128)(2,1)S(1)} %get-tuple-element.23.a_ref, f32[32,3072]{1,0:T(8,128)S(1)} %get-tuple-element.24.cs_ref, ...), custom_call_target="tpu_custom_call" | custom-call | flops 6600000000 | tf_op jit(solution)/shard_map/forward/pallas_call | solution.py:183
  9.5 2.5 %collective-permute-start.2 = (bf16[256,128]{1,0:T(8,128)(2,1)S(1)}, bf16[256,128]{1,0:T(8,128)(2,1)S(1)}, u32[]{:S(2)}, u32[]{:S(2)}) collective-permute-start(bf16[256,128]{1,0:T(8,128)(2,1)S(1)} %get-tuple-element.26), channel_id=1, source_target_pairs={{0,2},{1,3},{2,0},{3,1},{4,6},{5,7},{6,4},{7,5},{8,10},{9,11},{10,... | collective-permute-start | bytes 196616 | tf_op jit(solution)/shard_map/ppermute | solution.py:463
  12.0 2.0 %keep_rows.2.keep_ref = f32[1024,128]{1,0:T(8,128)S(1)} custom-call(s32[4096]{0:T(1024)S(1)} %get-tuple-element.42.row_ref, s32[1]{0:T(128)} %bitcast.me_ref, f32[3168,128]{1,0:T(8,128)S(1)} %get-tuple-element.25.q_ref), custom_call_target="tpu_custom_call" | custom-call | flops 2200000000 | tf_op jit(solution)/shard_map/keep_rows/pallas_call | solution.py:208
  14.1 3.7 %collective-permute-done.3.got_ref = bf16[768,128]{1,0:T(8,128)(2,1)S(1)} collective-permute-done((bf16[768,128]{1,0:T(8,128)(2,1)S(1)}, bf16[768,128]{1,0:T(8,128)(2,1)S(1)}, u32[]{:S(2)}, u32[]{:S(2)}) %collective-permute-start.3) | collective-permute-done | bytes 196640 | tf_op jit(solution)/shard_map/ppermute | solution.py:463
  17.8 2.9 %collective-permute-start.4 = (bf16[256,128]{1,0:T(8,128)(2,1)S(1)}, bf16[256,128]{1,0:T(8,128)(2,1)S(1)}, u32[]{:S(2)}, u32[]{:S(2)}) collective-permute-start(bf16[256,128]{1,0:T(8,128)(2,1)S(1)} %get-tuple-element.28), channel_id=1, source_target_pairs={{0,8},{1,9},{2,10},{3,11},{4,12},{5,13},{6,14},{7,15},{8,0},{9,1},... | collective-permute-start | bytes 196616 | tf_op jit(solution)/shard_map/ppermute | solution.py:463
  22.3 2.2 %collective-permute-done.5.refs_2_ = bf16[256,128]{1,0:T(8,128)(2,1)S(1)} collective-permute-done((bf16[256,128]{1,0:T(8,128)(2,1)S(1)}, bf16[256,128]{1,0:T(8,128)(2,1)S(1)}, u32[]{:S(2)}, u32[]{:S(2)}) %collective-permute-start.5) | collective-permute-done | bytes 65568 | tf_op jit(solution)/shard_map/ppermute | solution.py:463
  24.5 2.4 %collective-permute-done.6.refs_3_ = bf16[256,128]{1,0:T(8,128)(2,1)S(1)} collective-permute-done((bf16[256,128]{1,0:T(8,128)(2,1)S(1)}, bf16[256,128]{1,0:T(8,128)(2,1)S(1)}, u32[]{:S(2)}, u32[]{:S(2)}) %collective-permute-start.6) | collective-permute-done | bytes 65568 | tf_op jit(solution)/shard_map/ppermute | solution.py:463
  29.7 3.0 %collective-permute-done.7.refs_0_ = bf16[256,128]{1,0:T(8,128)(2,1)S(1)} collective-permute-done((bf16[256,128]{1,0:T(8,128)(2,1)S(1)}, bf16[256,128]{1,0:T(8,128)(2,1)S(1)}, u32[]{:S(2)}, u32[]{:S(2)}) %collective-permute-start.7) | collective-permute-done | bytes 65568 | tf_op jit(solution)/shard_map/ppermute | solution.py:463
  38.6 2.1 %place_pieces.8.z_ref = f32[6336,128]{1,0:T(8,128)S(1)} custom-call(s32[4096]{0:T(1024)S(1)} %get-tuple-element.41.place_ref, s32[1]{0:T(128)} %bitcast.me_ref, f32[6336,128]{1,0:T(8,128)S(1)} %place_pieces.7.before_ref, bf16[512,128]{1,0:T(8,128)(2,1)S(1)} %collective-permute-done.8.refs_0_, ...), custom_call_target="tpu_custom_call", output_to_operand_aliasing={{}: (2, {})} | custom-call | flops 2529999872 | tf_op jit(solution)/shard_map/place_pieces/pallas_call | solution.py:323
  40.7 2.1 %collective-permute-done.10.piece_ref = bf16[512,128]{1,0:T(8,128)(2,1)S(1)} collective-permute-done((bf16[512,128]{1,0:T(8,128)(2,1)S(1)}, bf16[512,128]{1,0:T(8,128)(2,1)S(1)}, u32[]{:S(2)}, u32[]{:S(2)}) %collective-permute-start.10) | collective-permute-done | bytes 131104 | tf_op jit(solution)/shard_map/ppermute | solution.py:463
  42.8 4.5 %inverse_other.2 = (f32[64,1536]{1,0:T(8,128)S(1)}, bf16[1152,352]{1,0:T(8,128)(2,1)S(1)}, f32[6336,128]{1,0:T(8,128)S(1)}) custom-call(s32[4096]{0:T(1024)S(1)} %get-tuple-element.41.place_ref, s32[1]{0:T(128)} %bitcast.me_ref, f32[6336,128]{1,0:T(8,128)S(1)} %place_pieces.8.z_ref, ...), custom_call_target="tpu_custom_call", output_to_operand_aliasing={{2}: (2, {})} | custom-call | flops 4950000128 | tf_op jit(solution)/shard_map/inverse_other/pallas_call | solution.py:387
  47.3 5.5 %collective-permute-start.11 = (f32[64,1536]{1,0:T(8,128)S(1)}, f32[64,1536]{1,0:T(8,128)S(1)}, u32[]{:S(2)}, u32[]{:S(2)}) collective-permute-start(f32[64,1536]{1,0:T(8,128)S(1)} %get-tuple-element.32), channel_id=1, source_target_pairs={{0,1},{1,0},{2,3},{3,2},{4,5},{5,4},{6,7},{7,6},{8,9},{9,8},{10,11... | collective-permute-start | bytes 1179656 | tf_op jit(solution)/shard_map/ppermute | solution.py:463
  52.9 2.2 %inverse_own.2.own_ref = f32[64,1536]{1,0:T(8,128)S(1)} custom-call(bf16[1152,352]{1,0:T(8,128)(2,1)S(1)} %get-tuple-element.31.t_ref, bf16[352,3072]{1,0:T(8,128)(2,1)S(1)} %get-tuple-element.23.a_ref, f32[32,3072]{1,0:T(8,128)S(1)} %get-tuple-element.24.cs_ref, bf16[64,1536]{1,0:T(8,128)(2,1)S(1)} %copy-done, bf16[2,64,64]{2,1,0:T(8,128)(2,1)S(1)} %copy-done.1, ...), custom_call_target="tpu_custom_call" | custom-call | flops 2310000128 | tf_op jit(solution)/shard_map/inverse_own/pallas_call | solution.py:425
  56.6 6.0 %forward.3 = (f32[3168,128]{1,0:T(8,128)S(1)}, bf16[768,128]{1,0:T(8,128)(2,1)S(1)}, bf16[256,128]{1,0:T(8,128)(2,1)S(1)}) custom-call(s32[4096]{0:T(1024)S(1)} %get-tuple-element.42.row_ref, s32[1]{0:T(128)} %bitcast.me_ref, bf16[352,3072]{1,0:T(8,128)(2,1)S(1)} %get-tuple-element.23.a_ref, f32[32,3072]{1,0:T(8,128)S(1)} %get-tuple-element.24.cs_ref, ...), custom_call_target="tpu_custom_call" | custom-call | flops 6600000000 | tf_op jit(solution)/shard_map/forward/pallas_call | solution.py:183
  64.2 2.0 %keep_rows.3.keep_ref = f32[1024,128]{1,0:T(8,128)S(1)} custom-call(s32[4096]{0:T(1024)S(1)} %get-tuple-element.42.row_ref, s32[1]{0:T(128)} %bitcast.me_ref, f32[3168,128]{1,0:T(8,128)S(1)} %get-tuple-element.33.q_ref), custom_call_target="tpu_custom_call" | custom-call | flops 2200000000 | tf_op jit(solution)/shard_map/keep_rows/pallas_call | solution.py:208
  66.2 4.3 %collective-permute-done.14.got_ref = bf16[768,128]{1,0:T(8,128)(2,1)S(1)} collective-permute-done((bf16[768,128]{1,0:T(8,128)(2,1)S(1)}, bf16[768,128]{1,0:T(8,128)(2,1)S(1)}, u32[]{:S(2)}, u32[]{:S(2)}) %collective-permute-start.14) | collective-permute-done | bytes 196640 | tf_op jit(solution)/shard_map/ppermute | solution.py:463
  71.5 2.6 %collective-permute-start.17 = (bf16[256,128]{1,0:T(8,128)(2,1)S(1)}, bf16[256,128]{1,0:T(8,128)(2,1)S(1)}, u32[]{:S(2)}, u32[]{:S(2)}) collective-permute-start(bf16[256,128]{1,0:T(8,128)(2,1)S(1)} %get-tuple-element.38), channel_id=1, source_target_pairs={{0,12},{1,13},{2,14},{3,15},{4,8},{5,9},{6,10},{7,11},{8,4},{9,5},... | collective-permute-start | bytes 196616 | tf_op jit(solution)/shard_map/ppermute | solution.py:463
  75.0 1.9 %collective-permute-done.17.refs_3_ = bf16[256,128]{1,0:T(8,128)(2,1)S(1)} collective-permute-done((bf16[256,128]{1,0:T(8,128)(2,1)S(1)}, bf16[256,128]{1,0:T(8,128)(2,1)S(1)}, u32[]{:S(2)}, u32[]{:S(2)}) %collective-permute-start.17) | collective-permute-done | bytes 65568 | tf_op jit(solution)/shard_map/ppermute | solution.py:463
  79.7 3.7 %collective-permute-done.18.refs_0_ = bf16[256,128]{1,0:T(8,128)(2,1)S(1)} collective-permute-done((bf16[256,128]{1,0:T(8,128)(2,1)S(1)}, bf16[256,128]{1,0:T(8,128)(2,1)S(1)}, u32[]{:S(2)}, u32[]{:S(2)}) %collective-permute-start.18) | collective-permute-done | bytes 65568 | tf_op jit(solution)/shard_map/ppermute | solution.py:463
  88.8 2.1 %place_pieces.11.z_ref = f32[6336,128]{1,0:T(8,128)S(1)} custom-call(s32[4096]{0:T(1024)S(1)} %get-tuple-element.41.place_ref, s32[1]{0:T(128)} %bitcast.me_ref, f32[6336,128]{1,0:T(8,128)S(1)} %place_pieces.10.before_ref, bf16[512,128]{1,0:T(8,128)(2,1)S(1)} %collective-permute-done.19.refs_0_, ...), custom_call_target="tpu_custom_call", output_to_operand_aliasing={{}: (2, {})} | custom-call | flops 2529999872 | tf_op jit(solution)/shard_map/place_pieces/pallas_call | solution.py:323
  90.8 1.8 %collective-permute-done.21.piece_ref = bf16[512,128]{1,0:T(8,128)(2,1)S(1)} collective-permute-done((bf16[512,128]{1,0:T(8,128)(2,1)S(1)}, bf16[512,128]{1,0:T(8,128)(2,1)S(1)}, u32[]{:S(2)}, u32[]{:S(2)}) %collective-permute-start.21) | collective-permute-done | bytes 131104 | tf_op jit(solution)/shard_map/ppermute | solution.py:463
  92.7 4.7 %inverse_other.3 = (f32[64,1536]{1,0:T(8,128)S(1)}, bf16[1152,352]{1,0:T(8,128)(2,1)S(1)}, f32[6336,128]{1,0:T(8,128)S(1)}) custom-call(s32[4096]{0:T(1024)S(1)} %get-tuple-element.41.place_ref, s32[1]{0:T(128)} %bitcast.me_ref, f32[6336,128]{1,0:T(8,128)S(1)} %place_pieces.11.z_ref, ...), custom_call_target="tpu_custom_call", output_to_operand_aliasing={{2}: (2, {})} | custom-call | flops 4950000128 | tf_op jit(solution)/shard_map/inverse_other/pallas_call | solution.py:387
  97.4 4.8 %collective-permute-start.22 = (f32[64,1536]{1,0:T(8,128)S(1)}, f32[64,1536]{1,0:T(8,128)S(1)}, u32[]{:S(2)}, u32[]{:S(2)}) collective-permute-start(f32[64,1536]{1,0:T(8,128)S(1)} %get-tuple-element.40), channel_id=1, source_target_pairs={{0,1},{1,0},{2,3},{3,2},{4,5},{5,4},{6,7},{7,6},{8,9},{9,8},{10,11... | collective-permute-start | bytes 1179656 | tf_op jit(solution)/shard_map/ppermute | solution.py:463
  102.2 2.2 %inverse_own.3.own_ref = f32[64,1536]{1,0:T(8,128)S(1)} custom-call(bf16[1152,352]{1,0:T(8,128)(2,1)S(1)} %get-tuple-element.39.t_ref, bf16[352,3072]{1,0:T(8,128)(2,1)S(1)} %get-tuple-element.23.a_ref, f32[32,3072]{1,0:T(8,128)S(1)} %get-tuple-element.24.cs_ref, bf16[64,1536]{1,0:T(8,128)(2,1)S(1)} %finish.2.own_ref.field_ref, ...), custom_call_target="tpu_custom_call" | custom-call | flops 2310000128 | tf_op jit(solution)/shard_map/inverse_own/pallas_call | solution.py:425
  (62 shorter events, 27.7 us)
Async XLA Ops:
  0.0 1.4 %collective-permute-start = (s32[3,1536]{1,0:T(4,128)}, s32[3,1536]{1,0:T(4,128)S(1)}, u32[]{:S(2)}, u32[]{:S(2)}) collective-permute-start(s32[3,1536]{1,0:T(4,128)} %own_ref.2), channel_id=1, source_target_pairs={{0,1},{1,0},{2,3},{3,2},{4,5},{5,4},{6,7},{7,6},{8,9},{9,8},{10,11... | collective-permute-start | bytes 55304 | tf_op jit(solution)/shard_map/ppermute | solution.py:463
  0.1 3.2 %collective-permute-start.1 = (bf16[64,1536]{1,0:T(8,128)(2,1)}, bf16[64,1536]{1,0:T(8,128)(2,1)S(1)}, u32[]{:S(2)}, u32[]{:S(2)}) collective-permute-start(bf16[64,1536]{1,0:T(8,128)(2,1)} %field_ref.1), channel_id=1, source_target_pairs={{0,1},{1,0},{2,3},{3,2},{4,5},{5,4},{6,7},{7,6},{8,9},{9,8},{10,11... | collective-permute-start | bytes 589832 | tf_op jit(solution)/shard_map/ppermute | solution.py:463
  2.1 24.8 %slice-start = ((s8[8388608]{0:T(1024)(128)(4,1)}), s8[4194304]{0:T(1024)(128)(4,1)S(1)}, s32[]{:S(2)}) async-start(s8[8388608]{0:T(1024)(128)(4,1)} %bitcast.3), calls=%async_computation | async-start | bytes 8388608
  9.5 12.6 %collective-permute-start.2 = (bf16[256,128]{1,0:T(8,128)(2,1)S(1)}, bf16[256,128]{1,0:T(8,128)(2,1)S(1)}, u32[]{:S(2)}, u32[]{:S(2)}) collective-permute-start(bf16[256,128]{1,0:T(8,128)(2,1)S(1)} %get-tuple-element.26), channel_id=1, source_target_pairs={{0,2},{1,3},{2,0},{3,1},{4,6},{5,7},{6,4},{7,5},{8,10},{9,11},{10,... | collective-permute-start | bytes 196616 | tf_op jit(solution)/shard_map/ppermute | solution.py:463
  11.9 5.8 %collective-permute-start.3 = (bf16[768,128]{1,0:T(8,128)(2,1)S(1)}, bf16[768,128]{1,0:T(8,128)(2,1)S(1)}, u32[]{:S(2)}, u32[]{:S(2)}) collective-permute-start(bf16[768,128]{1,0:T(8,128)(2,1)S(1)} %get-tuple-element.27), channel_id=1, source_target_pairs={{0,2},{1,3},{2,0},{3,1},{4,6},{5,7},{6,4},{7,5},{8,10},{9,11},{10,... | collective-permute-start | bytes 589832 | tf_op jit(solution)/shard_map/ppermute | solution.py:463
  17.8 4.5 %collective-permute-start.4 = (bf16[256,128]{1,0:T(8,128)(2,1)S(1)}, bf16[256,128]{1,0:T(8,128)(2,1)S(1)}, u32[]{:S(2)}, u32[]{:S(2)}) collective-permute-start(bf16[256,128]{1,0:T(8,128)(2,1)S(1)} %get-tuple-element.28), channel_id=1, source_target_pairs={{0,8},{1,9},{2,10},{3,11},{4,12},{5,13},{6,14},{7,15},{8,0},{9,1},... | collective-permute-start | bytes 196616 | tf_op jit(solution)/shard_map/ppermute | solution.py:463
  20.7 3.8 %collective-permute-start.5 = (bf16[256,128]{1,0:T(8,128)(2,1)S(1)}, bf16[256,128]{1,0:T(8,128)(2,1)S(1)}, u32[]{:S(2)}, u32[]{:S(2)}) collective-permute-start(bf16[256,128]{1,0:T(8,128)(2,1)S(1)} %get-tuple-element.29), channel_id=1, source_target_pairs={{0,4},{1,5},{2,6},{3,7},{4,0},{5,1},{6,2},{7,3},{8,12},{9,13},{10,... | collective-permute-start | bytes 196616 | tf_op jit(solution)/shard_map/ppermute | solution.py:463
  22.0 4.9 %collective-permute-start.6 = (bf16[256,128]{1,0:T(8,128)(2,1)S(1)}, bf16[256,128]{1,0:T(8,128)(2,1)S(1)}, u32[]{:S(2)}, u32[]{:S(2)}) collective-permute-start(bf16[256,128]{1,0:T(8,128)(2,1)S(1)} %get-tuple-element.30), channel_id=1, source_target_pairs={{0,12},{1,13},{2,14},{3,15},{4,8},{5,9},{6,10},{7,11},{8,4},{9,5},... | collective-permute-start | bytes 196616 | tf_op jit(solution)/shard_map/ppermute | solution.py:463
  28.6 4.1 %collective-permute-start.7 = (bf16[256,128]{1,0:T(8,128)(2,1)S(1)}, bf16[256,128]{1,0:T(8,128)(2,1)S(1)}, u32[]{:S(2)}, u32[]{:S(2)}) collective-permute-start(bf16[256,128]{1,0:T(8,128)(2,1)S(1)} %mix.2.refs_0_), channel_id=1, source_target_pairs={{0,8},{1,9},{2,10},{3,11},{4,12},{5,13},{6,14},{7,15},{8,0},{9,1},... | collective-permute-start | bytes 196616 | tf_op jit(solution)/shard_map/ppermute | solution.py:463
  32.7 5.9 %collective-permute-start.9 = (bf16[512,128]{1,0:T(8,128)(2,1)S(1)}, bf16[512,128]{1,0:T(8,128)(2,1)S(1)}, u32[]{:S(2)}, u32[]{:S(2)}) collective-permute-start(bf16[512,128]{1,0:T(8,128)(2,1)S(1)} %pad_maximum_fusion), channel_id=1, source_target_pairs={{0,2},{1,3},{2,0},{3,1},{4,6},{5,7},{6,4},{7,5},{8,10},{9,11},{10,... | collective-permute-start | bytes 393224 | tf_op jit(solution)/shard_map/ppermute | solution.py:463
  34.0 3.8 %collective-permute-start.8 = (bf16[512,128]{1,0:T(8,128)(2,1)S(1)}, bf16[512,128]{1,0:T(8,128)(2,1)S(1)}, u32[]{:S(2)}, u32[]{:S(2)}) collective-permute-start(bf16[512,128]{1,0:T(8,128)(2,1)S(1)} %pad_maximum_fusion), channel_id=1, source_target_pairs={{0,4},{1,5},{2,6},{3,7},{4,0},{5,1},{6,2},{7,3},{8,12},{9,13},{10,... | collective-permute-start | bytes 393224 | tf_op jit(solution)/shard_map/ppermute | solution.py:463
  37.8 5.0 %collective-permute-start.10 = (bf16[512,128]{1,0:T(8,128)(2,1)S(1)}, bf16[512,128]{1,0:T(8,128)(2,1)S(1)}, u32[]{:S(2)}, u32[]{:S(2)}) collective-permute-start(bf16[512,128]{1,0:T(8,128)(2,1)S(1)} %collective-permute-done.8.refs_0_), channel_id=1, source_target_pairs={{0,2},{1,3},{2,0},{3,1},{4,6},{5,7},{6,4},{7,5},{8,10},{9,11},{10,... | collective-permute-start | bytes 393224 | tf_op jit(solution)/shard_map/ppermute | solution.py:463
  47.3 7.7 %collective-permute-start.11 = (f32[64,1536]{1,0:T(8,128)S(1)}, f32[64,1536]{1,0:T(8,128)S(1)}, u32[]{:S(2)}, u32[]{:S(2)}) collective-permute-start(f32[64,1536]{1,0:T(8,128)S(1)} %get-tuple-element.32), channel_id=1, source_target_pairs={{0,1},{1,0},{2,3},{3,2},{4,5},{5,4},{6,7},{7,6},{8,9},{9,8},{10,11... | collective-permute-start | bytes 1179656 | tf_op jit(solution)/shard_map/ppermute | solution.py:463
  55.1 1.5 %collective-permute-start.12 = (bf16[64,1536]{1,0:T(8,128)(2,1)S(1)}, bf16[64,1536]{1,0:T(8,128)(2,1)S(1)}, u32[]{:S(2)}, u32[]{:S(2)}) collective-permute-start(bf16[64,1536]{1,0:T(8,128)(2,1)S(1)} %finish.2.own_ref.field_ref), channel_id=1, source_target_pairs={{0,1},{1,0},{2,3},{3,2},{4,5},{5,4},{6,7},{7,6},{8,9},{9,8},{10,11... | collective-permute-start | bytes 589832 | tf_op jit(solution)/shard_map/ppermute | solution.py:463
  62.6 11.5 %collective-permute-start.13 = (bf16[256,128]{1,0:T(8,128)(2,1)S(1)}, bf16[256,128]{1,0:T(8,128)(2,1)S(1)}, u32[]{:S(2)}, u32[]{:S(2)}) collective-permute-start(bf16[256,128]{1,0:T(8,128)(2,1)S(1)} %get-tuple-element.34), channel_id=1, source_target_pairs={{0,2},{1,3},{2,0},{3,1},{4,6},{5,7},{6,4},{7,5},{8,10},{9,11},{10,... | collective-permute-start | bytes 196616 | tf_op jit(solution)/shard_map/ppermute | solution.py:463
  63.0 7.5 %collective-permute-start.14 = (bf16[768,128]{1,0:T(8,128)(2,1)S(1)}, bf16[768,128]{1,0:T(8,128)(2,1)S(1)}, u32[]{:S(2)}, u32[]{:S(2)}) collective-permute-start(bf16[768,128]{1,0:T(8,128)(2,1)S(1)} %get-tuple-element.35), channel_id=1, source_target_pairs={{0,2},{1,3},{2,0},{3,1},{4,6},{5,7},{6,4},{7,5},{8,10},{9,11},{10,... | collective-permute-start | bytes 589832 | tf_op jit(solution)/shard_map/ppermute | solution.py:463
  70.5 4.3 %collective-permute-start.15 = (bf16[256,128]{1,0:T(8,128)(2,1)S(1)}, bf16[256,128]{1,0:T(8,128)(2,1)S(1)}, u32[]{:S(2)}, u32[]{:S(2)}) collective-permute-start(bf16[256,128]{1,0:T(8,128)(2,1)S(1)} %get-tuple-element.36), channel_id=1, source_target_pairs={{0,8},{1,9},{2,10},{3,11},{4,12},{5,13},{6,14},{7,15},{8,0},{9,1},... | collective-permute-start | bytes 196616 | tf_op jit(solution)/shard_map/ppermute | solution.py:463
  71.2 3.8 %collective-permute-start.16 = (bf16[256,128]{1,0:T(8,128)(2,1)S(1)}, bf16[256,128]{1,0:T(8,128)(2,1)S(1)}, u32[]{:S(2)}, u32[]{:S(2)}) collective-permute-start(bf16[256,128]{1,0:T(8,128)(2,1)S(1)} %get-tuple-element.37), channel_id=1, source_target_pairs={{0,4},{1,5},{2,6},{3,7},{4,0},{5,1},{6,2},{7,3},{8,12},{9,13},{10,... | collective-permute-start | bytes 196616 | tf_op jit(solution)/shard_map/ppermute | solution.py:463
  71.5 5.4 %collective-permute-start.17 = (bf16[256,128]{1,0:T(8,128)(2,1)S(1)}, bf16[256,128]{1,0:T(8,128)(2,1)S(1)}, u32[]{:S(2)}, u32[]{:S(2)}) collective-permute-start(bf16[256,128]{1,0:T(8,128)(2,1)S(1)} %get-tuple-element.38), channel_id=1, source_target_pairs={{0,12},{1,13},{2,14},{3,15},{4,8},{5,9},{6,10},{7,11},{8,4},{9,5},... | collective-permute-start | bytes 196616 | tf_op jit(solution)/shard_map/ppermute | solution.py:463
  78.6 4.8 %collective-permute-start.18 = (bf16[256,128]{1,0:T(8,128)(2,1)S(1)}, bf16[256,128]{1,0:T(8,128)(2,1)S(1)}, u32[]{:S(2)}, u32[]{:S(2)}) collective-permute-start(bf16[256,128]{1,0:T(8,128)(2,1)S(1)} %mix.3.refs_0_), channel_id=1, source_target_pairs={{0,8},{1,9},{2,10},{3,11},{4,12},{5,13},{6,14},{7,15},{8,0},{9,1},... | collective-permute-start | bytes 196616 | tf_op jit(solution)/shard_map/ppermute | solution.py:463
  83.4 5.4 %collective-permute-start.20 = (bf16[512,128]{1,0:T(8,128)(2,1)S(1)}, bf16[512,128]{1,0:T(8,128)(2,1)S(1)}, u32[]{:S(2)}, u32[]{:S(2)}) collective-permute-start(bf16[512,128]{1,0:T(8,128)(2,1)S(1)} %pad_maximum_fusion.1), channel_id=1, source_target_pairs={{0,2},{1,3},{2,0},{3,1},{4,6},{5,7},{6,4},{7,5},{8,10},{9,11},{10,... | collective-permute-start | bytes 393224 | tf_op jit(solution)/shard_map/ppermute | solution.py:463
  83.6 3.9 %collective-permute-start.19 = (bf16[512,128]{1,0:T(8,128)(2,1)S(1)}, bf16[512,128]{1,0:T(8,128)(2,1)S(1)}, u32[]{:S(2)}, u32[]{:S(2)}) collective-permute-start(bf16[512,128]{1,0:T(8,128)(2,1)S(1)} %pad_maximum_fusion.1), channel_id=1, source_target_pairs={{0,4},{1,5},{2,6},{3,7},{4,0},{5,1},{6,2},{7,3},{8,12},{9,13},{10,... | collective-permute-start | bytes 393224 | tf_op jit(solution)/shard_map/ppermute | solution.py:463
  87.5 5.2 %collective-permute-start.21 = (bf16[512,128]{1,0:T(8,128)(2,1)S(1)}, bf16[512,128]{1,0:T(8,128)(2,1)S(1)}, u32[]{:S(2)}, u32[]{:S(2)}) collective-permute-start(bf16[512,128]{1,0:T(8,128)(2,1)S(1)} %collective-permute-done.19.refs_0_), channel_id=1, source_target_pairs={{0,2},{1,3},{2,0},{3,1},{4,6},{5,7},{6,4},{7,5},{8,10},{9,11},{10,... | collective-permute-start | bytes 393224 | tf_op jit(solution)/shard_map/ppermute | solution.py:463
  97.4 6.9 %collective-permute-start.22 = (f32[64,1536]{1,0:T(8,128)S(1)}, f32[64,1536]{1,0:T(8,128)S(1)}, u32[]{:S(2)}, u32[]{:S(2)}) collective-permute-start(f32[64,1536]{1,0:T(8,128)S(1)} %get-tuple-element.40), channel_id=1, source_target_pairs={{0,1},{1,0},{2,3},{3,2},{4,5},{5,4},{6,7},{7,6},{8,9},{9,8},{10,11... | collective-permute-start | bytes 1179656 | tf_op jit(solution)/shard_map/ppermute | solution.py:463
  (5 other events, 52.0 us)

commit v4 on v3

--- a/solution.py
+++ b/solution.py
@@ -170,30 +170,30 @@
         lax.fori_loop(0, local, step, 0, unroll=32)
 
 
-def forward(rows, me, a, cs, own, other, norm, first, second, local):
+def forward(rows, me, a, cs, own, other, norm, lists, local):
     width, points = own.shape
-    shapes = [(len(owners) * local, 2 * width) for owners in (first, second)]
-
-    def kernel(row_ref, me_ref, a_ref, cs_ref, own_ref, other_ref, q_ref, first_ref, second_ref, hs_ref, b0_ref, b1_ref, stage_ref):
+    sizes = [len(owners) * local for owners in lists]
+
+    def kernel(row_ref, me_ref, a_ref, cs_ref, own_ref, other_ref, q_ref, *refs):
+        send_refs, (hs_ref, b0_ref, b1_ref, stage_ref) = refs[:-4], refs[-4:]
         spectrum(norm, a_ref, cs_ref, own_ref, other_ref, q_ref, hs_ref, (b0_ref, b1_ref))
-        gather_rows(row_ref, me_ref, q_ref, stage_ref, first + second, local)
-        first_ref[...] = stage_ref[: shapes[0][0], :].astype(BF16)
-        second_ref[...] = stage_ref[shapes[0][0] :, :].astype(BF16)
-
-    return pl.pallas_call(
-        kernel,
-        out_shape=(
-            jax.ShapeDtypeStruct((ROWS_Q, 2 * width), F32),
-            jax.ShapeDtypeStruct(shapes[0], BF16),
-            jax.ShapeDtypeStruct(shapes[1], BF16),
-        ),
+        gather_rows(row_ref, me_ref, q_ref, stage_ref, sum(lists, []), local)
+        at = 0
+        for ref in send_refs:
+            ref[...] = stage_ref[at : at + ref.shape[0], :].astype(BF16)
+            at += ref.shape[0]
+
+    return pl.pallas_call(
+        kernel,
+        out_shape=(jax.ShapeDtypeStruct((ROWS_Q, 2 * width), F32),)
+        + tuple(jax.ShapeDtypeStruct((size, 2 * width), BF16) for size in sizes),
         in_specs=[smem()] * 2 + [vmem()] * 4,
-        out_specs=(vmem(), vmem(), vmem()),
+        out_specs=(vmem(),) * (1 + len(sizes)),
         scratch_shapes=[
             pltpu.VMEM((width, 2 * points), F32),
             pltpu.VMEM((4 * width, 2 * points), BF16),
             pltpu.VMEM((4 * width, 2 * points), BF16),
-            pltpu.VMEM((shapes[0][0] + shapes[1][0], 2 * width), F32),
+            pltpu.VMEM((sum(sizes), 2 * width), F32),
         ],
         compiler_params=params(),
         cost_estimate=cost(6.0),
@@ -216,22 +216,19 @@
     )(rows, me, q)
 
 
-def merge(keep, got, count):
-    rows = got.shape[0] // count
-
-    def kernel(keep_ref, got_ref, *out_refs):
-        for n, ref in enumerate(out_refs):
-            here = slice(n * rows, (n + 1) * rows)
-            total = keep_ref[rows + n * rows : 2 * rows + n * rows, :] + got_ref[here, :].astype(F32)
-            ref[...] = total.astype(BF16)
-
-    return pl.pallas_call(
-        kernel,
-        out_shape=(jax.ShapeDtypeStruct((rows, got.shape[1]), BF16),) * count,
+def merge(keep, got, keep_at, got_at, rows):
+    def kernel(keep_ref, got_ref, out_ref):
+        total = keep_ref[keep_at : keep_at + rows, :]
+        total = total + got_ref[got_at : got_at + rows, :].astype(F32)
+        out_ref[...] = total.astype(BF16)
+
+    return pl.pallas_call(
+        kernel,
+        out_shape=jax.ShapeDtypeStruct((rows, got.shape[1]), BF16),
         in_specs=[vmem()] * 2,
-        out_specs=(vmem(),) * count,
-        compiler_params=params(),
-        cost_estimate=cost(0.3),
+        out_specs=vmem(),
+        compiler_params=params(),
+        cost_estimate=cost(0.2),
         name="merge",
     )(keep, got)
 
@@ -245,7 +242,7 @@
         got_refs, (out_ref, s_ref, acc_ref) = refs[:-3], refs[-3:]
         total = keep_ref[:modes, :]
         for ref in got_refs:
-            total = total + ref[...].astype(F32)
+            total = total + ref[:modes, :].astype(F32)
         s_ref[...] = total.T
         s_ref[width:, :] = s_ref[width:, :] * flip_ref[...]
 
@@ -471,25 +468,32 @@
     near, far = owners[: count // 4], owners[count // 4 :]
     weights = jnp.transpose(spec_weight, (0, 2, 3, 4, 1))
 
-    quad = count // 8
-    part = quad // 2 * local
+    quarter = count // 16
+    part = quarter * local
+    near = [near[n * quarter : (n + 1) * quarter] for n in range(4)]
+    far = [far[n * quarter : (n + 1) * quarter] for n in range(4)]
 
     theirs = swap(field, 1)
     a, cs = make_tables(coords, swap(coords, 1))
     for depth in range(LAYERS):
         if depth:
             theirs = swap(field, 1)
-        q, far_send, near_send = forward(
-            rows, me_array, a, cs, field, theirs, norm, far[quad // 2 :], far[: quad // 2], local
+        q, send_both, send_three, send_rest = forward(
+            rows, me_array, a, cs, field, theirs, norm,
+            [far[3], far[1], far[0] + far[2]], local,
         )
-        far_got, near_got = swap(far_send, 2), swap(near_send, 2)
-        keep = keep_rows(rows, me_array, q, near, local)
-        sends = merge(keep, far_got, 3)
-        gots = [near_got] + [swap(x, mask) for x, mask in zip(sends, (8, 4, 12))]
+        got_both, got_three, got_rest = (swap(x, 2) for x in (send_both, send_three, send_rest))
+        keep = keep_rows(rows, me_array, q, near[0] + near[1] + near[2] + near[3], local)
+        gots = [
+            swap(merge(keep, got_both, 3 * part, 0, part), 12),
+            swap(merge(keep, got_three, part, 0, part), 8),
+            swap(merge(keep, got_rest, 2 * part, part, part), 4),
+            got_rest,
+        ]
         for bit in range(4, bits):
             total = keep[:part] if bit == 4 else keep
             for got in gots:
-                total = total + got.astype(F32)
+                total = total + got[: total.shape[0]].astype(F32)
             half = total.shape[0] // 2
             keep = total[:half]
             gots = [swap(total[half:].astype(BF16), 1 << bit)]
@@ -497,16 +501,16 @@
         z = clear_table(2 * width)
         for bit in range(bits - 1, 3, -1):
             pieces = jnp.concatenate([pieces, swap(pieces, 1 << bit)], 0)
-        over = swap(pieces, 8)
-        z = place_pieces(places, me_array, z, [pieces], near[: quad // 2], local)
-        pieces = jnp.concatenate([pieces, over], 0)
-        across, far_first = swap(pieces, 4), swap(pieces, 2)
-        z = place_pieces(places, me_array, z, [over], near[quad // 2 : quad], local)
-        last = swap(across, 2)
+        over = [swap(pieces, mask) for mask in (8, 12, 4)]
+        far_first = swap(pieces, 2)
+        far_next = swap(jnp.concatenate(over[:2], 0), 2)
+        last = swap(over[2], 2)
+        z = place_pieces(places, me_array, z, [pieces], near[0], local)
         z = place_pieces(
-            places, me_array, z, [across, far_first], near[quad:] + far[:quad], local
+            places, me_array, z, [far_first] + over, far[0] + near[1] + near[3] + near[2], local
         )
-        theirs, t = inverse_other(places, me_array, z, last, a, cs, far[quad:], local)
+        z = place_pieces(places, me_array, z, [far_next], far[1] + far[3], local)
+        theirs, t = inverse_other(places, me_array, z, last, a, cs, far[2], local)
         got = swap(theirs, 1)
         own = inverse_own(t, a, cs, field, bypass_weight, bypass_bias, depth)
         field = finish(own, got)

time: 105 us -> 97.2 us (0.926)
  waiting for transfers between devices: 30.9 us -> 18.5 us
  starting transfers between devices: 28.1 us -> 32.3 us
    ppermute x23 -> x29, waiting for transfers between devices: 30.9 us -> 18.5 us  [swap(): return lax.ppermute(x, 'pts', [(i, i ^ mask) for i in range(count)])]
    ppermute x23 -> x29, starting transfers between devices: 28.1 us -> 32.3 us  [swap(): return lax.ppermute(x, 'pts', [(i, i ^ mask) for i in range(count)])]
  transfers between devices with their start and end apart: 23 -> 29, of which waited for: 16 -> 13; matrix products, arithmetic and copies ran while one was open for 1% -> 1% of each run, Pallas kernels for 18% -> 20%
where the time goes in v4:
time: 97.2 us; the launch traced here: 97 us
  Pallas kernels  44.2 us (45%)
  starting transfers between devices  32.3 us (33%)
  waiting for transfers between devices  18.5 us (19%)
    ppermute x29, starting transfers between devices, swap(): return lax.ppermute(x, 'pts', [(i, i ^ mask) for i in range(count)])  32.3 us
    ppermute x29, waiting for transfers between devices, swap(): return lax.ppermute(x, 'pts', [(i, i ^ mask) for i in range(count)])  18.5 us
    pallas_call x2, Pallas kernels, forward(): pl.pallas_call(kernel, out_shape=(jax.ShapeDtypeStruct((ROWS_Q, 2 * width...  12.1 us
    pallas_call x6, Pallas kernels, place_pieces(): pl.pallas_call(kernel, out_shape=jax.ShapeDtypeStruct(z.shape, F32), in_s...  9.21 us
    pallas_call x2, Pallas kernels, inverse_other(): pl.pallas_call(kernel, out_shape=(jax.ShapeDtypeStruct((width, points), F...  8.63 us
    pallas_call x2, Pallas kernels, inverse_own(): pl.pallas_call(kernel, out_shape=jax.ShapeDtypeStruct((width, points), F3...  4.34 us
    pallas_call x2, Pallas kernels, keep_rows(): pl.pallas_call(kernel, out_shape=jax.ShapeDtypeStruct((len(owners) * loca...  4.06 us
    pallas_call x2, Pallas kernels, mix(): pl.pallas_call(kernel, out_shape=jax.ShapeDtypeStruct((modes, double), BF...  3.31 us
  transfers between devices with their start and end apart: 29, of which 13 were waited for; matrix products, arithmetic and copies ran while one was open for 1% of the time, Pallas kernels for 20%

profile of v4, /device:TPU:1, one launch (start us, length us, event | category | flops | bytes accessed | tf_op | source)
XLA Modules:
  0.0 97.0 jit_solution(4410694735488772599)
XLA Ops:
  3.3 6.2 %forward.2 = (f32[3168,128]{1,0:T(8,128)S(1)}, bf16[256,128]{1,0:T(8,128)(2,1)S(1)}, bf16[256,128]{1,0:T(8,128)(2,1)S(1)}, bf16[512,128]{1,0:T(8,128)(2,1)S(1)}) custom-call(s32[4096]{0:T(1024)S(1)} %get-tuple-element.34.row_ref, s32[1]{0:T(128)} %bitcast.me_ref, bf16[352,3072]{1,0:T(8,128)(2,1)S(1)} %get-tuple-element.19.a_ref, ...), custom_call_target="tpu_custom_call" | custom-call | flops 6600000000 | tf_op jit(solution)/shard_map/forward/pallas_call | solution.py:186
  9.5 2.5 %collective-permute-start.2 = (bf16[256,128]{1,0:T(8,128)(2,1)S(1)}, bf16[256,128]{1,0:T(8,128)(2,1)S(1)}, u32[]{:S(2)}, u32[]{:S(2)}) collective-permute-start(bf16[256,128]{1,0:T(8,128)(2,1)S(1)} %get-tuple-element.22), channel_id=1, source_target_pairs={{0,2},{1,3},{2,0},{3,1},{4,6},{5,7},{6,4},{7,5},{8,10},{9,11},{10,... | collective-permute-start | bytes 196616 | tf_op jit(solution)/shard_map/ppermute | solution.py:460
  13.4 2.0 %keep_rows.2.keep_ref = f32[1024,128]{1,0:T(8,128)S(1)} custom-call(s32[4096]{0:T(1024)S(1)} %get-tuple-element.34.row_ref, s32[1]{0:T(128)} %bitcast.me_ref, f32[3168,128]{1,0:T(8,128)S(1)} %get-tuple-element.21.q_ref), custom_call_target="tpu_custom_call" | custom-call | flops 2200000000 | tf_op jit(solution)/shard_map/keep_rows/pallas_call | solution.py:208
  15.5 3.4 %collective-permute-start.3 = (bf16[256,128]{1,0:T(8,128)(2,1)S(1)}, bf16[256,128]{1,0:T(8,128)(2,1)S(1)}, u32[]{:S(2)}, u32[]{:S(2)}) collective-permute-start(bf16[256,128]{1,0:T(8,128)(2,1)S(1)} %merge.6), channel_id=1, source_target_pairs={{0,12},{1,13},{2,14},{3,15},{4,8},{5,9},{6,10},{7,11},{8,4},{9,5},... | collective-permute-start | bytes 196616 | tf_op jit(solution)/shard_map/ppermute | solution.py:460
  20.5 3.4 %collective-permute-done.5.refs_1_ = bf16[256,128]{1,0:T(8,128)(2,1)S(1)} collective-permute-done((bf16[256,128]{1,0:T(8,128)(2,1)S(1)}, bf16[256,128]{1,0:T(8,128)(2,1)S(1)}, u32[]{:S(2)}, u32[]{:S(2)}) %collective-permute-start.5) | collective-permute-done | bytes 65568 | tf_op jit(solution)/shard_map/ppermute | solution.py:460
  24.0 1.7 %mix.2.refs_0_ = bf16[256,128]{1,0:T(8,128)(2,1)S(1)} custom-call(f32[1,256]{1,0:T(1,128)S(1)} %bitcast.7, bf16[2,2,64,64,256]{4,3,2,1,0:T(8,128)(2,1)S(1)} %bitcast.5, f32[1024,128]{1,0:T(8,128)S(1)} %keep_rows.2.keep_ref, bf16[256,128]{1,0:T(8,128)(2,1)S(1)} %collective-permute-done.3.refs_0_, bf16[256,128]{1,0:T(8,128)(2,1)S(1)} %collective-permute-done.5.refs_1_, ...), custom_call_target="tpu_custom_call" | custom-call | flops 1980000000 | tf_op jit(solution)/shard_map/mix/pallas_call | solution.py:266
  25.9 1.9 %collective-permute-start.10 = (bf16[256,128]{1,0:T(8,128)(2,1)S(1)}, bf16[256,128]{1,0:T(8,128)(2,1)S(1)}, u32[]{:S(2)}, u32[]{:S(2)}) collective-permute-start(bf16[256,128]{1,0:T(8,128)(2,1)S(1)} %mix.2.refs_0_), channel_id=1, source_target_pairs={{0,12},{1,13},{2,14},{3,15},{4,8},{5,9},{6,10},{7,11},{8,4},{9,5},... | collective-permute-start | bytes 196616 | tf_op jit(solution)/shard_map/ppermute | solution.py:460
  30.9 1.8 %collective-permute-done.9.refs_1_ = bf16[256,128]{1,0:T(8,128)(2,1)S(1)} collective-permute-done((bf16[256,128]{1,0:T(8,128)(2,1)S(1)}, bf16[256,128]{1,0:T(8,128)(2,1)S(1)}, u32[]{:S(2)}, u32[]{:S(2)}) %collective-permute-start.9) | collective-permute-done | bytes 65568 | tf_op jit(solution)/shard_map/ppermute | solution.py:460
  32.7 3.2 %collective-permute-start.12 = (bf16[512,128]{1,0:T(8,128)(2,1)S(1)}, bf16[512,128]{1,0:T(8,128)(2,1)S(1)}, u32[]{:S(2)}, u32[]{:S(2)}) collective-permute-start(bf16[512,128]{1,0:T(8,128)(2,1)S(1)} %pad_maximum_fusion), channel_id=1, source_target_pairs={{0,2},{1,3},{2,0},{3,1},{4,6},{5,7},{6,4},{7,5},{8,10},{9,11},{10,... | collective-permute-start | bytes 393224 | tf_op jit(solution)/shard_map/ppermute | solution.py:460
  35.9 2.1 %place_pieces.7.before_ref = f32[6336,128]{1,0:T(8,128)S(1)} custom-call(s32[4096]{0:T(1024)S(1)} %get-tuple-element.33.place_ref, s32[1]{0:T(128)} %bitcast.me_ref, f32[6336,128]{1,0:T(8,128)S(1)} %place_pieces.6.before_ref, bf16[256,128]{1,0:T(8,128)(2,1)S(1)} %collective-permute-done.8.refs_0_, ...), custom_call_target="tpu_custom_call", output_to_operand_aliasing={{}: (2, {})} | custom-call | flops 2529999872 | tf_op jit(solution)/shard_map/place_pieces/pallas_call | solution.py:320
  39.7 4.2 %inverse_other.2 = (f32[64,1536]{1,0:T(8,128)S(1)}, bf16[1152,352]{1,0:T(8,128)(2,1)S(1)}, f32[6336,128]{1,0:T(8,128)S(1)}) custom-call(s32[4096]{0:T(1024)S(1)} %get-tuple-element.33.place_ref, s32[1]{0:T(128)} %bitcast.me_ref, f32[6336,128]{1,0:T(8,128)S(1)} %place_pieces.8.z_ref, ...), custom_call_target="tpu_custom_call", output_to_operand_aliasing={{2}: (2, {})} | custom-call | flops 4950000128 | tf_op jit(solution)/shard_map/inverse_other/pallas_call | solution.py:384
  43.9 3.3 %collective-permute-start.14 = (f32[64,1536]{1,0:T(8,128)S(1)}, f32[64,1536]{1,0:T(8,128)S(1)}, u32[]{:S(2)}, u32[]{:S(2)}) collective-permute-start(f32[64,1536]{1,0:T(8,128)S(1)} %get-tuple-element.26), channel_id=1, source_target_pairs={{0,1},{1,0},{2,3},{3,2},{4,5},{5,4},{6,7},{7,6},{8,9},{9,8},{10,11... | collective-permute-start | bytes 1179656 | tf_op jit(solution)/shard_map/ppermute | solution.py:460
  47.2 2.2 %inverse_own.2.own_ref = f32[64,1536]{1,0:T(8,128)S(1)} custom-call(bf16[1152,352]{1,0:T(8,128)(2,1)S(1)} %get-tuple-element.25.t_ref, bf16[352,3072]{1,0:T(8,128)(2,1)S(1)} %get-tuple-element.19.a_ref, f32[32,3072]{1,0:T(8,128)S(1)} %get-tuple-element.20.cs_ref, bf16[64,1536]{1,0:T(8,128)(2,1)S(1)} %copy-done, bf16[2,64,64]{2,1,0:T(8,128)(2,1)S(1)} %copy-done.1, ...), custom_call_target="tpu_custom_call" | custom-call | flops 2310000128 | tf_op jit(solution)/shard_map/inverse_own/pallas_call | solution.py:422
  51.0 6.0 %forward.3 = (f32[3168,128]{1,0:T(8,128)S(1)}, bf16[256,128]{1,0:T(8,128)(2,1)S(1)}, bf16[256,128]{1,0:T(8,128)(2,1)S(1)}, bf16[512,128]{1,0:T(8,128)(2,1)S(1)}) custom-call(s32[4096]{0:T(1024)S(1)} %get-tuple-element.34.row_ref, s32[1]{0:T(128)} %bitcast.me_ref, bf16[352,3072]{1,0:T(8,128)(2,1)S(1)} %get-tuple-element.19.a_ref, ...), custom_call_target="tpu_custom_call" | custom-call | flops 6600000000 | tf_op jit(solution)/shard_map/forward/pallas_call | solution.py:186
  59.6 2.0 %keep_rows.3.keep_ref = f32[1024,128]{1,0:T(8,128)S(1)} custom-call(s32[4096]{0:T(1024)S(1)} %get-tuple-element.34.row_ref, s32[1]{0:T(128)} %bitcast.me_ref, f32[3168,128]{1,0:T(8,128)S(1)} %get-tuple-element.27.q_ref), custom_call_target="tpu_custom_call" | custom-call | flops 2200000000 | tf_op jit(solution)/shard_map/keep_rows/pallas_call | solution.py:208
  61.7 1.7 %collective-permute-start.17 = (bf16[256,128]{1,0:T(8,128)(2,1)S(1)}, bf16[256,128]{1,0:T(8,128)(2,1)S(1)}, u32[]{:S(2)}, u32[]{:S(2)}) collective-permute-start(bf16[256,128]{1,0:T(8,128)(2,1)S(1)} %merge.9), channel_id=1, source_target_pairs={{0,12},{1,13},{2,14},{3,15},{4,8},{5,9},{6,10},{7,11},{8,4},{9,5},... | collective-permute-start | bytes 196616 | tf_op jit(solution)/shard_map/ppermute | solution.py:460
  66.7 3.5 %collective-permute-done.19.refs_1_ = bf16[256,128]{1,0:T(8,128)(2,1)S(1)} collective-permute-done((bf16[256,128]{1,0:T(8,128)(2,1)S(1)}, bf16[256,128]{1,0:T(8,128)(2,1)S(1)}, u32[]{:S(2)}, u32[]{:S(2)}) %collective-permute-start.19) | collective-permute-done | bytes 65568 | tf_op jit(solution)/shard_map/ppermute | solution.py:460
  70.2 1.7 %mix.3.refs_0_ = bf16[256,128]{1,0:T(8,128)(2,1)S(1)} custom-call(f32[1,256]{1,0:T(1,128)S(1)} %bitcast.8, bf16[2,2,64,64,256]{4,3,2,1,0:T(8,128)(2,1)S(1)} %bitcast.6, f32[1024,128]{1,0:T(8,128)S(1)} %keep_rows.3.keep_ref, bf16[256,128]{1,0:T(8,128)(2,1)S(1)} %collective-permute-done.17.refs_0_, bf16[256,128]{1,0:T(8,128)(2,1)S(1)} %collective-permute-done.19.refs_1_, ...), custom_call_target="tpu_custom_call" | custom-call | flops 1980000000 | tf_op jit(solution)/shard_map/mix/pallas_call | solution.py:266
  71.9 2.4 %collective-permute-start.24 = (bf16[256,128]{1,0:T(8,128)(2,1)S(1)}, bf16[256,128]{1,0:T(8,128)(2,1)S(1)}, u32[]{:S(2)}, u32[]{:S(2)}) collective-permute-start(bf16[256,128]{1,0:T(8,128)(2,1)S(1)} %mix.3.refs_0_), channel_id=1, source_target_pairs={{0,12},{1,13},{2,14},{3,15},{4,8},{5,9},{6,10},{7,11},{8,4},{9,5},... | collective-permute-start | bytes 196616 | tf_op jit(solution)/shard_map/ppermute | solution.py:460
  77.6 3.8 %collective-permute-done.23.refs_1_ = bf16[256,128]{1,0:T(8,128)(2,1)S(1)} collective-permute-done((bf16[256,128]{1,0:T(8,128)(2,1)S(1)}, bf16[256,128]{1,0:T(8,128)(2,1)S(1)}, u32[]{:S(2)}, u32[]{:S(2)}) %collective-permute-start.23) | collective-permute-done | bytes 65568 | tf_op jit(solution)/shard_map/ppermute | solution.py:460
  83.0 2.1 %place_pieces.10.before_ref = f32[6336,128]{1,0:T(8,128)S(1)} custom-call(s32[4096]{0:T(1024)S(1)} %get-tuple-element.33.place_ref, s32[1]{0:T(128)} %bitcast.me_ref, f32[6336,128]{1,0:T(8,128)S(1)} %place_pieces.9.before_ref, bf16[256,128]{1,0:T(8,128)(2,1)S(1)} %collective-permute-done.22.refs_0_, ...), custom_call_target="tpu_custom_call", output_to_operand_aliasing={{}: (2, {})} | custom-call | flops 2529999872 | tf_op jit(solution)/shard_map/place_pieces/pallas_call | solution.py:320
  86.9 4.4 %inverse_other.3 = (f32[64,1536]{1,0:T(8,128)S(1)}, bf16[1152,352]{1,0:T(8,128)(2,1)S(1)}, f32[6336,128]{1,0:T(8,128)S(1)}) custom-call(s32[4096]{0:T(1024)S(1)} %get-tuple-element.33.place_ref, s32[1]{0:T(128)} %bitcast.me_ref, f32[6336,128]{1,0:T(8,128)S(1)} %place_pieces.11.z_ref, ...), custom_call_target="tpu_custom_call", output_to_operand_aliasing={{2}: (2, {})} | custom-call | flops 4950000128 | tf_op jit(solution)/shard_map/inverse_other/pallas_call | solution.py:384
  91.3 2.7 %collective-permute-start.28 = (f32[64,1536]{1,0:T(8,128)S(1)}, f32[64,1536]{1,0:T(8,128)S(1)}, u32[]{:S(2)}, u32[]{:S(2)}) collective-permute-start(f32[64,1536]{1,0:T(8,128)S(1)} %get-tuple-element.32), channel_id=1, source_target_pairs={{0,1},{1,0},{2,3},{3,2},{4,5},{5,4},{6,7},{7,6},{8,9},{9,8},{10,11... | collective-permute-start | bytes 1179656 | tf_op jit(solution)/shard_map/ppermute | solution.py:460
  94.0 2.2 %inverse_own.3.own_ref = f32[64,1536]{1,0:T(8,128)S(1)} custom-call(bf16[1152,352]{1,0:T(8,128)(2,1)S(1)} %get-tuple-element.31.t_ref, bf16[352,3072]{1,0:T(8,128)(2,1)S(1)} %get-tuple-element.19.a_ref, f32[32,3072]{1,0:T(8,128)S(1)} %get-tuple-element.20.cs_ref, bf16[64,1536]{1,0:T(8,128)(2,1)S(1)} %finish.2.own_ref.field_ref, ...), custom_call_target="tpu_custom_call" | custom-call | flops 2310000128 | tf_op jit(solution)/shard_map/inverse_own/pallas_call | solution.py:422
  (78 shorter events, 26.5 us)
Async XLA Ops:
  9.5 6.0 %collective-permute-start.2 = (bf16[256,128]{1,0:T(8,128)(2,1)S(1)}, bf16[256,128]{1,0:T(8,128)(2,1)S(1)}, u32[]{:S(2)}, u32[]{:S(2)}) collective-permute-start(bf16[256,128]{1,0:T(8,128)(2,1)S(1)} %get-tuple-element.22), channel_id=1, source_target_pairs={{0,2},{1,3},{2,0},{3,1},{4,6},{5,7},{6,4},{7,5},{8,10},{9,11},{10,... | collective-permute-start | bytes 196616 | tf_op jit(solution)/shard_map/ppermute | solution.py:460
  11.9 6.9 %collective-permute-start.4 = (bf16[256,128]{1,0:T(8,128)(2,1)S(1)}, bf16[256,128]{1,0:T(8,128)(2,1)S(1)}, u32[]{:S(2)}, u32[]{:S(2)}) collective-permute-start(bf16[256,128]{1,0:T(8,128)(2,1)S(1)} %get-tuple-element.23), channel_id=1, source_target_pairs={{0,2},{1,3},{2,0},{3,1},{4,6},{5,7},{6,4},{7,5},{8,10},{9,11},{10,... | collective-permute-start | bytes 196616 | tf_op jit(solution)/shard_map/ppermute | solution.py:460
  12.0 7.0 %collective-permute-start.6 = (bf16[512,128]{1,0:T(8,128)(2,1)S(1)}, bf16[512,128]{1,0:T(8,128)(2,1)S(1)}, u32[]{:S(2)}, u32[]{:S(2)}) collective-permute-start(bf16[512,128]{1,0:T(8,128)(2,1)S(1)} %get-tuple-element.24), channel_id=1, source_target_pairs={{0,2},{1,3},{2,0},{3,1},{4,6},{5,7},{6,4},{7,5},{8,10},{9,11},{10,... | collective-permute-start | bytes 393224 | tf_op jit(solution)/shard_map/ppermute | solution.py:460
  15.5 5.0 %collective-permute-start.3 = (bf16[256,128]{1,0:T(8,128)(2,1)S(1)}, bf16[256,128]{1,0:T(8,128)(2,1)S(1)}, u32[]{:S(2)}, u32[]{:S(2)}) collective-permute-start(bf16[256,128]{1,0:T(8,128)(2,1)S(1)} %merge.6), channel_id=1, source_target_pairs={{0,12},{1,13},{2,14},{3,15},{4,8},{5,9},{6,10},{7,11},{8,4},{9,5},... | collective-permute-start | bytes 196616 | tf_op jit(solution)/shard_map/ppermute | solution.py:460
  18.9 5.1 %collective-permute-start.5 = (bf16[256,128]{1,0:T(8,128)(2,1)S(1)}, bf16[256,128]{1,0:T(8,128)(2,1)S(1)}, u32[]{:S(2)}, u32[]{:S(2)}) collective-permute-start(bf16[256,128]{1,0:T(8,128)(2,1)S(1)} %merge.7), channel_id=1, source_target_pairs={{0,8},{1,9},{2,10},{3,11},{4,12},{5,13},{6,14},{7,15},{8,0},{9,1},... | collective-permute-start | bytes 196616 | tf_op jit(solution)/shard_map/ppermute | solution.py:460
  19.0 5.0 %collective-permute-start.7 = (bf16[256,128]{1,0:T(8,128)(2,1)S(1)}, bf16[256,128]{1,0:T(8,128)(2,1)S(1)}, u32[]{:S(2)}, u32[]{:S(2)}) collective-permute-start(bf16[256,128]{1,0:T(8,128)(2,1)S(1)} %merge.8), channel_id=1, source_target_pairs={{0,4},{1,5},{2,6},{3,7},{4,0},{5,1},{6,2},{7,3},{8,12},{9,13},{10,... | collective-permute-start | bytes 196616 | tf_op jit(solution)/shard_map/ppermute | solution.py:460
  25.6 10.2 %collective-permute-start.11 = (bf16[256,128]{1,0:T(8,128)(2,1)S(1)}, bf16[256,128]{1,0:T(8,128)(2,1)S(1)}, u32[]{:S(2)}, u32[]{:S(2)}) collective-permute-start(bf16[256,128]{1,0:T(8,128)(2,1)S(1)} %mix.2.refs_0_), channel_id=1, source_target_pairs={{0,4},{1,5},{2,6},{3,7},{4,0},{5,1},{6,2},{7,3},{8,12},{9,13},{10,... | collective-permute-start | bytes 196616 | tf_op jit(solution)/shard_map/ppermute | solution.py:460
  25.9 5.0 %collective-permute-start.10 = (bf16[256,128]{1,0:T(8,128)(2,1)S(1)}, bf16[256,128]{1,0:T(8,128)(2,1)S(1)}, u32[]{:S(2)}, u32[]{:S(2)}) collective-permute-start(bf16[256,128]{1,0:T(8,128)(2,1)S(1)} %mix.2.refs_0_), channel_id=1, source_target_pairs={{0,12},{1,13},{2,14},{3,15},{4,8},{5,9},{6,10},{7,11},{8,4},{9,5},... | collective-permute-start | bytes 196616 | tf_op jit(solution)/shard_map/ppermute | solution.py:460
  27.8 4.8 %collective-permute-start.9 = (bf16[256,128]{1,0:T(8,128)(2,1)S(1)}, bf16[256,128]{1,0:T(8,128)(2,1)S(1)}, u32[]{:S(2)}, u32[]{:S(2)}) collective-permute-start(bf16[256,128]{1,0:T(8,128)(2,1)S(1)} %mix.2.refs_0_), channel_id=1, source_target_pairs={{0,8},{1,9},{2,10},{3,11},{4,12},{5,13},{6,14},{7,15},{8,0},{9,1},... | collective-permute-start | bytes 196616 | tf_op jit(solution)/shard_map/ppermute | solution.py:460
  28.4 7.6 %collective-permute-start.8 = (bf16[256,128]{1,0:T(8,128)(2,1)S(1)}, bf16[256,128]{1,0:T(8,128)(2,1)S(1)}, u32[]{:S(2)}, u32[]{:S(2)}) collective-permute-start(bf16[256,128]{1,0:T(8,128)(2,1)S(1)} %mix.2.refs_0_), channel_id=1, source_target_pairs={{0,2},{1,3},{2,0},{3,1},{4,6},{5,7},{6,4},{7,5},{8,10},{9,11},{10,... | collective-permute-start | bytes 196616 | tf_op jit(solution)/shard_map/ppermute | solution.py:460
  32.7 5.5 %collective-permute-start.12 = (bf16[512,128]{1,0:T(8,128)(2,1)S(1)}, bf16[512,128]{1,0:T(8,128)(2,1)S(1)}, u32[]{:S(2)}, u32[]{:S(2)}) collective-permute-start(bf16[512,128]{1,0:T(8,128)(2,1)S(1)} %pad_maximum_fusion), channel_id=1, source_target_pairs={{0,2},{1,3},{2,0},{3,1},{4,6},{5,7},{6,4},{7,5},{8,10},{9,11},{10,... | collective-permute-start | bytes 393224 | tf_op jit(solution)/shard_map/ppermute | solution.py:460
  43.9 5.5 %collective-permute-start.14 = (f32[64,1536]{1,0:T(8,128)S(1)}, f32[64,1536]{1,0:T(8,128)S(1)}, u32[]{:S(2)}, u32[]{:S(2)}) collective-permute-start(f32[64,1536]{1,0:T(8,128)S(1)} %get-tuple-element.26), channel_id=1, source_target_pairs={{0,1},{1,0},{2,3},{3,2},{4,5},{5,4},{6,7},{7,6},{8,9},{9,8},{10,11... | collective-permute-start | bytes 1179656 | tf_op jit(solution)/shard_map/ppermute | solution.py:460
  56.9 4.7 %collective-permute-start.16 = (bf16[256,128]{1,0:T(8,128)(2,1)S(1)}, bf16[256,128]{1,0:T(8,128)(2,1)S(1)}, u32[]{:S(2)}, u32[]{:S(2)}) collective-permute-start(bf16[256,128]{1,0:T(8,128)(2,1)S(1)} %get-tuple-element.28), channel_id=1, source_target_pairs={{0,2},{1,3},{2,0},{3,1},{4,6},{5,7},{6,4},{7,5},{8,10},{9,11},{10,... | collective-permute-start | bytes 196616 | tf_op jit(solution)/shard_map/ppermute | solution.py:460
  58.2 5.3 %collective-permute-start.18 = (bf16[256,128]{1,0:T(8,128)(2,1)S(1)}, bf16[256,128]{1,0:T(8,128)(2,1)S(1)}, u32[]{:S(2)}, u32[]{:S(2)}) collective-permute-start(bf16[256,128]{1,0:T(8,128)(2,1)S(1)} %get-tuple-element.29), channel_id=1, source_target_pairs={{0,2},{1,3},{2,0},{3,1},{4,6},{5,7},{6,4},{7,5},{8,10},{9,11},{10,... | collective-permute-start | bytes 196616 | tf_op jit(solution)/shard_map/ppermute | solution.py:460
  58.5 6.2 %collective-permute-start.20 = (bf16[512,128]{1,0:T(8,128)(2,1)S(1)}, bf16[512,128]{1,0:T(8,128)(2,1)S(1)}, u32[]{:S(2)}, u32[]{:S(2)}) collective-permute-start(bf16[512,128]{1,0:T(8,128)(2,1)S(1)} %get-tuple-element.30), channel_id=1, source_target_pairs={{0,2},{1,3},{2,0},{3,1},{4,6},{5,7},{6,4},{7,5},{8,10},{9,11},{10,... | collective-permute-start | bytes 393224 | tf_op jit(solution)/shard_map/ppermute | solution.py:460
  61.7 5.0 %collective-permute-start.17 = (bf16[256,128]{1,0:T(8,128)(2,1)S(1)}, bf16[256,128]{1,0:T(8,128)(2,1)S(1)}, u32[]{:S(2)}, u32[]{:S(2)}) collective-permute-start(bf16[256,128]{1,0:T(8,128)(2,1)S(1)} %merge.9), channel_id=1, source_target_pairs={{0,12},{1,13},{2,14},{3,15},{4,8},{5,9},{6,10},{7,11},{8,4},{9,5},... | collective-permute-start | bytes 196616 | tf_op jit(solution)/shard_map/ppermute | solution.py:460
  63.4 6.7 %collective-permute-start.19 = (bf16[256,128]{1,0:T(8,128)(2,1)S(1)}, bf16[256,128]{1,0:T(8,128)(2,1)S(1)}, u32[]{:S(2)}, u32[]{:S(2)}) collective-permute-start(bf16[256,128]{1,0:T(8,128)(2,1)S(1)} %merge.10), channel_id=1, source_target_pairs={{0,8},{1,9},{2,10},{3,11},{4,12},{5,13},{6,14},{7,15},{8,0},{9,1},... | collective-permute-start | bytes 196616 | tf_op jit(solution)/shard_map/ppermute | solution.py:460
  64.7 5.5 %collective-permute-start.21 = (bf16[256,128]{1,0:T(8,128)(2,1)S(1)}, bf16[256,128]{1,0:T(8,128)(2,1)S(1)}, u32[]{:S(2)}, u32[]{:S(2)}) collective-permute-start(bf16[256,128]{1,0:T(8,128)(2,1)S(1)} %merge.11), channel_id=1, source_target_pairs={{0,4},{1,5},{2,6},{3,7},{4,0},{5,1},{6,2},{7,3},{8,12},{9,13},{10,... | collective-permute-start | bytes 196616 | tf_op jit(solution)/shard_map/ppermute | solution.py:460
  71.8 9.8 %collective-permute-start.25 = (bf16[256,128]{1,0:T(8,128)(2,1)S(1)}, bf16[256,128]{1,0:T(8,128)(2,1)S(1)}, u32[]{:S(2)}, u32[]{:S(2)}) collective-permute-start(bf16[256,128]{1,0:T(8,128)(2,1)S(1)} %mix.3.refs_0_), channel_id=1, source_target_pairs={{0,4},{1,5},{2,6},{3,7},{4,0},{5,1},{6,2},{7,3},{8,12},{9,13},{10,... | collective-permute-start | bytes 196616 | tf_op jit(solution)/shard_map/ppermute | solution.py:460
  71.9 5.7 %collective-permute-start.24 = (bf16[256,128]{1,0:T(8,128)(2,1)S(1)}, bf16[256,128]{1,0:T(8,128)(2,1)S(1)}, u32[]{:S(2)}, u32[]{:S(2)}) collective-permute-start(bf16[256,128]{1,0:T(8,128)(2,1)S(1)} %mix.3.refs_0_), channel_id=1, source_target_pairs={{0,12},{1,13},{2,14},{3,15},{4,8},{5,9},{6,10},{7,11},{8,4},{9,5},... | collective-permute-start | bytes 196616 | tf_op jit(solution)/shard_map/ppermute | solution.py:460
  74.3 7.1 %collective-permute-start.23 = (bf16[256,128]{1,0:T(8,128)(2,1)S(1)}, bf16[256,128]{1,0:T(8,128)(2,1)S(1)}, u32[]{:S(2)}, u32[]{:S(2)}) collective-permute-start(bf16[256,128]{1,0:T(8,128)(2,1)S(1)} %mix.3.refs_0_), channel_id=1, source_target_pairs={{0,8},{1,9},{2,10},{3,11},{4,12},{5,13},{6,14},{7,15},{8,0},{9,1},... | collective-permute-start | bytes 196616 | tf_op jit(solution)/shard_map/ppermute | solution.py:460
  74.5 8.4 %collective-permute-start.22 = (bf16[256,128]{1,0:T(8,128)(2,1)S(1)}, bf16[256,128]{1,0:T(8,128)(2,1)S(1)}, u32[]{:S(2)}, u32[]{:S(2)}) collective-permute-start(bf16[256,128]{1,0:T(8,128)(2,1)S(1)} %mix.3.refs_0_), channel_id=1, source_target_pairs={{0,2},{1,3},{2,0},{3,1},{4,6},{5,7},{6,4},{7,5},{8,10},{9,11},{10,... | collective-permute-start | bytes 196616 | tf_op jit(solution)/shard_map/ppermute | solution.py:460
  81.6 5.3 %collective-permute-start.27 = (bf16[256,128]{1,0:T(8,128)(2,1)S(1)}, bf16[256,128]{1,0:T(8,128)(2,1)S(1)}, u32[]{:S(2)}, u32[]{:S(2)}) collective-permute-start(bf16[256,128]{1,0:T(8,128)(2,1)S(1)} %collective-permute-done.25.refs_3_), channel_id=1, source_target_pairs={{0,2},{1,3},{2,0},{3,1},{4,6},{5,7},{6,4},{7,5},{8,10},{9,11},{10,... | collective-permute-start | bytes 196616 | tf_op jit(solution)/shard_map/ppermute | solution.py:460
  91.3 4.9 %collective-permute-start.28 = (f32[64,1536]{1,0:T(8,128)S(1)}, f32[64,1536]{1,0:T(8,128)S(1)}, u32[]{:S(2)}, u32[]{:S(2)}) collective-permute-start(f32[64,1536]{1,0:T(8,128)S(1)} %get-tuple-element.32), channel_id=1, source_target_pairs={{0,1},{1,0},{2,3},{3,2},{4,5},{5,4},{6,7},{7,6},{8,9},{9,8},{10,11... | collective-permute-start | bytes 1179656 | tf_op jit(solution)/shard_map/ppermute | solution.py:460
  (11 other events, 75.4 us)

commit v5 on v4

--- a/solution.py
+++ b/solution.py
@@ -113,34 +113,34 @@
     ]
 
 
-def spectrum(norm, a_ref, cs_ref, own_ref, other_ref, q_ref, hs_ref, b_refs):
-    width, points = own_ref.shape
-    hs_ref[:, :points] = own_ref[...].astype(F32) * norm
-    hs_ref[:, points:] = other_ref[...].astype(F32) * norm
+def sums(norm, half, a_ref, cs_ref, h_ref, hs_ref, b_refs, write):
+    width, points = h_ref.shape
+    here = slice(half * points, (half + 1) * points)
+    hs_ref[...] = h_ref[...].astype(F32) * norm
 
     def product(b):
         return lax.dot_general(
-            a_ref[...], b, (((1,), (1,)), ((), ())), preferred_element_type=F32
+            a_ref[:, here], b, (((1,), (1,)), ((), ())), preferred_element_type=F32
         )
 
     first = product(hs_ref[...].astype(BF16))
-    q_ref[0:ROWS_A, :] = jnp.concatenate([first, jnp.zeros_like(first)], 1)
-
+    write(0, jnp.concatenate([first, jnp.zeros_like(first)], 1))
     for pair in range(HALF // 2):
         b_ref = b_refs[pair % 2]
-        for half in range(2):
-            k = 2 * pair + 1 + half
-            b_ref[2 * half * width : (2 * half + 1) * width, :] = (
-                hs_ref[...] * cs_ref[k : k + 1, :]
+        for part in range(2):
+            k = 2 * pair + 1 + part
+            b_ref[2 * part * width : (2 * part + 1) * width, :] = (
+                hs_ref[...] * cs_ref[k : k + 1, here]
             ).astype(BF16)
-            b_ref[(2 * half + 1) * width : (2 * half + 2) * width, :] = (
-                hs_ref[...] * cs_ref[16 + k : 17 + k, :]
+            b_ref[(2 * part + 1) * width : (2 * part + 2) * width, :] = (
+                hs_ref[...] * cs_ref[16 + k : 17 + k, here]
             ).astype(BF16)
         both = product(b_ref[...])
-        k = 2 * pair + 1
-        q_ref[k * ROWS_A : (k + 1) * ROWS_A, :] = both[:, : 2 * width]
-        q_ref[(k + 1) * ROWS_A : (k + 2) * ROWS_A, :] = both[:, 2 * width :]
-
+        write(2 * pair + 1, both[:, : 2 * width])
+        write(2 * pair + 2, both[:, 2 * width :])
+
+
+def combine_rows(q_ref, width):
     sign = sign_lanes(width)
 
     def combine(i, carry):
@@ -159,9 +159,39 @@
     lax.fori_loop(0, KZ * GROUPS, combine, 0, unroll=9)
 
 
-def gather_rows(row_ref, me_ref, q_ref, out_ref, owners, local):
+def sum_scratch(width, points):
+    return [
+        pltpu.VMEM((width, points), F32),
+        pltpu.VMEM((4 * width, points), BF16),
+        pltpu.VMEM((4 * width, points), BF16),
+    ]
+
+
+def forward_own(a, cs, own, norm):
+    width, points = own.shape
+
+    def kernel(a_ref, cs_ref, own_ref, q_ref, hs_ref, b0_ref, b1_ref):
+        def write(k, total):
+            q_ref[k * ROWS_A : (k + 1) * ROWS_A, :] = total
+
+        sums(norm, 0, a_ref, cs_ref, own_ref, hs_ref, (b0_ref, b1_ref), write)
+
+    return pl.pallas_call(
+        kernel,
+        out_shape=jax.ShapeDtypeStruct((ROWS_Q, 2 * width), F32),
+        in_specs=[vmem()] * 3,
+        out_specs=vmem(),
+        scratch_shapes=sum_scratch(width, points),
+        compiler_params=params(),
+        cost_estimate=cost(2.0),
+        name="forward_own",
+    )(a, cs, own)
+
+
+def gather_rows(row_ref, q_ref, out_ref, owners, local):
+    me = lax.axis_index("pts")
     for at, owner in enumerate(owners):
-        base = jnp.bitwise_xor(me_ref[0], owner) * local
+        base = jnp.bitwise_xor(me, owner) * local
 
         def step(j, carry, base=base, at=at):
             out_ref[pl.ds(at * local + j, 1), :] = q_ref[pl.ds(row_ref[base + j], 1), :]
@@ -170,14 +200,23 @@
         lax.fori_loop(0, local, step, 0, unroll=32)
 
 
-def forward(rows, me, a, cs, own, other, norm, lists, local):
-    width, points = own.shape
+def forward(rows, a, cs, q, other, norm, lists, local):
+    width, points = other.shape
     sizes = [len(owners) * local for owners in lists]
 
-    def kernel(row_ref, me_ref, a_ref, cs_ref, own_ref, other_ref, q_ref, *refs):
-        send_refs, (hs_ref, b0_ref, b1_ref, stage_ref) = refs[:-4], refs[-4:]
-        spectrum(norm, a_ref, cs_ref, own_ref, other_ref, q_ref, hs_ref, (b0_ref, b1_ref))
-        gather_rows(row_ref, me_ref, q_ref, stage_ref, sum(lists, []), local)
+    def kernel(list_ref, a_ref, cs_ref, before_ref, other_ref, q_ref, *refs):
+        send_refs, (hs_ref, b0_ref, b1_ref, stage_ref, row_ref, sem) = refs[:-6], refs[-6:]
+        copy = pltpu.make_async_copy(list_ref, row_ref, sem)
+        copy.start()
+
+        def write(k, total):
+            here = slice(k * ROWS_A, (k + 1) * ROWS_A)
+            q_ref[here, :] = before_ref[here, :] + total
+
+        sums(norm, 1, a_ref, cs_ref, other_ref, hs_ref, (b0_ref, b1_ref), write)
+        combine_rows(q_ref, width)
+        copy.wait()
+        gather_rows(row_ref, q_ref, stage_ref, sum(lists, []), local)
         at = 0
         for ref in send_refs:
             ref[...] = stage_ref[at : at + ref.shape[0], :].astype(BF16)
@@ -187,33 +226,55 @@
         kernel,
         out_shape=(jax.ShapeDtypeStruct((ROWS_Q, 2 * width), F32),)
         + tuple(jax.ShapeDtypeStruct((size, 2 * width), BF16) for size in sizes),
-        in_specs=[smem()] * 2 + [vmem()] * 4,
+        in_specs=[pl.BlockSpec(memory_space=pl.ANY)] + [vmem()] * 4,
         out_specs=(vmem(),) * (1 + len(sizes)),
-        scratch_shapes=[
-            pltpu.VMEM((width, 2 * points), F32),
-            pltpu.VMEM((4 * width, 2 * points), BF16),
-            pltpu.VMEM((4 * width, 2 * points), BF16),
+        scratch_shapes=sum_scratch(width, points) + [
             pltpu.VMEM((sum(sizes), 2 * width), F32),
+            pltpu.SMEM(rows.shape, rows.dtype),
+            pltpu.SemaphoreType.DMA,
         ],
         compiler_params=params(),
-        cost_estimate=cost(6.0),
+        cost_estimate=cost(4.0),
         name="forward",
-    )(rows, me, a, cs, own, other)
-
-
-def keep_rows(rows, me, q, owners, local):
-    def kernel(row_ref, me_ref, q_ref, out_ref):
-        gather_rows(row_ref, me_ref, q_ref, out_ref, owners, local)
+    )(rows, a, cs, q, other)
+
+
+def more_rows(rows, q, lists, local):
+    sizes = [len(owners) * local for owners in lists]
+
+    def kernel(row_ref, q_ref, *refs):
+        out_refs, stage_ref = refs[:-1], refs[-1]
+        gather_rows(row_ref, q_ref, stage_ref, sum(lists, []), local)
+        at = 0
+        for ref in out_refs:
+            ref[...] = stage_ref[at : at + ref.shape[0], :].astype(BF16)
+            at += ref.shape[0]
+
+    return pl.pallas_call(
+        kernel,
+        out_shape=tuple(jax.ShapeDtypeStruct((size, q.shape[1]), BF16) for size in sizes),
+        in_specs=[smem()] + [vmem()],
+        out_specs=(vmem(),) * len(sizes),
+        scratch_shapes=[pltpu.VMEM((sum(sizes), q.shape[1]), F32)],
+        compiler_params=params(),
+        cost_estimate=cost(1.5),
+        name="more_rows",
+    )(rows, q)
+
+
+def keep_rows(rows, q, owners, local):
+    def kernel(row_ref, q_ref, out_ref):
+        gather_rows(row_ref, q_ref, out_ref, owners, local)
 
     return pl.pallas_call(
         kernel,
         out_shape=jax.ShapeDtypeStruct((len(owners) * local, q.shape[1]), F32),
-        in_specs=[smem()] * 2 + [vmem()],
+        in_specs=[smem()] + [vmem()],
         out_specs=vmem(),
         compiler_params=params(),
         cost_estimate=cost(2.0),
         name="keep_rows",
-    )(rows, me, q)
+    )(rows, q)
 
 
 def merge(keep, got, keep_at, got_at, rows):
@@ -275,9 +336,10 @@
     )(flip, weights, keep, *gots)
 
 
-def place_rows(place_ref, me_ref, m_ref, z_ref, owners, local):
+def place_rows(place_ref, m_ref, z_ref, owners, local):
+    me = lax.axis_index("pts")
     for at, owner in enumerate(owners):
-        base = jnp.bitwise_xor(me_ref[0], owner) * local
+        base = jnp.bitwise_xor(me, owner) * local
 
         def step(j, carry, base=base, at=at):
             z_ref[pl.ds(place_ref[base + j], 1), :] = m_ref[pl.ds(at * local + j, 1), :]
@@ -304,30 +366,30 @@
     )()
 
 
-def place_pieces(places, me, z, pieces, owners, local):
+def place_pieces(places, z, pieces, owners, local):
     double = pieces[0].shape[1]
     count = len(owners) * local
     n = len(pieces)
 
-    def kernel(place_ref, me_ref, before_ref, *refs):
+    def kernel(place_ref, before_ref, *refs):
         z_ref, m_ref = refs[n:]
         at = 0
         for ref in refs[:n]:
             m_ref[at : at + ref.shape[0], :] = ref[...].astype(F32)
             at += ref.shape[0]
-        place_rows(place_ref, me_ref, m_ref, z_ref, owners, local)
+        place_rows(place_ref, m_ref, z_ref, owners, local)
 
     return pl.pallas_call(
         kernel,
         out_shape=jax.ShapeDtypeStruct(z.shape, F32),
-        in_specs=[smem()] * 2 + [vmem()] * (n + 1),
-        out_specs=vmem(),
-        input_output_aliases={2: 0},
+        in_specs=[smem()] + [vmem()] * (n + 1),
+        out_specs=vmem(),
+        input_output_aliases={1: 0},
         scratch_shapes=[pltpu.VMEM((count, double), F32)],
         compiler_params=params(),
         cost_estimate=cost(0.5 + 0.45 * count / 256),
         name="place_pieces",
-    )(places, me, z, *pieces)
+    )(places, z, *pieces)
 
 
 def evaluate(t_ref, a_ref, cs_ref, start, points, width, write):
@@ -345,14 +407,17 @@
         write(slice(at, at + chunk), total)
 
 
-def inverse_other(places, me, z, piece, a, cs, owners, local):
+def inverse_other(places, z, piece, a, cs, owners, local):
     double = piece.shape[1]
     width = double // 2
     points = a.shape[1] // 2
 
-    def kernel(place_ref, me_ref, z_ref, piece_ref, a_ref, cs_ref, other_ref, t_ref, zz_ref, m_ref):
+    def kernel(list_ref, z_ref, piece_ref, a_ref, cs_ref, other_ref, t_ref, zz_ref, m_ref, place_ref, sem):
+        copy = pltpu.make_async_copy(list_ref, place_ref, sem)
+        copy.start()
         m_ref[...] = piece_ref[...].astype(F32)
-        place_rows(place_ref, me_ref, m_ref, zz_ref, owners, local)
+        copy.wait()
+        place_rows(place_ref, m_ref, zz_ref, owners, local)
         sign = sign_lanes(width)
 
         def combine(i, carry):
@@ -388,14 +453,18 @@
             jax.ShapeDtypeStruct((KZ * double, ROWS_A), BF16),
             jax.ShapeDtypeStruct(z.shape, F32),
         ),
-        in_specs=[smem()] * 2 + [vmem()] * 4,
+        in_specs=[pl.BlockSpec(memory_space=pl.ANY)] + [vmem()] * 4,
         out_specs=(vmem(), vmem(), vmem()),
-        input_output_aliases={2: 2},
-        scratch_shapes=[pltpu.VMEM(piece.shape, F32)],
+        input_output_aliases={1: 2},
+        scratch_shapes=[
+            pltpu.VMEM(piece.shape, F32),
+            pltpu.SMEM(places.shape, places.dtype),
+            pltpu.SemaphoreType.DMA,
+        ],
         compiler_params=params(),
         cost_estimate=cost(4.5),
         name="inverse_other",
-    )(places, me, z, piece, a, cs)[:2]
+    )(places, z, piece, a, cs)[:2]
 
 
 def inverse_own(t, a, cs, field, weight, bias, layer):
@@ -463,7 +532,6 @@
     places = rows + jnp.where(flip, ROWS_Q, 0)
     signs = jnp.where(flip, -1.0, 1.0).astype(F32)
     my_signs = lax.dynamic_slice(signs, (me * local,), (local,)).reshape(1, local)
-    me_array = jnp.full((1,), me, jnp.int32)
     owners = owners_of(count)
     near, far = owners[: count // 4], owners[count // 4 :]
     weights = jnp.transpose(spec_weight, (0, 2, 3, 4, 1))
@@ -478,12 +546,11 @@
     for depth in range(LAYERS):
         if depth:
             theirs = swap(field, 1)
-        q, send_both, send_three, send_rest = forward(
-            rows, me_array, a, cs, field, theirs, norm,
-            [far[3], far[1], far[0] + far[2]], local,
-        )
+        q = forward_own(a, cs, field, norm)
+        q, send_both = forward(rows, a, cs, q, theirs, norm, [far[3]], local)
+        send_three, send_rest = more_rows(rows, q, [far[1], far[0] + far[2]], local)
         got_both, got_three, got_rest = (swap(x, 2) for x in (send_both, send_three, send_rest))
-        keep = keep_rows(rows, me_array, q, near[0] + near[1] + near[2] + near[3], local)
+        keep = keep_rows(rows, q, near[0] + near[1] + near[2] + near[3], local)
         gots = [
             swap(merge(keep, got_both, 3 * part, 0, part), 12),
             swap(merge(keep, got_three, part, 0, part), 8),
@@ -505,12 +572,12 @@
         far_first = swap(pieces, 2)
         far_next = swap(jnp.concatenate(over[:2], 0), 2)
         last = swap(over[2], 2)
-        z = place_pieces(places, me_array, z, [pieces], near[0], local)
+        z = place_pieces(places, z, [pieces], near[0], local)
         z = place_pieces(
-            places, me_array, z, [far_first] + over, far[0] + near[1] + near[3] + near[2], local
+            places, z, [far_first] + over, far[0] + near[1] + near[3] + near[2], local
         )
-        z = place_pieces(places, me_array, z, [far_next], far[1] + far[3], local)
-        theirs, t = inverse_other(places, me_array, z, last, a, cs, far[2], local)
+        z = place_pieces(places, z, [far_next], far[1] + far[3], local)
+        theirs, t = inverse_other(places, z, last, a, cs, far[2], local)
         got = swap(theirs, 1)
         own = inverse_own(t, a, cs, field, bypass_weight, bypass_bias, depth)
         field = finish(own, got)

time: 97.2 us -> 93.9 us (0.966)
  waiting for transfers between devices: 18.5 us -> 15.5 us
    pallas_call x0 -> x4, Pallas kernels: none -> 6.57 us  [the longest x2 3.49 us: more_rows(): pl.pallas_call(kernel, out_shape=tuple((jax.ShapeDtypeStruct((size, q.sha...]
    pallas_call x2, Pallas kernels: 12.1 us -> 5.92 us  [forward(): pl.pallas_call(kernel, out_shape=(jax.ShapeDtypeStruct((ROWS_Q, 2 * width...]
    ppermute x29, waiting for transfers between devices: 18.5 us -> 15.5 us  [swap(): return lax.ppermute(x, 'pts', [(i, i ^ mask) for i in range(count)])]
  transfers between devices with their start and end apart: 29 -> 29, of which waited for: 13 -> 12; matrix products, arithmetic and copies ran while one was open for 1% -> 1% of each run, Pallas kernels for 20% -> 28%
where the time goes in v5:
time: 93.9 us; the launch traced here: 93.7 us
  Pallas kernels  44.6 us (47%)
  starting transfers between devices  31.6 us (34%)
  waiting for transfers between devices  15.5 us (17%)
    ppermute x29, starting transfers between devices, swap(): return lax.ppermute(x, 'pts', [(i, i ^ mask) for i in range(count)])  31.6 us
    ppermute x29, waiting for transfers between devices, swap(): return lax.ppermute(x, 'pts', [(i, i ^ mask) for i in range(count)])  15.5 us
    pallas_call x6, Pallas kernels, place_pieces(): pl.pallas_call(kernel, out_shape=jax.ShapeDtypeStruct(z.shape, F32), in_s...  9.21 us
    pallas_call x2, Pallas kernels, inverse_other(): pl.pallas_call(kernel, out_shape=(jax.ShapeDtypeStruct((width, points), F...  8.64 us
    pallas_call x2, Pallas kernels, forward(): pl.pallas_call(kernel, out_shape=(jax.ShapeDtypeStruct((ROWS_Q, 2 * width...  5.92 us
    pallas_call x2, Pallas kernels, inverse_own(): pl.pallas_call(kernel, out_shape=jax.ShapeDtypeStruct((width, points), F3...  4.31 us
    pallas_call x2, Pallas kernels, keep_rows(): pl.pallas_call(kernel, out_shape=jax.ShapeDtypeStruct((len(owners) * loca...  4.07 us
    pallas_call x2, Pallas kernels, more_rows(): pl.pallas_call(kernel, out_shape=tuple((jax.ShapeDtypeStruct((size, q.sha...  3.49 us
  transfers between devices with their start and end apart: 29, of which 12 were waited for; matrix products, arithmetic and copies ran while one was open for 1% of the time, Pallas kernels for 28%

profile of v5, /device:TPU:1, one launch (start us, length us, event | category | flops | bytes accessed | tf_op | source)
XLA Modules:
  0.0 93.7 jit_solution(14674208865550912883)
XLA Ops:
  3.3 1.5 %forward_own.2.before_ref = f32[3168,128]{1,0:T(8,128)S(1)} custom-call(bf16[352,3072]{1,0:T(8,128)(2,1)S(1)} %get-tuple-element.19.a_ref, f32[32,3072]{1,0:T(8,128)S(1)} %get-tuple-element.20.cs_ref, bf16[64,1536]{1,0:T(8,128)(2,1)S(1)} %copy-done), custom_call_target="tpu_custom_call" | custom-call | flops 2200000000 | tf_op jit(solution)/shard_map/forward_own/pallas_call | solution.py:179
  4.8 3.1 %forward.2 = (f32[3168,128]{1,0:T(8,128)S(1)}, bf16[256,128]{1,0:T(8,128)(2,1)S(1)}) custom-call(s32[4096]{0:T(1024)S(1)} %get-tuple-element.34.list_ref.row_ref, bf16[352,3072]{1,0:T(8,128)(2,1)S(1)} %get-tuple-element.19.a_ref, f32[32,3072]{1,0:T(8,128)S(1)} %get-tuple-element.20.cs_ref, f32[3168,128]{1,0:T(8,128)S(1)} %forward_own.2.before_ref, ...), custom_call_target="tpu_custom_call" | custom-call | flops 4400000000 | tf_op jit(solution)/shard_map/forward/pallas_call | solution.py:225
  7.9 2.5 %collective-permute-start.2 = (bf16[256,128]{1,0:T(8,128)(2,1)S(1)}, bf16[256,128]{1,0:T(8,128)(2,1)S(1)}, u32[]{:S(2)}, u32[]{:S(2)}) collective-permute-start(bf16[256,128]{1,0:T(8,128)(2,1)S(1)} %get-tuple-element.22), channel_id=1, source_target_pairs={{0,2},{1,3},{2,0},{3,1},{4,6},{5,7},{6,4},{7,5},{8,10},{9,11},{10,... | collective-permute-start | bytes 196616 | tf_op jit(solution)/shard_map/ppermute | solution.py:529
  10.4 1.7 %more_rows.2 = (bf16[256,128]{1,0:T(8,128)(2,1)S(1)}, bf16[512,128]{1,0:T(8,128)(2,1)S(1)}) custom-call(s32[4096]{0:T(1024)S(1)} %get-tuple-element.34.list_ref.row_ref, f32[3168,128]{1,0:T(8,128)S(1)} %get-tuple-element.21.q_ref), custom_call_target="tpu_custom_call" | custom-call | flops 1650000000 | tf_op jit(solution)/shard_map/more_rows/pallas_call | solution.py:253
  13.7 2.0 %keep_rows.2.keep_ref = f32[1024,128]{1,0:T(8,128)S(1)} custom-call(s32[4096]{0:T(1024)S(1)} %get-tuple-element.34.list_ref.row_ref, f32[3168,128]{1,0:T(8,128)S(1)} %get-tuple-element.21.q_ref), custom_call_target="tpu_custom_call" | custom-call | flops 2200000000 | tf_op jit(solution)/shard_map/keep_rows/pallas_call | solution.py:269
  15.7 2.4 %collective-permute-start.5 = (bf16[256,128]{1,0:T(8,128)(2,1)S(1)}, bf16[256,128]{1,0:T(8,128)(2,1)S(1)}, u32[]{:S(2)}, u32[]{:S(2)}) collective-permute-start(bf16[256,128]{1,0:T(8,128)(2,1)S(1)} %merge.7), channel_id=1, source_target_pairs={{0,8},{1,9},{2,10},{3,11},{4,12},{5,13},{6,14},{7,15},{8,0},{9,1},... | collective-permute-start | bytes 196616 | tf_op jit(solution)/shard_map/ppermute | solution.py:529
  19.9 3.8 %collective-permute-done.3.refs_0_ = bf16[256,128]{1,0:T(8,128)(2,1)S(1)} collective-permute-done((bf16[256,128]{1,0:T(8,128)(2,1)S(1)}, bf16[256,128]{1,0:T(8,128)(2,1)S(1)}, u32[]{:S(2)}, u32[]{:S(2)}) %collective-permute-start.3) | collective-permute-done | bytes 65568 | tf_op jit(solution)/shard_map/ppermute | solution.py:529
  23.7 1.7 %mix.2.refs_0_ = bf16[256,128]{1,0:T(8,128)(2,1)S(1)} custom-call(f32[1,256]{1,0:T(1,128)S(1)} %bitcast.6, bf16[2,2,64,64,256]{4,3,2,1,0:T(8,128)(2,1)S(1)} %bitcast.4, f32[1024,128]{1,0:T(8,128)S(1)} %keep_rows.2.keep_ref, bf16[256,128]{1,0:T(8,128)(2,1)S(1)} %collective-permute-done.3.refs_0_, bf16[256,128]{1,0:T(8,128)(2,1)S(1)} %collective-permute-done.5.refs_1_, ...), custom_call_target="tpu_custom_call" | custom-call | flops 1980000000 | tf_op jit(solution)/shard_map/mix/pallas_call | solution.py:327
  29.6 1.8 %collective-permute-done.10.refs_2_ = bf16[256,128]{1,0:T(8,128)(2,1)S(1)} collective-permute-done((bf16[256,128]{1,0:T(8,128)(2,1)S(1)}, bf16[256,128]{1,0:T(8,128)(2,1)S(1)}, u32[]{:S(2)}, u32[]{:S(2)}) %collective-permute-start.10) | collective-permute-done | bytes 65568 | tf_op jit(solution)/shard_map/ppermute | solution.py:529
  34.4 2.1 %place_pieces.7.before_ref = f32[6336,128]{1,0:T(8,128)S(1)} custom-call(s32[4096]{0:T(1024)S(1)} %get-tuple-element.33.place_ref.list_ref, f32[6336,128]{1,0:T(8,128)S(1)} %place_pieces.6.before_ref, bf16[256,128]{1,0:T(8,128)(2,1)S(1)} %collective-permute-done.8.refs_0_, ...), custom_call_target="tpu_custom_call", output_to_operand_aliasing={{}: (1, {})} | custom-call | flops 2529999872 | tf_op jit(solution)/shard_map/place_pieces/pallas_call | solution.py:382
  38.6 4.2 %inverse_other.2 = (f32[64,1536]{1,0:T(8,128)S(1)}, bf16[1152,352]{1,0:T(8,128)(2,1)S(1)}, f32[6336,128]{1,0:T(8,128)S(1)}) custom-call(s32[4096]{0:T(1024)S(1)} %get-tuple-element.33.place_ref.list_ref, f32[6336,128]{1,0:T(8,128)S(1)} %place_pieces.8.z_ref, bf16[256,128]{1,0:T(8,128)(2,1)S(1)} %collective-permute-done.13.piece_ref, ...), custom_call_target="tpu_custom_call", output_to_operand_aliasing={{2}: (1, {})} | custom-call | flops 4950000128 | tf_op jit(solution)/shard_map/inverse_other/pallas_call | solution.py:449
  42.9 5.0 %collective-permute-start.14 = (f32[64,1536]{1,0:T(8,128)S(1)}, f32[64,1536]{1,0:T(8,128)S(1)}, u32[]{:S(2)}, u32[]{:S(2)}) collective-permute-start(f32[64,1536]{1,0:T(8,128)S(1)} %get-tuple-element.26), channel_id=1, source_target_pairs={{0,1},{1,0},{2,3},{3,2},{4,5},{5,4},{6,7},{7,6},{8,9},{9,8},{10,11... | collective-permute-start | bytes 1179656 | tf_op jit(solution)/shard_map/ppermute | solution.py:529
  47.9 2.2 %inverse_own.2.own_ref = f32[64,1536]{1,0:T(8,128)S(1)} custom-call(bf16[1152,352]{1,0:T(8,128)(2,1)S(1)} %get-tuple-element.25.t_ref, bf16[352,3072]{1,0:T(8,128)(2,1)S(1)} %get-tuple-element.19.a_ref, f32[32,3072]{1,0:T(8,128)S(1)} %get-tuple-element.20.cs_ref, bf16[64,1536]{1,0:T(8,128)(2,1)S(1)} %copy-done, bf16[2,64,64]{2,1,0:T(8,128)(2,1)S(1)} %copy-done.1, ...), custom_call_target="tpu_custom_call" | custom-call | flops 2310000128 | tf_op jit(solution)/shard_map/inverse_own/pallas_call | solution.py:491
  50.3 1.5 %forward_own.3.before_ref = f32[3168,128]{1,0:T(8,128)S(1)} custom-call(bf16[352,3072]{1,0:T(8,128)(2,1)S(1)} %get-tuple-element.19.a_ref, f32[32,3072]{1,0:T(8,128)S(1)} %get-tuple-element.20.cs_ref, bf16[64,1536]{1,0:T(8,128)(2,1)S(1)} %finish.2.own_ref.field_ref), custom_call_target="tpu_custom_call" | custom-call | flops 2200000000 | tf_op jit(solution)/shard_map/forward_own/pallas_call | solution.py:179
  51.8 2.9 %forward.3 = (f32[3168,128]{1,0:T(8,128)S(1)}, bf16[256,128]{1,0:T(8,128)(2,1)S(1)}) custom-call(s32[4096]{0:T(1024)S(1)} %get-tuple-element.34.list_ref.row_ref, bf16[352,3072]{1,0:T(8,128)(2,1)S(1)} %get-tuple-element.19.a_ref, f32[32,3072]{1,0:T(8,128)S(1)} %get-tuple-element.20.cs_ref, f32[3168,128]{1,0:T(8,128)S(1)} %forward_own.3.before_ref, ...), custom_call_target="tpu_custom_call" | custom-call | flops 4400000000 | tf_op jit(solution)/shard_map/forward/pallas_call | solution.py:225
  55.0 1.7 %more_rows.3 = (bf16[256,128]{1,0:T(8,128)(2,1)S(1)}, bf16[512,128]{1,0:T(8,128)(2,1)S(1)}) custom-call(s32[4096]{0:T(1024)S(1)} %get-tuple-element.34.list_ref.row_ref, f32[3168,128]{1,0:T(8,128)S(1)} %get-tuple-element.27.q_ref), custom_call_target="tpu_custom_call" | custom-call | flops 1650000000 | tf_op jit(solution)/shard_map/more_rows/pallas_call | solution.py:253
  58.3 2.0 %keep_rows.3.keep_ref = f32[1024,128]{1,0:T(8,128)S(1)} custom-call(s32[4096]{0:T(1024)S(1)} %get-tuple-element.34.list_ref.row_ref, f32[3168,128]{1,0:T(8,128)S(1)} %get-tuple-element.27.q_ref), custom_call_target="tpu_custom_call" | custom-call | flops 2200000000 | tf_op jit(solution)/shard_map/keep_rows/pallas_call | solution.py:269
  60.5 1.8 %collective-permute-start.17 = (bf16[256,128]{1,0:T(8,128)(2,1)S(1)}, bf16[256,128]{1,0:T(8,128)(2,1)S(1)}, u32[]{:S(2)}, u32[]{:S(2)}) collective-permute-start(bf16[256,128]{1,0:T(8,128)(2,1)S(1)} %merge.9), channel_id=1, source_target_pairs={{0,12},{1,13},{2,14},{3,15},{4,8},{5,9},{6,10},{7,11},{8,4},{9,5},... | collective-permute-start | bytes 196616 | tf_op jit(solution)/shard_map/ppermute | solution.py:529
  67.0 1.7 %mix.3.refs_0_ = bf16[256,128]{1,0:T(8,128)(2,1)S(1)} custom-call(f32[1,256]{1,0:T(1,128)S(1)} %bitcast.7, bf16[2,2,64,64,256]{4,3,2,1,0:T(8,128)(2,1)S(1)} %bitcast.5, f32[1024,128]{1,0:T(8,128)S(1)} %keep_rows.3.keep_ref, bf16[256,128]{1,0:T(8,128)(2,1)S(1)} %collective-permute-done.17.refs_0_, bf16[256,128]{1,0:T(8,128)(2,1)S(1)} %collective-permute-done.19.refs_1_, ...), custom_call_target="tpu_custom_call" | custom-call | flops 1980000000 | tf_op jit(solution)/shard_map/mix/pallas_call | solution.py:327
  68.8 1.7 %collective-permute-start.24 = (bf16[256,128]{1,0:T(8,128)(2,1)S(1)}, bf16[256,128]{1,0:T(8,128)(2,1)S(1)}, u32[]{:S(2)}, u32[]{:S(2)}) collective-permute-start(bf16[256,128]{1,0:T(8,128)(2,1)S(1)} %mix.3.refs_0_), channel_id=1, source_target_pairs={{0,12},{1,13},{2,14},{3,15},{4,8},{5,9},{6,10},{7,11},{8,4},{9,5},... | collective-permute-start | bytes 196616 | tf_op jit(solution)/shard_map/ppermute | solution.py:529
  76.8 2.1 %place_pieces.10.before_ref = f32[6336,128]{1,0:T(8,128)S(1)} custom-call(s32[4096]{0:T(1024)S(1)} %get-tuple-element.33.place_ref.list_ref, f32[6336,128]{1,0:T(8,128)S(1)} %place_pieces.9.before_ref, bf16[256,128]{1,0:T(8,128)(2,1)S(1)} %collective-permute-done.22.refs_0_, ...), custom_call_target="tpu_custom_call", output_to_operand_aliasing={{}: (1, {})} | custom-call | flops 2529999872 | tf_op jit(solution)/shard_map/place_pieces/pallas_call | solution.py:382
  81.2 4.4 %inverse_other.3 = (f32[64,1536]{1,0:T(8,128)S(1)}, bf16[1152,352]{1,0:T(8,128)(2,1)S(1)}, f32[6336,128]{1,0:T(8,128)S(1)}) custom-call(s32[4096]{0:T(1024)S(1)} %get-tuple-element.33.place_ref.list_ref, f32[6336,128]{1,0:T(8,128)S(1)} %place_pieces.11.z_ref, ...), custom_call_target="tpu_custom_call", output_to_operand_aliasing={{2}: (1, {})} | custom-call | flops 4950000128 | tf_op jit(solution)/shard_map/inverse_other/pallas_call | solution.py:449
  85.7 5.1 %collective-permute-start.28 = (f32[64,1536]{1,0:T(8,128)S(1)}, f32[64,1536]{1,0:T(8,128)S(1)}, u32[]{:S(2)}, u32[]{:S(2)}) collective-permute-start(f32[64,1536]{1,0:T(8,128)S(1)} %get-tuple-element.32), channel_id=1, source_target_pairs={{0,1},{1,0},{2,3},{3,2},{4,5},{5,4},{6,7},{7,6},{8,9},{9,8},{10,11... | collective-permute-start | bytes 1179656 | tf_op jit(solution)/shard_map/ppermute | solution.py:529
  90.8 2.1 %inverse_own.3.own_ref = f32[64,1536]{1,0:T(8,128)S(1)} custom-call(bf16[1152,352]{1,0:T(8,128)(2,1)S(1)} %get-tuple-element.31.t_ref, bf16[352,3072]{1,0:T(8,128)(2,1)S(1)} %get-tuple-element.19.a_ref, f32[32,3072]{1,0:T(8,128)S(1)} %get-tuple-element.20.cs_ref, bf16[64,1536]{1,0:T(8,128)(2,1)S(1)} %finish.2.own_ref.field_ref, ...), custom_call_target="tpu_custom_call" | custom-call | flops 2310000128 | tf_op jit(solution)/shard_map/inverse_own/pallas_call | solution.py:491
  (82 shorter events, 32.3 us)
Async XLA Ops:
  0.1 4.8 %collective-permute-start.1 = (bf16[64,1536]{1,0:T(8,128)(2,1)}, bf16[64,1536]{1,0:T(8,128)(2,1)S(1)}, u32[]{:S(2)}, u32[]{:S(2)}) collective-permute-start(bf16[64,1536]{1,0:T(8,128)(2,1)} %field_ref.1), channel_id=1, source_target_pairs={{0,1},{1,0},{2,3},{3,2},{4,5},{5,4},{6,7},{7,6},{8,9},{9,8},{10,11... | collective-permute-start | bytes 589832 | tf_op jit(solution)/shard_map/ppermute | solution.py:529
  7.9 10.2 %collective-permute-start.2 = (bf16[256,128]{1,0:T(8,128)(2,1)S(1)}, bf16[256,128]{1,0:T(8,128)(2,1)S(1)}, u32[]{:S(2)}, u32[]{:S(2)}) collective-permute-start(bf16[256,128]{1,0:T(8,128)(2,1)S(1)} %get-tuple-element.22), channel_id=1, source_target_pairs={{0,2},{1,3},{2,0},{3,1},{4,6},{5,7},{6,4},{7,5},{8,10},{9,11},{10,... | collective-permute-start | bytes 196616 | tf_op jit(solution)/shard_map/ppermute | solution.py:529
  12.2 7.1 %collective-permute-start.6 = (bf16[512,128]{1,0:T(8,128)(2,1)S(1)}, bf16[512,128]{1,0:T(8,128)(2,1)S(1)}, u32[]{:S(2)}, u32[]{:S(2)}) collective-permute-start(bf16[512,128]{1,0:T(8,128)(2,1)S(1)} %get-tuple-element.24), channel_id=1, source_target_pairs={{0,2},{1,3},{2,0},{3,1},{4,6},{5,7},{6,4},{7,5},{8,10},{9,11},{10,... | collective-permute-start | bytes 393224 | tf_op jit(solution)/shard_map/ppermute | solution.py:529
  15.7 4.1 %collective-permute-start.5 = (bf16[256,128]{1,0:T(8,128)(2,1)S(1)}, bf16[256,128]{1,0:T(8,128)(2,1)S(1)}, u32[]{:S(2)}, u32[]{:S(2)}) collective-permute-start(bf16[256,128]{1,0:T(8,128)(2,1)S(1)} %merge.7), channel_id=1, source_target_pairs={{0,8},{1,9},{2,10},{3,11},{4,12},{5,13},{6,14},{7,15},{8,0},{9,1},... | collective-permute-start | bytes 196616 | tf_op jit(solution)/shard_map/ppermute | solution.py:529
  18.1 5.5 %collective-permute-start.3 = (bf16[256,128]{1,0:T(8,128)(2,1)S(1)}, bf16[256,128]{1,0:T(8,128)(2,1)S(1)}, u32[]{:S(2)}, u32[]{:S(2)}) collective-permute-start(bf16[256,128]{1,0:T(8,128)(2,1)S(1)} %merge.6), channel_id=1, source_target_pairs={{0,12},{1,13},{2,14},{3,15},{4,8},{5,9},{6,10},{7,11},{8,4},{9,5},... | collective-permute-start | bytes 196616 | tf_op jit(solution)/shard_map/ppermute | solution.py:529
  19.3 4.4 %collective-permute-start.7 = (bf16[256,128]{1,0:T(8,128)(2,1)S(1)}, bf16[256,128]{1,0:T(8,128)(2,1)S(1)}, u32[]{:S(2)}, u32[]{:S(2)}) collective-permute-start(bf16[256,128]{1,0:T(8,128)(2,1)S(1)} %merge.8), channel_id=1, source_target_pairs={{0,4},{1,5},{2,6},{3,7},{4,0},{5,1},{6,2},{7,3},{8,12},{9,13},{10,... | collective-permute-start | bytes 196616 | tf_op jit(solution)/shard_map/ppermute | solution.py:529
  25.4 7.6 %collective-permute-start.11 = (bf16[256,128]{1,0:T(8,128)(2,1)S(1)}, bf16[256,128]{1,0:T(8,128)(2,1)S(1)}, u32[]{:S(2)}, u32[]{:S(2)}) collective-permute-start(bf16[256,128]{1,0:T(8,128)(2,1)S(1)} %mix.2.refs_0_), channel_id=1, source_target_pairs={{0,4},{1,5},{2,6},{3,7},{4,0},{5,1},{6,2},{7,3},{8,12},{9,13},{10,... | collective-permute-start | bytes 196616 | tf_op jit(solution)/shard_map/ppermute | solution.py:529
  26.4 4.9 %collective-permute-start.10 = (bf16[256,128]{1,0:T(8,128)(2,1)S(1)}, bf16[256,128]{1,0:T(8,128)(2,1)S(1)}, u32[]{:S(2)}, u32[]{:S(2)}) collective-permute-start(bf16[256,128]{1,0:T(8,128)(2,1)S(1)} %mix.2.refs_0_), channel_id=1, source_target_pairs={{0,12},{1,13},{2,14},{3,15},{4,8},{5,9},{6,10},{7,11},{8,4},{9,5},... | collective-permute-start | bytes 196616 | tf_op jit(solution)/shard_map/ppermute | solution.py:529
  28.0 4.9 %collective-permute-start.9 = (bf16[256,128]{1,0:T(8,128)(2,1)S(1)}, bf16[256,128]{1,0:T(8,128)(2,1)S(1)}, u32[]{:S(2)}, u32[]{:S(2)}) collective-permute-start(bf16[256,128]{1,0:T(8,128)(2,1)S(1)} %mix.2.refs_0_), channel_id=1, source_target_pairs={{0,8},{1,9},{2,10},{3,11},{4,12},{5,13},{6,14},{7,15},{8,0},{9,1},... | collective-permute-start | bytes 196616 | tf_op jit(solution)/shard_map/ppermute | solution.py:529
  28.1 6.3 %collective-permute-start.8 = (bf16[256,128]{1,0:T(8,128)(2,1)S(1)}, bf16[256,128]{1,0:T(8,128)(2,1)S(1)}, u32[]{:S(2)}, u32[]{:S(2)}) collective-permute-start(bf16[256,128]{1,0:T(8,128)(2,1)S(1)} %mix.2.refs_0_), channel_id=1, source_target_pairs={{0,2},{1,3},{2,0},{3,1},{4,6},{5,7},{6,4},{7,5},{8,10},{9,11},{10,... | collective-permute-start | bytes 196616 | tf_op jit(solution)/shard_map/ppermute | solution.py:529
  32.9 4.3 %collective-permute-start.12 = (bf16[512,128]{1,0:T(8,128)(2,1)S(1)}, bf16[512,128]{1,0:T(8,128)(2,1)S(1)}, u32[]{:S(2)}, u32[]{:S(2)}) collective-permute-start(bf16[512,128]{1,0:T(8,128)(2,1)S(1)} %pad_maximum_fusion), channel_id=1, source_target_pairs={{0,2},{1,3},{2,0},{3,1},{4,6},{5,7},{6,4},{7,5},{8,10},{9,11},{10,... | collective-permute-start | bytes 393224 | tf_op jit(solution)/shard_map/ppermute | solution.py:529
  33.0 5.6 %collective-permute-start.13 = (bf16[256,128]{1,0:T(8,128)(2,1)S(1)}, bf16[256,128]{1,0:T(8,128)(2,1)S(1)}, u32[]{:S(2)}, u32[]{:S(2)}) collective-permute-start(bf16[256,128]{1,0:T(8,128)(2,1)S(1)} %collective-permute-done.11.refs_3_), channel_id=1, source_target_pairs={{0,2},{1,3},{2,0},{3,1},{4,6},{5,7},{6,4},{7,5},{8,10},{9,11},{10,... | collective-permute-start | bytes 196616 | tf_op jit(solution)/shard_map/ppermute | solution.py:529
  42.9 7.2 %collective-permute-start.14 = (f32[64,1536]{1,0:T(8,128)S(1)}, f32[64,1536]{1,0:T(8,128)S(1)}, u32[]{:S(2)}, u32[]{:S(2)}) collective-permute-start(f32[64,1536]{1,0:T(8,128)S(1)} %get-tuple-element.26), channel_id=1, source_target_pairs={{0,1},{1,0},{2,3},{3,2},{4,5},{5,4},{6,7},{7,6},{8,9},{9,8},{10,11... | collective-permute-start | bytes 1179656 | tf_op jit(solution)/shard_map/ppermute | solution.py:529
  54.7 5.7 %collective-permute-start.16 = (bf16[256,128]{1,0:T(8,128)(2,1)S(1)}, bf16[256,128]{1,0:T(8,128)(2,1)S(1)}, u32[]{:S(2)}, u32[]{:S(2)}) collective-permute-start(bf16[256,128]{1,0:T(8,128)(2,1)S(1)} %get-tuple-element.28), channel_id=1, source_target_pairs={{0,2},{1,3},{2,0},{3,1},{4,6},{5,7},{6,4},{7,5},{8,10},{9,11},{10,... | collective-permute-start | bytes 196616 | tf_op jit(solution)/shard_map/ppermute | solution.py:529
  58.0 5.3 %collective-permute-start.20 = (bf16[512,128]{1,0:T(8,128)(2,1)S(1)}, bf16[512,128]{1,0:T(8,128)(2,1)S(1)}, u32[]{:S(2)}, u32[]{:S(2)}) collective-permute-start(bf16[512,128]{1,0:T(8,128)(2,1)S(1)} %get-tuple-element.30), channel_id=1, source_target_pairs={{0,2},{1,3},{2,0},{3,1},{4,6},{5,7},{6,4},{7,5},{8,10},{9,11},{10,... | collective-permute-start | bytes 393224 | tf_op jit(solution)/shard_map/ppermute | solution.py:529
  60.3 4.2 %collective-permute-start.19 = (bf16[256,128]{1,0:T(8,128)(2,1)S(1)}, bf16[256,128]{1,0:T(8,128)(2,1)S(1)}, u32[]{:S(2)}, u32[]{:S(2)}) collective-permute-start(bf16[256,128]{1,0:T(8,128)(2,1)S(1)} %merge.10), channel_id=1, source_target_pairs={{0,8},{1,9},{2,10},{3,11},{4,12},{5,13},{6,14},{7,15},{8,0},{9,1},... | collective-permute-start | bytes 196616 | tf_op jit(solution)/shard_map/ppermute | solution.py:529
  60.5 5.1 %collective-permute-start.17 = (bf16[256,128]{1,0:T(8,128)(2,1)S(1)}, bf16[256,128]{1,0:T(8,128)(2,1)S(1)}, u32[]{:S(2)}, u32[]{:S(2)}) collective-permute-start(bf16[256,128]{1,0:T(8,128)(2,1)S(1)} %merge.9), channel_id=1, source_target_pairs={{0,12},{1,13},{2,14},{3,15},{4,8},{5,9},{6,10},{7,11},{8,4},{9,5},... | collective-permute-start | bytes 196616 | tf_op jit(solution)/shard_map/ppermute | solution.py:529
  68.7 8.0 %collective-permute-start.25 = (bf16[256,128]{1,0:T(8,128)(2,1)S(1)}, bf16[256,128]{1,0:T(8,128)(2,1)S(1)}, u32[]{:S(2)}, u32[]{:S(2)}) collective-permute-start(bf16[256,128]{1,0:T(8,128)(2,1)S(1)} %mix.3.refs_0_), channel_id=1, source_target_pairs={{0,4},{1,5},{2,6},{3,7},{4,0},{5,1},{6,2},{7,3},{8,12},{9,13},{10,... | collective-permute-start | bytes 196616 | tf_op jit(solution)/shard_map/ppermute | solution.py:529
  68.8 4.9 %collective-permute-start.24 = (bf16[256,128]{1,0:T(8,128)(2,1)S(1)}, bf16[256,128]{1,0:T(8,128)(2,1)S(1)}, u32[]{:S(2)}, u32[]{:S(2)}) collective-permute-start(bf16[256,128]{1,0:T(8,128)(2,1)S(1)} %mix.3.refs_0_), channel_id=1, source_target_pairs={{0,12},{1,13},{2,14},{3,15},{4,8},{5,9},{6,10},{7,11},{8,4},{9,5},... | collective-permute-start | bytes 196616 | tf_op jit(solution)/shard_map/ppermute | solution.py:529
  70.6 4.7 %collective-permute-start.23 = (bf16[256,128]{1,0:T(8,128)(2,1)S(1)}, bf16[256,128]{1,0:T(8,128)(2,1)S(1)}, u32[]{:S(2)}, u32[]{:S(2)}) collective-permute-start(bf16[256,128]{1,0:T(8,128)(2,1)S(1)} %mix.3.refs_0_), channel_id=1, source_target_pairs={{0,8},{1,9},{2,10},{3,11},{4,12},{5,13},{6,14},{7,15},{8,0},{9,1},... | collective-permute-start | bytes 196616 | tf_op jit(solution)/shard_map/ppermute | solution.py:529
  71.4 5.4 %collective-permute-start.22 = (bf16[256,128]{1,0:T(8,128)(2,1)S(1)}, bf16[256,128]{1,0:T(8,128)(2,1)S(1)}, u32[]{:S(2)}, u32[]{:S(2)}) collective-permute-start(bf16[256,128]{1,0:T(8,128)(2,1)S(1)} %mix.3.refs_0_), channel_id=1, source_target_pairs={{0,2},{1,3},{2,0},{3,1},{4,6},{5,7},{6,4},{7,5},{8,10},{9,11},{10,... | collective-permute-start | bytes 196616 | tf_op jit(solution)/shard_map/ppermute | solution.py:529
  75.3 4.5 %collective-permute-start.26 = (bf16[512,128]{1,0:T(8,128)(2,1)S(1)}, bf16[512,128]{1,0:T(8,128)(2,1)S(1)}, u32[]{:S(2)}, u32[]{:S(2)}) collective-permute-start(bf16[512,128]{1,0:T(8,128)(2,1)S(1)} %pad_maximum_fusion.1), channel_id=1, source_target_pairs={{0,2},{1,3},{2,0},{3,1},{4,6},{5,7},{6,4},{7,5},{8,10},{9,11},{10,... | collective-permute-start | bytes 393224 | tf_op jit(solution)/shard_map/ppermute | solution.py:529
  76.7 4.5 %collective-permute-start.27 = (bf16[256,128]{1,0:T(8,128)(2,1)S(1)}, bf16[256,128]{1,0:T(8,128)(2,1)S(1)}, u32[]{:S(2)}, u32[]{:S(2)}) collective-permute-start(bf16[256,128]{1,0:T(8,128)(2,1)S(1)} %collective-permute-done.25.refs_3_), channel_id=1, source_target_pairs={{0,2},{1,3},{2,0},{3,1},{4,6},{5,7},{6,4},{7,5},{8,10},{9,11},{10,... | collective-permute-start | bytes 196616 | tf_op jit(solution)/shard_map/ppermute | solution.py:529
  85.7 7.3 %collective-permute-start.28 = (f32[64,1536]{1,0:T(8,128)S(1)}, f32[64,1536]{1,0:T(8,128)S(1)}, u32[]{:S(2)}, u32[]{:S(2)}) collective-permute-start(f32[64,1536]{1,0:T(8,128)S(1)} %get-tuple-element.32), channel_id=1, source_target_pairs={{0,1},{1,0},{2,3},{3,2},{4,5},{5,4},{6,7},{7,6},{8,9},{9,8},{10,11... | collective-permute-start | bytes 1179656 | tf_op jit(solution)/shard_map/ppermute | solution.py:529
  (11 other events, 61.3 us)

commit v6 on v5

--- a/solution.py
+++ b/solution.py
@@ -401,21 +401,26 @@
         )
         total = r[:width]
         for k in range(1, KZ):
-            lo = 2 * k * width
+            lo = (2 * k - 1) * width
             total = total + r[lo : lo + width] * cs_ref[k : k + 1, here]
             total = total + r[lo + width : lo + 2 * width] * cs_ref[16 + k : 17 + k, here]
         write(slice(at, at + chunk), total)
 
 
-def inverse_other(places, z, piece, a, cs, owners, local):
-    double = piece.shape[1]
+def inverse_other(places, z, pieces, a, cs, owners, local):
+    double = pieces[0].shape[1]
+    n = len(pieces)
     width = double // 2
     points = a.shape[1] // 2
 
-    def kernel(list_ref, z_ref, piece_ref, a_ref, cs_ref, other_ref, t_ref, zz_ref, m_ref, place_ref, sem):
+    def kernel(list_ref, z_ref, a_ref, cs_ref, *refs):
+        other_ref, t_ref, zz_ref, m_ref, place_ref, sem = refs[n:]
         copy = pltpu.make_async_copy(list_ref, place_ref, sem)
         copy.start()
-        m_ref[...] = piece_ref[...].astype(F32)
+        at = 0
+        for ref in refs[:n]:
+            m_ref[at : at + ref.shape[0], :] = ref[...].astype(F32)
+            at += ref.shape[0]
         copy.wait()
         place_rows(place_ref, m_ref, zz_ref, owners, local)
         sign = sign_lanes(width)
@@ -437,9 +442,11 @@
 
         lax.fori_loop(0, KZ * GROUPS, combine, 0, unroll=9)
         for k in range(KZ):
-            t_ref[k * double : (k + 1) * double, :] = zz_ref[
-                k * ROWS_A : (k + 1) * ROWS_A, :
-            ].T.astype(BF16)
+            block = zz_ref[k * ROWS_A : (k + 1) * ROWS_A, :].T.astype(BF16)
+            if k == 0:
+                t_ref[:width, :] = block[:width]
+            else:
+                t_ref[k * double - width : (k + 1) * double - width, :] = block
 
         def write(here, total):
             other_ref[:, here] = total
@@ -450,21 +457,21 @@
         kernel,
         out_shape=(
             jax.ShapeDtypeStruct((width, points), F32),
-            jax.ShapeDtypeStruct((KZ * double, ROWS_A), BF16),
+            jax.ShapeDtypeStruct((KZ * double - width, ROWS_A), BF16),
             jax.ShapeDtypeStruct(z.shape, F32),
         ),
-        in_specs=[pl.BlockSpec(memory_space=pl.ANY)] + [vmem()] * 4,
+        in_specs=[pl.BlockSpec(memory_space=pl.ANY)] + [vmem()] * (3 + n),
         out_specs=(vmem(), vmem(), vmem()),
         input_output_aliases={1: 2},
         scratch_shapes=[
-            pltpu.VMEM(piece.shape, F32),
+            pltpu.VMEM((len(owners) * local, double), F32),
             pltpu.SMEM(places.shape, places.dtype),
             pltpu.SemaphoreType.DMA,
         ],
         compiler_params=params(),
         cost_estimate=cost(4.5),
         name="inverse_other",
-    )(places, z, piece, a, cs)[:2]
+    )(places, z, a, cs, *pieces)[:2]
 
 
 def inverse_own(t, a, cs, field, weight, bias, layer):
@@ -547,8 +554,8 @@
         if depth:
             theirs = swap(field, 1)
         q = forward_own(a, cs, field, norm)
-        q, send_both = forward(rows, a, cs, q, theirs, norm, [far[3]], local)
-        send_three, send_rest = more_rows(rows, q, [far[1], far[0] + far[2]], local)
+        q, send_both, send_three = forward(rows, a, cs, q, theirs, norm, [far[3], far[1]], local)
+        (send_rest,) = more_rows(rows, q, [far[0] + far[2]], local)
         got_both, got_three, got_rest = (swap(x, 2) for x in (send_both, send_three, send_rest))
         keep = keep_rows(rows, q, near[0] + near[1] + near[2] + near[3], local)
         gots = [
@@ -568,16 +575,17 @@
         z = clear_table(2 * width)
         for bit in range(bits - 1, 3, -1):
             pieces = jnp.concatenate([pieces, swap(pieces, 1 << bit)], 0)
-        over = [swap(pieces, mask) for mask in (8, 12, 4)]
+        over = [swap(pieces, mask) for mask in (4, 12, 8)]
         far_first = swap(pieces, 2)
         far_next = swap(jnp.concatenate(over[:2], 0), 2)
         last = swap(over[2], 2)
         z = place_pieces(places, z, [pieces], near[0], local)
         z = place_pieces(
-            places, z, [far_first] + over, far[0] + near[1] + near[3] + near[2], local
+            places, z, [far_first] + over, far[0] + near[2] + near[3] + near[1], local
         )
-        z = place_pieces(places, z, [far_next], far[1] + far[3], local)
-        theirs, t = inverse_other(places, z, last, a, cs, far[2], local)
+        theirs, t = inverse_other(
+            places, z, [far_next, last], a, cs, far[2] + far[3] + far[1], local
+        )
         got = swap(theirs, 1)
         own = inverse_own(t, a, cs, field, bypass_weight, bypass_bias, depth)
         field = finish(own, got)

time: 93.9 us -> 92 us (0.980)
  starting transfers between devices: 31.6 us -> 33.8 us
  Pallas kernels: 44.6 us -> 42.5 us
  waiting for transfers between devices: 15.5 us -> 13.4 us
    pallas_call x6 -> x4, Pallas kernels: 9.21 us -> 6.35 us  [place_pieces(): pl.pallas_call(kernel, out_shape=jax.ShapeDtypeStruct(z.shape, F32), in_s...]
    ppermute x29, starting transfers between devices: 31.6 us -> 33.8 us  [swap(): return lax.ppermute(x, 'pts', [(i, i ^ mask) for i in range(count)])]
    ppermute x29, waiting for transfers between devices: 15.5 us -> 13.4 us  [swap(): return lax.ppermute(x, 'pts', [(i, i ^ mask) for i in range(count)])]
    pallas_call x2, Pallas kernels: 8.64 us -> 9.66 us  [inverse_other(): pl.pallas_call(kernel, out_shape=(jax.ShapeDtypeStruct((width, points), F...]
  transfers between devices with their start and end apart: 29 -> 29, of which waited for: 12 -> 9; matrix products, arithmetic and copies ran while one was open for 1% -> 1% of each run, Pallas kernels for 28% -> 24%
where the time goes in v6:
time: 92 us; the launch traced here: 91.7 us
  Pallas kernels  42.5 us (46%)
  starting transfers between devices  33.8 us (37%)
  waiting for transfers between devices  13.4 us (15%)
    ppermute x29, starting transfers between devices, swap(): return lax.ppermute(x, 'pts', [(i, i ^ mask) for i in range(count)])  33.8 us
    ppermute x29, waiting for transfers between devices, swap(): return lax.ppermute(x, 'pts', [(i, i ^ mask) for i in range(count)])  13.4 us
    pallas_call x2, Pallas kernels, inverse_other(): pl.pallas_call(kernel, out_shape=(jax.ShapeDtypeStruct((width, points), F...  9.66 us
    pallas_call x2, Pallas kernels, forward(): pl.pallas_call(kernel, out_shape=(jax.ShapeDtypeStruct((ROWS_Q, 2 * width...  6.55 us
    pallas_call x4, Pallas kernels, place_pieces(): pl.pallas_call(kernel, out_shape=jax.ShapeDtypeStruct(z.shape, F32), in_s...  6.35 us
    pallas_call x2, Pallas kernels, inverse_own(): pl.pallas_call(kernel, out_shape=jax.ShapeDtypeStruct((width, points), F3...  4.1 us
    pallas_call x2, Pallas kernels, keep_rows(): pl.pallas_call(kernel, out_shape=jax.ShapeDtypeStruct((len(owners) * loca...  4.07 us
    pallas_call x2, Pallas kernels, mix(): pl.pallas_call(kernel, out_shape=jax.ShapeDtypeStruct((modes, double), BF...  3.3 us
  transfers between devices with their start and end apart: 29, of which 9 were waited for; matrix products, arithmetic and copies ran while one was open for 1% of the time, Pallas kernels for 24%

profile of v6, /device:TPU:1, one launch (start us, length us, event | category | flops | bytes accessed | tf_op | source)
XLA Modules:
  0.0 91.7 jit_solution(10426840651010362678)
XLA Ops:
  3.3 1.5 %forward_own.2.before_ref = f32[3168,128]{1,0:T(8,128)S(1)} custom-call(bf16[352,3072]{1,0:T(8,128)(2,1)S(1)} %get-tuple-element.17.a_ref, f32[32,3072]{1,0:T(8,128)S(1)} %get-tuple-element.18.cs_ref, bf16[64,1536]{1,0:T(8,128)(2,1)S(1)} %copy-done), custom_call_target="tpu_custom_call" | custom-call | flops 2200000000 | tf_op jit(solution)/shard_map/forward_own/pallas_call | solution.py:179
  4.8 3.4 %forward.2 = (f32[3168,128]{1,0:T(8,128)S(1)}, bf16[256,128]{1,0:T(8,128)(2,1)S(1)}, bf16[256,128]{1,0:T(8,128)(2,1)S(1)}) custom-call(s32[4096]{0:T(1024)S(1)} %get-tuple-element.30.list_ref.row_ref, bf16[352,3072]{1,0:T(8,128)(2,1)S(1)} %get-tuple-element.17.a_ref, f32[32,3072]{1,0:T(8,128)S(1)} %get-tuple-element.18.cs_ref, ...), custom_call_target="tpu_custom_call" | custom-call | flops 4400000000 | tf_op jit(solution)/shard_map/forward/pallas_call | solution.py:225
  8.2 2.5 %collective-permute-start.2 = (bf16[256,128]{1,0:T(8,128)(2,1)S(1)}, bf16[256,128]{1,0:T(8,128)(2,1)S(1)}, u32[]{:S(2)}, u32[]{:S(2)}) collective-permute-start(bf16[256,128]{1,0:T(8,128)(2,1)S(1)} %get-tuple-element.20), channel_id=1, source_target_pairs={{0,2},{1,3},{2,0},{3,1},{4,6},{5,7},{6,4},{7,5},{8,10},{9,11},{10,... | collective-permute-start | bytes 196616 | tf_op jit(solution)/shard_map/ppermute | solution.py:536
  13.7 2.0 %keep_rows.2.keep_ref = f32[1024,128]{1,0:T(8,128)S(1)} custom-call(s32[4096]{0:T(1024)S(1)} %get-tuple-element.30.list_ref.row_ref, f32[3168,128]{1,0:T(8,128)S(1)} %get-tuple-element.19.q_ref), custom_call_target="tpu_custom_call" | custom-call | flops 2200000000 | tf_op jit(solution)/shard_map/keep_rows/pallas_call | solution.py:269
  15.7 3.4 %collective-permute-start.3 = (bf16[256,128]{1,0:T(8,128)(2,1)S(1)}, bf16[256,128]{1,0:T(8,128)(2,1)S(1)}, u32[]{:S(2)}, u32[]{:S(2)}) collective-permute-start(bf16[256,128]{1,0:T(8,128)(2,1)S(1)} %merge.6), channel_id=1, source_target_pairs={{0,12},{1,13},{2,14},{3,15},{4,8},{5,9},{6,10},{7,11},{8,4},{9,5},... | collective-permute-start | bytes 196616 | tf_op jit(solution)/shard_map/ppermute | solution.py:536
  20.8 3.5 %collective-permute-done.5.refs_1_ = bf16[256,128]{1,0:T(8,128)(2,1)S(1)} collective-permute-done((bf16[256,128]{1,0:T(8,128)(2,1)S(1)}, bf16[256,128]{1,0:T(8,128)(2,1)S(1)}, u32[]{:S(2)}, u32[]{:S(2)}) %collective-permute-start.5) | collective-permute-done | bytes 65568 | tf_op jit(solution)/shard_map/ppermute | solution.py:536
  24.3 1.7 %mix.2.refs_0_ = bf16[256,128]{1,0:T(8,128)(2,1)S(1)} custom-call(f32[1,256]{1,0:T(1,128)S(1)} %bitcast.6, bf16[2,2,64,64,256]{4,3,2,1,0:T(8,128)(2,1)S(1)} %bitcast.4, f32[1024,128]{1,0:T(8,128)S(1)} %keep_rows.2.keep_ref, bf16[256,128]{1,0:T(8,128)(2,1)S(1)} %collective-permute-done.3.refs_0_, bf16[256,128]{1,0:T(8,128)(2,1)S(1)} %collective-permute-done.5.refs_1_, ...), custom_call_target="tpu_custom_call" | custom-call | flops 1980000000 | tf_op jit(solution)/shard_map/mix/pallas_call | solution.py:327
  30.0 2.1 %collective-permute-done.10.refs_2_ = bf16[256,128]{1,0:T(8,128)(2,1)S(1)} collective-permute-done((bf16[256,128]{1,0:T(8,128)(2,1)S(1)}, bf16[256,128]{1,0:T(8,128)(2,1)S(1)}, u32[]{:S(2)}, u32[]{:S(2)}) %collective-permute-start.10) | collective-permute-done | bytes 65568 | tf_op jit(solution)/shard_map/ppermute | solution.py:536
  33.6 2.1 %place_pieces.5.z_ref = f32[6336,128]{1,0:T(8,128)S(1)} custom-call(s32[4096]{0:T(1024)S(1)} %get-tuple-element.29.place_ref.list_ref, f32[6336,128]{1,0:T(8,128)S(1)} %place_pieces.4.before_ref, bf16[256,128]{1,0:T(8,128)(2,1)S(1)} %collective-permute-done.8.refs_0_, ...), custom_call_target="tpu_custom_call", output_to_operand_aliasing={{}: (1, {})} | custom-call | flops 2529999872 | tf_op jit(solution)/shard_map/place_pieces/pallas_call | solution.py:382
  36.9 4.7 %inverse_other.2 = (f32[64,1536]{1,0:T(8,128)S(1)}, bf16[1088,352]{1,0:T(8,128)(2,1)S(1)}, f32[6336,128]{1,0:T(8,128)S(1)}) custom-call(s32[4096]{0:T(1024)S(1)} %get-tuple-element.29.place_ref.list_ref, f32[6336,128]{1,0:T(8,128)S(1)} %place_pieces.5.z_ref, bf16[352,3072]{1,0:T(8,128)(2,1)S(1)} %get-tuple-element.17.a_ref, ...), custom_call_target="tpu_custom_call", output_to_operand_aliasing={{2}: (1, {})} | custom-call | flops 4950000128 | tf_op jit(solution)/shard_map/inverse_other/pallas_call | solution.py:456
  41.6 4.8 %collective-permute-start.14 = (f32[64,1536]{1,0:T(8,128)S(1)}, f32[64,1536]{1,0:T(8,128)S(1)}, u32[]{:S(2)}, u32[]{:S(2)}) collective-permute-start(f32[64,1536]{1,0:T(8,128)S(1)} %get-tuple-element.23), channel_id=1, source_target_pairs={{0,1},{1,0},{2,3},{3,2},{4,5},{5,4},{6,7},{7,6},{8,9},{9,8},{10,11... | collective-permute-start | bytes 1179656 | tf_op jit(solution)/shard_map/ppermute | solution.py:536
  46.4 2.1 %inverse_own.2.own_ref = f32[64,1536]{1,0:T(8,128)S(1)} custom-call(bf16[1088,352]{1,0:T(8,128)(2,1)S(1)} %get-tuple-element.22.t_ref, bf16[352,3072]{1,0:T(8,128)(2,1)S(1)} %get-tuple-element.17.a_ref, f32[32,3072]{1,0:T(8,128)S(1)} %get-tuple-element.18.cs_ref, bf16[64,1536]{1,0:T(8,128)(2,1)S(1)} %copy-done, bf16[2,64,64]{2,1,0:T(8,128)(2,1)S(1)} %copy-done.1, ...), custom_call_target="tpu_custom_call" | custom-call | flops 2310000128 | tf_op jit(solution)/shard_map/inverse_own/pallas_call | solution.py:498
  48.7 1.5 %forward_own.3.before_ref = f32[3168,128]{1,0:T(8,128)S(1)} custom-call(bf16[352,3072]{1,0:T(8,128)(2,1)S(1)} %get-tuple-element.17.a_ref, f32[32,3072]{1,0:T(8,128)S(1)} %get-tuple-element.18.cs_ref, bf16[64,1536]{1,0:T(8,128)(2,1)S(1)} %finish.2.own_ref.field_ref), custom_call_target="tpu_custom_call" | custom-call | flops 2200000000 | tf_op jit(solution)/shard_map/forward_own/pallas_call | solution.py:179
  50.2 3.2 %forward.3 = (f32[3168,128]{1,0:T(8,128)S(1)}, bf16[256,128]{1,0:T(8,128)(2,1)S(1)}, bf16[256,128]{1,0:T(8,128)(2,1)S(1)}) custom-call(s32[4096]{0:T(1024)S(1)} %get-tuple-element.30.list_ref.row_ref, bf16[352,3072]{1,0:T(8,128)(2,1)S(1)} %get-tuple-element.17.a_ref, f32[32,3072]{1,0:T(8,128)S(1)} %get-tuple-element.18.cs_ref, ...), custom_call_target="tpu_custom_call" | custom-call | flops 4400000000 | tf_op jit(solution)/shard_map/forward/pallas_call | solution.py:225
  56.8 2.0 %keep_rows.3.keep_ref = f32[1024,128]{1,0:T(8,128)S(1)} custom-call(s32[4096]{0:T(1024)S(1)} %get-tuple-element.30.list_ref.row_ref, f32[3168,128]{1,0:T(8,128)S(1)} %get-tuple-element.24.q_ref), custom_call_target="tpu_custom_call" | custom-call | flops 2200000000 | tf_op jit(solution)/shard_map/keep_rows/pallas_call | solution.py:269
  58.9 1.8 %collective-permute-start.17 = (bf16[256,128]{1,0:T(8,128)(2,1)S(1)}, bf16[256,128]{1,0:T(8,128)(2,1)S(1)}, u32[]{:S(2)}, u32[]{:S(2)}) collective-permute-start(bf16[256,128]{1,0:T(8,128)(2,1)S(1)} %merge.9), channel_id=1, source_target_pairs={{0,12},{1,13},{2,14},{3,15},{4,8},{5,9},{6,10},{7,11},{8,4},{9,5},... | collective-permute-start | bytes 196616 | tf_op jit(solution)/shard_map/ppermute | solution.py:536
  60.8 1.9 %collective-permute-start.21 = (bf16[256,128]{1,0:T(8,128)(2,1)S(1)}, bf16[256,128]{1,0:T(8,128)(2,1)S(1)}, u32[]{:S(2)}, u32[]{:S(2)}) collective-permute-start(bf16[256,128]{1,0:T(8,128)(2,1)S(1)} %merge.11), channel_id=1, source_target_pairs={{0,4},{1,5},{2,6},{3,7},{4,0},{5,1},{6,2},{7,3},{8,12},{9,13},{10,... | collective-permute-start | bytes 196616 | tf_op jit(solution)/shard_map/ppermute | solution.py:536
  64.0 2.3 %collective-permute-done.19.refs_1_ = bf16[256,128]{1,0:T(8,128)(2,1)S(1)} collective-permute-done((bf16[256,128]{1,0:T(8,128)(2,1)S(1)}, bf16[256,128]{1,0:T(8,128)(2,1)S(1)}, u32[]{:S(2)}, u32[]{:S(2)}) %collective-permute-start.19) | collective-permute-done | bytes 65568 | tf_op jit(solution)/shard_map/ppermute | solution.py:536
  66.3 1.7 %mix.3.refs_0_ = bf16[256,128]{1,0:T(8,128)(2,1)S(1)} custom-call(f32[1,256]{1,0:T(1,128)S(1)} %bitcast.7, bf16[2,2,64,64,256]{4,3,2,1,0:T(8,128)(2,1)S(1)} %bitcast.5, f32[1024,128]{1,0:T(8,128)S(1)} %keep_rows.3.keep_ref, bf16[256,128]{1,0:T(8,128)(2,1)S(1)} %collective-permute-done.17.refs_0_, bf16[256,128]{1,0:T(8,128)(2,1)S(1)} %collective-permute-done.19.refs_1_, ...), custom_call_target="tpu_custom_call" | custom-call | flops 1980000000 | tf_op jit(solution)/shard_map/mix/pallas_call | solution.py:327
  68.9 2.3 %collective-permute-start.24 = (bf16[256,128]{1,0:T(8,128)(2,1)S(1)}, bf16[256,128]{1,0:T(8,128)(2,1)S(1)}, u32[]{:S(2)}, u32[]{:S(2)}) collective-permute-start(bf16[256,128]{1,0:T(8,128)(2,1)S(1)} %mix.3.refs_0_), channel_id=1, source_target_pairs={{0,12},{1,13},{2,14},{3,15},{4,8},{5,9},{6,10},{7,11},{8,4},{9,5},... | collective-permute-start | bytes 196616 | tf_op jit(solution)/shard_map/ppermute | solution.py:536
  76.5 2.1 %place_pieces.7.z_ref = f32[6336,128]{1,0:T(8,128)S(1)} custom-call(s32[4096]{0:T(1024)S(1)} %get-tuple-element.29.place_ref.list_ref, f32[6336,128]{1,0:T(8,128)S(1)} %place_pieces.6.before_ref, bf16[256,128]{1,0:T(8,128)(2,1)S(1)} %collective-permute-done.22.refs_0_, ...), custom_call_target="tpu_custom_call", output_to_operand_aliasing={{}: (1, {})} | custom-call | flops 2529999872 | tf_op jit(solution)/shard_map/place_pieces/pallas_call | solution.py:382
  79.5 4.9 %inverse_other.3 = (f32[64,1536]{1,0:T(8,128)S(1)}, bf16[1088,352]{1,0:T(8,128)(2,1)S(1)}, f32[6336,128]{1,0:T(8,128)S(1)}) custom-call(s32[4096]{0:T(1024)S(1)} %get-tuple-element.29.place_ref.list_ref, f32[6336,128]{1,0:T(8,128)S(1)} %place_pieces.7.z_ref, bf16[352,3072]{1,0:T(8,128)(2,1)S(1)} %get-tuple-element.17.a_ref, ...), custom_call_target="tpu_custom_call", output_to_operand_aliasing={{2}: (1, {})} | custom-call | flops 4950000128 | tf_op jit(solution)/shard_map/inverse_other/pallas_call | solution.py:456
  84.5 4.4 %collective-permute-start.28 = (f32[64,1536]{1,0:T(8,128)S(1)}, f32[64,1536]{1,0:T(8,128)S(1)}, u32[]{:S(2)}, u32[]{:S(2)}) collective-permute-start(f32[64,1536]{1,0:T(8,128)S(1)} %get-tuple-element.28), channel_id=1, source_target_pairs={{0,1},{1,0},{2,3},{3,2},{4,5},{5,4},{6,7},{7,6},{8,9},{9,8},{10,11... | collective-permute-start | bytes 1179656 | tf_op jit(solution)/shard_map/ppermute | solution.py:536
  88.9 2.0 %inverse_own.3.own_ref = f32[64,1536]{1,0:T(8,128)S(1)} custom-call(bf16[1088,352]{1,0:T(8,128)(2,1)S(1)} %get-tuple-element.27.t_ref, bf16[352,3072]{1,0:T(8,128)(2,1)S(1)} %get-tuple-element.17.a_ref, f32[32,3072]{1,0:T(8,128)S(1)} %get-tuple-element.18.cs_ref, bf16[64,1536]{1,0:T(8,128)(2,1)S(1)} %finish.2.own_ref.field_ref, ...), custom_call_target="tpu_custom_call" | custom-call | flops 2310000128 | tf_op jit(solution)/shard_map/inverse_own/pallas_call | solution.py:498
  (80 shorter events, 27.5 us)
Async XLA Ops:
  0.1 4.8 %collective-permute-start.1 = (bf16[64,1536]{1,0:T(8,128)(2,1)}, bf16[64,1536]{1,0:T(8,128)(2,1)S(1)}, u32[]{:S(2)}, u32[]{:S(2)}) collective-permute-start(bf16[64,1536]{1,0:T(8,128)(2,1)} %field_ref.1), channel_id=1, source_target_pairs={{0,1},{1,0},{2,3},{3,2},{4,5},{5,4},{6,7},{7,6},{8,9},{9,8},{10,11... | collective-permute-start | bytes 589832 | tf_op jit(solution)/shard_map/ppermute | solution.py:536
  8.2 7.5 %collective-permute-start.2 = (bf16[256,128]{1,0:T(8,128)(2,1)S(1)}, bf16[256,128]{1,0:T(8,128)(2,1)S(1)}, u32[]{:S(2)}, u32[]{:S(2)}) collective-permute-start(bf16[256,128]{1,0:T(8,128)(2,1)S(1)} %get-tuple-element.20), channel_id=1, source_target_pairs={{0,2},{1,3},{2,0},{3,1},{4,6},{5,7},{6,4},{7,5},{8,10},{9,11},{10,... | collective-permute-start | bytes 196616 | tf_op jit(solution)/shard_map/ppermute | solution.py:536
  10.7 8.5 %collective-permute-start.4 = (bf16[256,128]{1,0:T(8,128)(2,1)S(1)}, bf16[256,128]{1,0:T(8,128)(2,1)S(1)}, u32[]{:S(2)}, u32[]{:S(2)}) collective-permute-start(bf16[256,128]{1,0:T(8,128)(2,1)S(1)} %get-tuple-element.21), channel_id=1, source_target_pairs={{0,2},{1,3},{2,0},{3,1},{4,6},{5,7},{6,4},{7,5},{8,10},{9,11},{10,... | collective-permute-start | bytes 196616 | tf_op jit(solution)/shard_map/ppermute | solution.py:536
  12.2 7.0 %collective-permute-start.6 = (bf16[512,128]{1,0:T(8,128)(2,1)S(1)}, bf16[512,128]{1,0:T(8,128)(2,1)S(1)}, u32[]{:S(2)}, u32[]{:S(2)}) collective-permute-start(bf16[512,128]{1,0:T(8,128)(2,1)S(1)} %more_rows.2), channel_id=1, source_target_pairs={{0,2},{1,3},{2,0},{3,1},{4,6},{5,7},{6,4},{7,5},{8,10},{9,11},{10,... | collective-permute-start | bytes 393224 | tf_op jit(solution)/shard_map/ppermute | solution.py:536
  15.7 5.0 %collective-permute-start.3 = (bf16[256,128]{1,0:T(8,128)(2,1)S(1)}, bf16[256,128]{1,0:T(8,128)(2,1)S(1)}, u32[]{:S(2)}, u32[]{:S(2)}) collective-permute-start(bf16[256,128]{1,0:T(8,128)(2,1)S(1)} %merge.6), channel_id=1, source_target_pairs={{0,12},{1,13},{2,14},{3,15},{4,8},{5,9},{6,10},{7,11},{8,4},{9,5},... | collective-permute-start | bytes 196616 | tf_op jit(solution)/shard_map/ppermute | solution.py:536
  19.2 5.1 %collective-permute-start.5 = (bf16[256,128]{1,0:T(8,128)(2,1)S(1)}, bf16[256,128]{1,0:T(8,128)(2,1)S(1)}, u32[]{:S(2)}, u32[]{:S(2)}) collective-permute-start(bf16[256,128]{1,0:T(8,128)(2,1)S(1)} %merge.7), channel_id=1, source_target_pairs={{0,8},{1,9},{2,10},{3,11},{4,12},{5,13},{6,14},{7,15},{8,0},{9,1},... | collective-permute-start | bytes 196616 | tf_op jit(solution)/shard_map/ppermute | solution.py:536
  19.3 5.0 %collective-permute-start.7 = (bf16[256,128]{1,0:T(8,128)(2,1)S(1)}, bf16[256,128]{1,0:T(8,128)(2,1)S(1)}, u32[]{:S(2)}, u32[]{:S(2)}) collective-permute-start(bf16[256,128]{1,0:T(8,128)(2,1)S(1)} %merge.8), channel_id=1, source_target_pairs={{0,4},{1,5},{2,6},{3,7},{4,0},{5,1},{6,2},{7,3},{8,12},{9,13},{10,... | collective-permute-start | bytes 196616 | tf_op jit(solution)/shard_map/ppermute | solution.py:536
  26.0 6.4 %collective-permute-start.11 = (bf16[256,128]{1,0:T(8,128)(2,1)S(1)}, bf16[256,128]{1,0:T(8,128)(2,1)S(1)}, u32[]{:S(2)}, u32[]{:S(2)}) collective-permute-start(bf16[256,128]{1,0:T(8,128)(2,1)S(1)} %mix.2.refs_0_), channel_id=1, source_target_pairs={{0,8},{1,9},{2,10},{3,11},{4,12},{5,13},{6,14},{7,15},{8,0},{9,1},... | collective-permute-start | bytes 196616 | tf_op jit(solution)/shard_map/ppermute | solution.py:536
  26.9 5.2 %collective-permute-start.10 = (bf16[256,128]{1,0:T(8,128)(2,1)S(1)}, bf16[256,128]{1,0:T(8,128)(2,1)S(1)}, u32[]{:S(2)}, u32[]{:S(2)}) collective-permute-start(bf16[256,128]{1,0:T(8,128)(2,1)S(1)} %mix.2.refs_0_), channel_id=1, source_target_pairs={{0,12},{1,13},{2,14},{3,15},{4,8},{5,9},{6,10},{7,11},{8,4},{9,5},... | collective-permute-start | bytes 196616 | tf_op jit(solution)/shard_map/ppermute | solution.py:536
  28.7 4.9 %collective-permute-start.8 = (bf16[256,128]{1,0:T(8,128)(2,1)S(1)}, bf16[256,128]{1,0:T(8,128)(2,1)S(1)}, u32[]{:S(2)}, u32[]{:S(2)}) collective-permute-start(bf16[256,128]{1,0:T(8,128)(2,1)S(1)} %mix.2.refs_0_), channel_id=1, source_target_pairs={{0,2},{1,3},{2,0},{3,1},{4,6},{5,7},{6,4},{7,5},{8,10},{9,11},{10,... | collective-permute-start | bytes 196616 | tf_op jit(solution)/shard_map/ppermute | solution.py:536
  32.1 4.8 %collective-permute-start.12 = (bf16[512,128]{1,0:T(8,128)(2,1)S(1)}, bf16[512,128]{1,0:T(8,128)(2,1)S(1)}, u32[]{:S(2)}, u32[]{:S(2)}) collective-permute-start(bf16[512,128]{1,0:T(8,128)(2,1)S(1)} %pad_maximum_fusion), channel_id=1, source_target_pairs={{0,2},{1,3},{2,0},{3,1},{4,6},{5,7},{6,4},{7,5},{8,10},{9,11},{10,... | collective-permute-start | bytes 393224 | tf_op jit(solution)/shard_map/ppermute | solution.py:536
  32.4 4.5 %collective-permute-start.13 = (bf16[256,128]{1,0:T(8,128)(2,1)S(1)}, bf16[256,128]{1,0:T(8,128)(2,1)S(1)}, u32[]{:S(2)}, u32[]{:S(2)}) collective-permute-start(bf16[256,128]{1,0:T(8,128)(2,1)S(1)} %collective-permute-done.11.refs_3_), channel_id=1, source_target_pairs={{0,2},{1,3},{2,0},{3,1},{4,6},{5,7},{6,4},{7,5},{8,10},{9,11},{10,... | collective-permute-start | bytes 196616 | tf_op jit(solution)/shard_map/ppermute | solution.py:536
  41.6 6.9 %collective-permute-start.14 = (f32[64,1536]{1,0:T(8,128)S(1)}, f32[64,1536]{1,0:T(8,128)S(1)}, u32[]{:S(2)}, u32[]{:S(2)}) collective-permute-start(f32[64,1536]{1,0:T(8,128)S(1)} %get-tuple-element.23), channel_id=1, source_target_pairs={{0,1},{1,0},{2,3},{3,2},{4,5},{5,4},{6,7},{7,6},{8,9},{9,8},{10,11... | collective-permute-start | bytes 1179656 | tf_op jit(solution)/shard_map/ppermute | solution.py:536
  53.4 5.4 %collective-permute-start.16 = (bf16[256,128]{1,0:T(8,128)(2,1)S(1)}, bf16[256,128]{1,0:T(8,128)(2,1)S(1)}, u32[]{:S(2)}, u32[]{:S(2)}) collective-permute-start(bf16[256,128]{1,0:T(8,128)(2,1)S(1)} %get-tuple-element.25), channel_id=1, source_target_pairs={{0,2},{1,3},{2,0},{3,1},{4,6},{5,7},{6,4},{7,5},{8,10},{9,11},{10,... | collective-permute-start | bytes 196616 | tf_op jit(solution)/shard_map/ppermute | solution.py:536
  53.8 6.8 %collective-permute-start.18 = (bf16[256,128]{1,0:T(8,128)(2,1)S(1)}, bf16[256,128]{1,0:T(8,128)(2,1)S(1)}, u32[]{:S(2)}, u32[]{:S(2)}) collective-permute-start(bf16[256,128]{1,0:T(8,128)(2,1)S(1)} %get-tuple-element.26), channel_id=1, source_target_pairs={{0,2},{1,3},{2,0},{3,1},{4,6},{5,7},{6,4},{7,5},{8,10},{9,11},{10,... | collective-permute-start | bytes 196616 | tf_op jit(solution)/shard_map/ppermute | solution.py:536
  56.4 4.4 %collective-permute-start.20 = (bf16[512,128]{1,0:T(8,128)(2,1)S(1)}, bf16[512,128]{1,0:T(8,128)(2,1)S(1)}, u32[]{:S(2)}, u32[]{:S(2)}) collective-permute-start(bf16[512,128]{1,0:T(8,128)(2,1)S(1)} %more_rows.3), channel_id=1, source_target_pairs={{0,2},{1,3},{2,0},{3,1},{4,6},{5,7},{6,4},{7,5},{8,10},{9,11},{10,... | collective-permute-start | bytes 393224 | tf_op jit(solution)/shard_map/ppermute | solution.py:536
  58.9 5.1 %collective-permute-start.17 = (bf16[256,128]{1,0:T(8,128)(2,1)S(1)}, bf16[256,128]{1,0:T(8,128)(2,1)S(1)}, u32[]{:S(2)}, u32[]{:S(2)}) collective-permute-start(bf16[256,128]{1,0:T(8,128)(2,1)S(1)} %merge.9), channel_id=1, source_target_pairs={{0,12},{1,13},{2,14},{3,15},{4,8},{5,9},{6,10},{7,11},{8,4},{9,5},... | collective-permute-start | bytes 196616 | tf_op jit(solution)/shard_map/ppermute | solution.py:536
  60.7 5.7 %collective-permute-start.19 = (bf16[256,128]{1,0:T(8,128)(2,1)S(1)}, bf16[256,128]{1,0:T(8,128)(2,1)S(1)}, u32[]{:S(2)}, u32[]{:S(2)}) collective-permute-start(bf16[256,128]{1,0:T(8,128)(2,1)S(1)} %merge.10), channel_id=1, source_target_pairs={{0,8},{1,9},{2,10},{3,11},{4,12},{5,13},{6,14},{7,15},{8,0},{9,1},... | collective-permute-start | bytes 196616 | tf_op jit(solution)/shard_map/ppermute | solution.py:536
  60.8 5.6 %collective-permute-start.21 = (bf16[256,128]{1,0:T(8,128)(2,1)S(1)}, bf16[256,128]{1,0:T(8,128)(2,1)S(1)}, u32[]{:S(2)}, u32[]{:S(2)}) collective-permute-start(bf16[256,128]{1,0:T(8,128)(2,1)S(1)} %merge.11), channel_id=1, source_target_pairs={{0,4},{1,5},{2,6},{3,7},{4,0},{5,1},{6,2},{7,3},{8,12},{9,13},{10,... | collective-permute-start | bytes 196616 | tf_op jit(solution)/shard_map/ppermute | solution.py:536
  68.0 8.1 %collective-permute-start.25 = (bf16[256,128]{1,0:T(8,128)(2,1)S(1)}, bf16[256,128]{1,0:T(8,128)(2,1)S(1)}, u32[]{:S(2)}, u32[]{:S(2)}) collective-permute-start(bf16[256,128]{1,0:T(8,128)(2,1)S(1)} %mix.3.refs_0_), channel_id=1, source_target_pairs={{0,8},{1,9},{2,10},{3,11},{4,12},{5,13},{6,14},{7,15},{8,0},{9,1},... | collective-permute-start | bytes 196616 | tf_op jit(solution)/shard_map/ppermute | solution.py:536
  68.9 5.0 %collective-permute-start.24 = (bf16[256,128]{1,0:T(8,128)(2,1)S(1)}, bf16[256,128]{1,0:T(8,128)(2,1)S(1)}, u32[]{:S(2)}, u32[]{:S(2)}) collective-permute-start(bf16[256,128]{1,0:T(8,128)(2,1)S(1)} %mix.3.refs_0_), channel_id=1, source_target_pairs={{0,12},{1,13},{2,14},{3,15},{4,8},{5,9},{6,10},{7,11},{8,4},{9,5},... | collective-permute-start | bytes 196616 | tf_op jit(solution)/shard_map/ppermute | solution.py:536
  71.4 5.1 %collective-permute-start.22 = (bf16[256,128]{1,0:T(8,128)(2,1)S(1)}, bf16[256,128]{1,0:T(8,128)(2,1)S(1)}, u32[]{:S(2)}, u32[]{:S(2)}) collective-permute-start(bf16[256,128]{1,0:T(8,128)(2,1)S(1)} %mix.3.refs_0_), channel_id=1, source_target_pairs={{0,2},{1,3},{2,0},{3,1},{4,6},{5,7},{6,4},{7,5},{8,10},{9,11},{10,... | collective-permute-start | bytes 196616 | tf_op jit(solution)/shard_map/ppermute | solution.py:536
  74.9 4.6 %collective-permute-start.26 = (bf16[512,128]{1,0:T(8,128)(2,1)S(1)}, bf16[512,128]{1,0:T(8,128)(2,1)S(1)}, u32[]{:S(2)}, u32[]{:S(2)}) collective-permute-start(bf16[512,128]{1,0:T(8,128)(2,1)S(1)} %pad_maximum_fusion.1), channel_id=1, source_target_pairs={{0,2},{1,3},{2,0},{3,1},{4,6},{5,7},{6,4},{7,5},{8,10},{9,11},{10,... | collective-permute-start | bytes 393224 | tf_op jit(solution)/shard_map/ppermute | solution.py:536
  84.5 6.5 %collective-permute-start.28 = (f32[64,1536]{1,0:T(8,128)S(1)}, f32[64,1536]{1,0:T(8,128)S(1)}, u32[]{:S(2)}, u32[]{:S(2)}) collective-permute-start(f32[64,1536]{1,0:T(8,128)S(1)} %get-tuple-element.28), channel_id=1, source_target_pairs={{0,1},{1,0},{2,3},{3,2},{4,5},{5,4},{6,7},{7,6},{8,9},{9,8},{10,11... | collective-permute-start | bytes 1179656 | tf_op jit(solution)/shard_map/ppermute | solution.py:536
  (11 other events, 65.0 us)
